TPU v7x, 32 devices: a whole 2x2x4 slice. The times are simulated.
32 devices in a mesh: ctx: 2 (over y), exp: 16 (over z, x, core).
Axes of the slice: x: 2, y: 2, z: 4, core: 2. Of those that a mesh axis runs over, the one named last changes fastest.
Arguments:
- tokens: bfloat16 [16, 256, 2048], P('exp', 'ctx'), may hold values from -6 to 6
- queries: bfloat16 [16, 256, 1024], P('exp', 'ctx'), may hold values from -60 to 60
- keys: bfloat16 [16, 256, 1024], P('exp', 'ctx'), may hold values from -4 to 4
- values: bfloat16 [16, 256, 1024], P('exp', 'ctx'), may hold values from -12 to 12
- out_proj: bfloat16 [1024, 2048], replicated, may hold values from -0.1875 to 0.1875
- mod_scale: float32 [16, 2048], P('exp'), may hold values from -2.5 to 2.5
- mod_shift: float32 [16, 2048], P('exp'), may hold values from -2.5 to 2.5
- expert_ids: int32 [16, 256, 2], P('exp', 'ctx'), may hold values from 0 to 7, all different within a row; in each aligned block of 128 rows (0 to 127, 128 to 255, ..., all dimensions but the last counted through in order) at most 48 rows name the same one
- gates: float32 [16, 256, 2], P('exp', 'ctx'), may hold values from 0.2 to 1
- w_gate: bfloat16 [8192, 2048], P(('ctx', 'exp')), may hold values from -0.125 to 0.125
- w_up: bfloat16 [8192, 2048], P(('ctx', 'exp')), may hold values from -0.125 to 0.125
- w_down: bfloat16 [8192, 2048], P(('ctx', 'exp')), may hold values from -0.1875 to 0.1875
- out_grad: bfloat16 [16, 256, 2048], P('exp', 'ctx'), may hold values from -0.1875 to 0.1875
Outputs:
- layer_out: bfloat16 [16, 256, 2048], P('exp', 'ctx')
- grad_gate: bfloat16 [8192, 2048], P(('ctx', 'exp'))
- grad_up: bfloat16 [8192, 2048], P(('ctx', 'exp'))
- grad_down: bfloat16 [8192, 2048], P(('ctx', 'exp'))
Inputs may be any that keep to these rules, and one draw needn't show every extreme that they name: `expert_ids`: the two ids of a token differ. Among the 128 tokens of one device no expert is named more than 48 times, and in some device some expert exactly 48 times.
All inputs are finite; a program needn't handle non-finite values.
Results may differ from a plain program's by a relative error of at most 0.0075.
Values may be sent and summed in bfloat16 or wider, within the bound.
No kernel may reach another device: no remote copies, remote signals or barrier semaphores. Data moves between devices by JAX's collectives and lax.ppermute only.
A program may use at most 128 MiB of HBM per device.

v0:
```python
import jax
import jax.numpy as jnp
from jax import lax
from jax.sharding import PartitionSpec as P

HEADS = 8
HD = 128
SHARDS = 4


def per_device(
    tokens,
    queries,
    keys,
    values,
    out_proj,
    mod_scale,
    mod_shift,
    expert_ids,
    gates,
    w_gate,
    w_up,
    w_down,
    out_grad,
):
    ctx_count = lax.axis_size("ctx")
    exp_count = lax.axis_size("exp")
    local_tokens = tokens.shape[1]
    model_width = tokens.shape[2]
    score_scale = HD ** (-0.5)
    query_rows = queries[0]
    key_rows = keys[0]
    value_rows = values[0]
    query_heads = query_rows.reshape(local_tokens, HEADS, HD)
    running_top = jnp.full((HEADS, local_tokens), -1e30, jnp.float32)
    key_piece = lax.all_gather(key_rows, "ctx", axis=0, tiled=True).reshape(-1, HEADS, HD)
    value_piece = lax.all_gather(value_rows, "ctx", axis=0, tiled=True).reshape(-1, HEADS, HD)
    scores = (
        jnp.einsum("qhd,khd->hqk", query_heads, key_piece, preferred_element_type=jnp.float32)
        * score_scale
    )
    new_top = jnp.maximum(running_top, jnp.max(scores, axis=-1))
    exponent = jnp.exp(scores - new_top[..., None])
    running_sum = jnp.sum(exponent, axis=-1)
    accum = jnp.einsum(
        "hqk,khd->hqd",
        exponent.astype(jnp.bfloat16),
        value_piece,
        preferred_element_type=jnp.float32,
    )
    attended = (
        jnp.transpose(accum / running_sum[..., None], (1, 0, 2))
        .reshape(local_tokens, HEADS * HD)
        .astype(jnp.bfloat16)
    )
    mixed = tokens[0].astype(jnp.float32) + jnp.dot(
        attended, out_proj, preferred_element_type=jnp.float32
    )
    mean_square = jnp.mean(mixed * mixed, axis=-1, keepdims=True)
    normed = (mixed * lax.rsqrt(mean_square + 1e-06) * (1.0 + mod_scale) + mod_shift).astype(
        jnp.bfloat16
    )
    expert_total = ctx_count * exp_count // SHARDS
    capacity = 3 * local_tokens // expert_total
    group_count = exp_count // SHARDS
    chosen = expert_ids[0].reshape(-1)
    one_hot = (chosen[:, None] == jnp.arange(expert_total, dtype=jnp.int32)[None, :]).astype(
        jnp.int32
    )
    before = jnp.cumsum(one_hot, axis=0) - one_hot
    slot_index = jnp.sum(one_hot * before, axis=1)
    position = chosen * capacity + slot_index
    chooser = (
        jnp.arange(expert_total * capacity, dtype=jnp.int32)[:, None] == position[None, :]
    ).astype(jnp.bfloat16)
    gate_flat = gates[0].reshape(-1)
    token_rows = jnp.repeat(normed, 2, axis=0)
    grad_rows = (
        gate_flat[:, None] * jnp.repeat(out_grad[0], 2, axis=0).astype(jnp.float32)
    ).astype(jnp.bfloat16)
    stacked = jnp.concatenate([token_rows, grad_rows], axis=1)
    placed = jnp.dot(chooser, stacked, preferred_element_type=jnp.float32).astype(jnp.bfloat16)
    slot_width = capacity * 2 * model_width
    plain_slots = placed.reshape(ctx_count, group_count, slot_width)
    middle = lax.all_to_all(plain_slots, "ctx", split_axis=0, concat_axis=0, tiled=True)
    shaped = middle.reshape(ctx_count, group_count, 1, slot_width)
    widened = jnp.broadcast_to(shaped, (ctx_count, group_count, SHARDS, slot_width))
    arrived = lax.all_to_all(
        widened.reshape(ctx_count, exp_count, slot_width),
        "exp",
        split_axis=1,
        concat_axis=1,
        tiled=True,
    )
    arrived = arrived.reshape(-1, 2 * model_width)
    expert_rows = arrived[:, :model_width]
    row_grads = arrived[:, model_width:]
    gate_pre = jnp.einsum("rd,fd->rf", expert_rows, w_gate, preferred_element_type=jnp.float32)
    up_pre = jnp.einsum("rd,fd->rf", expert_rows, w_up, preferred_element_type=jnp.float32)
    sigmoid_gate = jax.nn.sigmoid(gate_pre)
    activation = gate_pre * sigmoid_gate
    hidden = (activation * up_pre).astype(jnp.bfloat16)
    piece_out = jnp.einsum("rf,fd->rd", hidden, w_down, preferred_element_type=jnp.float32).astype(
        jnp.bfloat16
    )
    out_width = capacity * model_width
    piece_out = piece_out.reshape(ctx_count, exp_count, out_width)
    by_piece = lax.all_to_all(piece_out, "exp", split_axis=1, concat_axis=1, tiled=True)
    piece_sums = jnp.sum(
        by_piece.astype(jnp.float32).reshape(ctx_count, group_count, SHARDS, out_width), axis=2
    )
    expert_sums = lax.all_to_all(
        piece_sums.astype(jnp.bfloat16), "ctx", split_axis=0, concat_axis=0, tiled=True
    ).astype(piece_sums.dtype)
    expert_sums = expert_sums.reshape(expert_total * capacity, model_width)
    hidden_grad = jnp.einsum("rd,fd->rf", row_grads, w_down, preferred_element_type=jnp.float32)
    gate_cot = (
        hidden_grad * up_pre * sigmoid_gate * (1.0 + gate_pre * (1.0 - sigmoid_gate))
    ).astype(jnp.bfloat16)
    up_cot = (hidden_grad * activation).astype(jnp.bfloat16)
    grad_down = jnp.einsum(
        "rf,rd->fd", hidden, row_grads, preferred_element_type=jnp.float32
    ).astype(jnp.bfloat16)
    grad_gate = jnp.einsum(
        "rf,rd->fd", gate_cot, expert_rows, preferred_element_type=jnp.float32
    ).astype(jnp.bfloat16)
    grad_up = jnp.einsum(
        "rf,rd->fd", up_cot, expert_rows, preferred_element_type=jnp.float32
    ).astype(jnp.bfloat16)
    picked = jnp.take(expert_sums, position, axis=0)
    combined = jnp.sum((gate_flat[:, None] * picked).reshape(local_tokens, 2, model_width), axis=1)
    layer_out = (mixed + combined).astype(jnp.bfloat16)[None]
    return (layer_out, grad_gate, grad_up, grad_down)


def solution(mesh):
    placed = (
        P("exp", "ctx", None),
        P("exp", "ctx", None),
        P("exp", "ctx", None),
        P("exp", "ctx", None),
        P(),
        P("exp", None),
        P("exp", None),
        P("exp", "ctx", None),
        P("exp", "ctx", None),
        P(("ctx", "exp"), None),
        P(("ctx", "exp"), None),
        P(("ctx", "exp"), None),
        P("exp", "ctx", None),
    )
    return jax.shard_map(
        per_device,
        mesh=mesh,
        in_specs=placed,
        out_specs=(
            P("exp", "ctx", None),
            P(("ctx", "exp"), None),
            P(("ctx", "exp"), None),
            P(("ctx", "exp"), None),
        ),
        check_vma=False,
    )
```

profile of v0, /device:TPU:10, one launch (start us, length us, event | category | flops | bytes accessed | tf_op | source)
XLA Modules:
  0.0 644.1 jit_solution(12046386126268213849)
XLA Ops:
  3.0 8.7 %all-gather = bf16[1,256,1024]{1,2,0:T(8,128)(2,1)S(1)} all-gather(bf16[1,128,1024]{1,2,0:T(8,128)(2,1)S(1)} %copy.79), channel_id=2, replica_groups=mesh['ctx'=2,'exp'=16] {'ctx'}, dimensions={1}, use_global_device_ids=true | all-gather | bytes 786432 | tf_op jit(solution)/shard_map/all_gather | solution.py:36
  13.1 7.9 %all-gather.1 = bf16[1,256,1024]{2,1,0:T(8,128)(2,1)S(1)} all-gather(bf16[1,128,1024]{2,1,0:T(8,128)(2,1)S(1)} %copy-done.4), channel_id=3, replica_groups=mesh['ctx'=2,'exp'=16] {'ctx'}, dimensions={1}, use_global_device_ids=true | all-gather | bytes 786432 | tf_op jit(solution)/shard_map/all_gather | solution.py:37
  40.4 5.0 reshape.143
  45.4 38.6 %all_to_all.20 = bf16[2,4,196608]{2,1,0:T(4,128)(2,1)S(1)} all-to-all(bf16[2,4,196608]{2,1,0:T(4,128)(2,1)} %reshape.143), channel_id=1, replica_groups=mesh['ctx'=2,'exp'=16] {'ctx'}, dimensions={0} | all-to-all | bytes 6291456 | tf_op jit(solution)/shard_map/all_to_all | solution.py:85
  84.0 10.9 %copy.89 = bf16[2,4,196608]{2,0,1:T(2,128)(2,1)S(1)} copy(bf16[2,4,196608]{2,1,0:T(4,128)(2,1)S(1)} %all_to_all.20) | data formatting | bytes 6291456 | tf_op jit(solution)/shard_map/all_to_all | solution.py:85
  94.9 7.0 %broadcast_in_dim.37 = bf16[2,4,4,196608]{3,0,2,1:T(2,128)(2,1)S(1)} broadcast(bf16[2,4,196608]{2,0,1:T(2,128)(2,1)S(1)} %copy.89), dimensions={0,1,3} | broadcast | bytes 15728640 | tf_op jit(solution)/shard_map/broadcast_in_dim | solution.py:87
  101.9 278.1 %all_to_all.21 = bf16[2,16,196608]{2,0,1:T(2,128)(2,1)S(1)} all-to-all(bf16[2,16,196608]{2,0,1:T(2,128)(2,1)S(1)} %bitcast.51), channel_id=1, replica_groups=mesh['ctx'=2,'exp'=16] {'exp'}, dimensions={1} | all-to-all | bytes 25165824 | tf_op jit(solution)/shard_map/all_to_all | solution.py:88
  380.0 16.0 %copy.90 = bf16[2,16,196608]{2,1,0:T(8,128)(2,1)} copy(bf16[2,16,196608]{2,0,1:T(2,128)(2,1)S(1)} %all_to_all.21) | data formatting | bytes 25165824 | tf_op jit(solution)/shard_map/all_to_all | solution.py:88
  396.0 12.0 %reshape.145 = bf16[1536,4096]{1,0:T(8,128)(2,1)} reshape(bf16[2,16,196608]{2,1,0:T(8,128)(2,1)} %copy.90) | data formatting | bytes 25165824 | tf_op jit(solution)/shard_map/reshape | solution.py:95
  408.1 4.9 fusion.10
  418.0 4.4 convolution_convert_fusion
  422.4 7.3 %reshape.146 = bf16[2,16,98304]{2,1,0:T(8,128)(2,1)} reshape(bf16[1536,2048]{1,0:T(8,128)(2,1)} %convolution_convert_fusion) | data formatting | bytes 12582912 | tf_op jit(solution)/shard_map/reshape | solution.py:107
  429.7 12.6 %copy.91 = bf16[2,16,98304]{2,0,1:T(2,128)(2,1)} copy(bf16[2,16,98304]{2,1,0:T(8,128)(2,1)} %reshape.146) | data formatting | bytes 12582912 | tf_op jit(solution)/shard_map/reshape | solution.py:107
  442.4 6.7 %all-to-all-start.2 = ((bf16[2,16,98304]{2,0,1:T(2,128)(2,1)}), bf16[2,16,98304]{2,0,1:T(2,128)(2,1)}, u32[]{:S(2)}, u32[]{:S(2)}) async-start(bf16[2,16,98304]{2,0,1:T(2,128)(2,1)} %copy.91), calls=%async_computation.2 | async-start | bytes 12582912 | tf_op jit(solution)/shard_map/all_to_all | solution.py:108
  449.9 5.7 fusion.18
  455.6 4.9 fusion.2
  464.9 121.4 %all-to-all-done.2 = bf16[2,16,98304]{2,0,1:T(2,128)(2,1)} async-done(((bf16[2,16,98304]{2,0,1:T(2,128)(2,1)}), bf16[2,16,98304]{2,0,1:T(2,128)(2,1)}, u32[]{:S(2)}, u32[]{:S(2)}) %all-to-all-start.2) | async-done | bytes 6291488 | tf_op jit(solution)/shard_map/all_to_all | solution.py:108
  586.2 9.9 %bitcast_reduce_fusion = bf16[2,4,98304]{2,0,1:T(2,128)(2,1)} fusion(bf16[2,16,98304]{2,0,1:T(2,128)(2,1)} %all-to-all-done.2), kind=kLoop, calls=%fused_computation.2 | loop fusion | flops 2359296 | bytes 7864320 | tf_op jit(solution)/shard_map/reduce_sum | solution.py:109
  596.1 3.8 copy.92
  599.9 4.9 all-to-all-start.3
  604.8 6.6 %fusion.15 = bf16[256,2048]{1,0:T(8,128)(2,1)} fusion(bf16[1536,4096]{1,0:T(8,128)(2,1)} %reshape.145, f32[1536,256]{1,0:T(8,128)} %copy-done.13, f32[1536,256]{1,0:T(8,128)} %copy-done.11), kind=kOutput, calls=%fused_computation.17 | convolution fusion | flops 1613496320 | bytes 10485760 | tf_op jit(solution)/shard_map/rf,rd->fd/dot_general | solution.py:127
  611.4 13.4 %all-to-all-done.3 = bf16[2,4,98304]{2,1,0:T(4,128)(2,1)} async-done(((bf16[2,4,98304]{2,1,0:T(4,128)(2,1)}), bf16[2,4,98304]{2,1,0:T(4,128)(2,1)}, u32[]{:S(2)}, u32[]{:S(2)}) %all-to-all-start.3) | async-done | bytes 1572896 | tf_op jit(solution)/shard_map/all_to_all | solution.py:112
  628.0 5.5 gather_fusion
  637.1 5.7 multiply_reduce_fusion
  (82 shorter events, 40.8 us)
Async XLA Ops:
  0.6 417.4 %copy-start = (bf16[256,2048]{1,0:T(8,128)(2,1)S(1)}, bf16[256,2048]{1,0:T(8,128)(2,1)}, u32[]{:S(2)}) copy-start(bf16[256,2048]{1,0:T(8,128)(2,1)} %param.24) | copy-start | bytes 3145732
  0.6 12.4 %copy-start.4 = (bf16[1,128,1024]{2,1,0:T(8,128)(2,1)S(1)}, bf16[1,128,1024]{2,1,0:T(8,128)(2,1)}, u32[]{:S(2)}) copy-start(bf16[1,128,1024]{2,1,0:T(8,128)(2,1)} %param.16) | copy-start | bytes 786436
  21.2 1.0 copy-start.3
  22.3 3.0 copy-start.7
  22.3 3.1 copy-start.6
  32.0 3.7 copy-start.8
  35.7 2.1 copy-start.2
  396.0 12.1 %copy-start.9 = (bf16[256,2048]{1,0:T(8,128)(2,1)S(1)}, bf16[256,2048]{1,0:T(8,128)(2,1)}, u32[]{:S(2)}) copy-start(bf16[256,2048]{1,0:T(8,128)(2,1)} %param.22) | copy-start | bytes 3145732
  408.1 6.4 copy-start.1
  408.1 6.6 %copy-start.10 = (bf16[256,2048]{1,0:T(8,128)(2,1)S(1)}, bf16[256,2048]{1,0:T(8,128)(2,1)}, u32[]{:S(2)}) copy-start(bf16[256,2048]{1,0:T(8,128)(2,1)} %param.23) | copy-start | bytes 3145732
  414.7 3.3 copy-start.11
  442.3 6.9 %copy-start.5 = (s32[1,128,2]{1,2,0:T(2,128)S(1)}, s32[1,128,2]{1,2,0:T(2,128)}, u32[]{:S(2)}) copy-start(s32[1,128,2]{1,2,0:T(2,128)} %param.20) | copy-start | bytes 3076
  442.4 143.9 %all-to-all-start.2 = ((bf16[2,16,98304]{2,0,1:T(2,128)(2,1)}), bf16[2,16,98304]{2,0,1:T(2,128)(2,1)}, u32[]{:S(2)}, u32[]{:S(2)}) async-start(bf16[2,16,98304]{2,0,1:T(2,128)(2,1)} %copy.91), calls=%async_computation.2 | async-start | bytes 12582912 | tf_op jit(solution)/shard_map/all_to_all | solution.py:108
  449.9 11.8 %slice-start = ((s8[12582912]{0:T(1024)(128)(4,1)}), s8[4194304]{0:T(1024)(128)(4,1)S(1)}, s32[]{:S(2)}) async-start(s8[12582912]{0:T(1024)(128)(4,1)} %bitcast.52), calls=%async_computation.4 | async-start | bytes 8388608
  449.9 11.8 %slice-start.1 = ((s8[12582912]{0:T(1024)(128)(4,1)}), s8[4194304]{0:T(1024)(128)(4,1)S(1)}, s32[]{:S(2)}) async-start(s8[12582912]{0:T(1024)(128)(4,1)} %bitcast.52), calls=%async_computation.5 | async-start | bytes 8388608
  455.6 6.0 slice-start.2
  455.6 6.0 copy-start.12
  455.6 6.0 copy-start.14
  460.5 1.2 copy-start.13
  599.9 24.9 %all-to-all-start.3 = ((bf16[2,4,98304]{2,1,0:T(4,128)(2,1)}), bf16[2,4,98304]{2,1,0:T(4,128)(2,1)}, u32[]{:S(2)}, u32[]{:S(2)}) async-start(bf16[2,4,98304]{2,1,0:T(4,128)(2,1)} %copy.92), calls=%async_computation.3 | async-start | bytes 3145728 | tf_op jit(solution)/shard_map/all_to_all | solution.py:112
where the time goes:
time: 651 us; the launch traced here: 644 us
  blocking collectives  333 us (51%)
  waiting for transfers between devices  135 us (21%)
  local copies, waits for them, and re-layouts  103 us (16%)
  matrix products  39.4 us (6%)
  other arithmetic  20.8 us (3%)
  starting transfers between devices  11.6 us (2%)
    all_to_all x1, blocking collectives, per_device(): lax.all_to_all(widened.reshape(ctx_count, exp_count, slot_width), 'exp',...  278 us
    all_to_all x1, waiting for transfers between devices, per_device(): lax.all_to_all(piece_out, 'exp', split_axis=1, concat_axis=1, tiled=True)  121 us
    all_to_all x1, blocking collectives, per_device(): lax.all_to_all(plain_slots, 'ctx', split_axis=0, concat_axis=0, tiled=True)  38.6 us
    reshape x2, local copies, waits for them, and re-layouts, per_device(): piece_out = piece_out.reshape(ctx_count, exp_count, out_width)  19.9 us
    all_to_all x1, local copies, waits for them, and re-layouts, per_device(): lax.all_to_all(widened.reshape(ctx_count, exp_count, slot_width), 'exp',...  16 us
    all_to_all x1, waiting for transfers between devices, per_device(): lax.all_to_all(piece_sums.astype(jnp.bfloat16), 'ctx', split_axis=0, conc...  13.4 us
  transfers between devices with their start and end apart: 2, of which 2 were waited for; matrix products, arithmetic and copies ran while one was open for 3% of the time, Pallas kernels for 0%

commit v1 on v0

v1 whole, which is shorter than its diff:
```python
import functools

import jax
import jax.numpy as jnp
from jax import lax
from jax.experimental import pallas as pl
from jax.experimental.pallas import tpu as pltpu
from jax.sharding import PartitionSpec as P

HEADS = 8
HD = 128
SHARDS = 4
UNIT = 48
VMEM_LIMIT = 48 * 1024 * 1024
AXES = ("ctx", "exp")

NT = (((1,), (1,)), ((), ()))
TN = (((0,), (0,)), ((), ()))


def dot(a, b, dims=(((1,), (0,)), ((), ()))):
    return lax.dot_general(a, b, dims, preferred_element_type=jnp.float32)


def params():
    return pltpu.CompilerParams(vmem_limit_bytes=VMEM_LIMIT)


VMEM = functools.partial(pl.BlockSpec, memory_space=pltpu.VMEM)
SMEM = functools.partial(pl.BlockSpec, memory_space=pltpu.SMEM)
ANY = functools.partial(pl.BlockSpec, memory_space=pl.ANY)


def choosers(pos, slots):
    tokens = pos.shape[0]
    line = lax.broadcasted_iota(jnp.int32, (tokens, slots), 1)
    return [(pos[:, k : k + 1] == line).astype(jnp.bfloat16) for k in range(2)]


def slot_kernel(capacity, slots, me_ref, ids_ref, gates_ref, grad_ref, pos_ref, *unit_refs):
    ids = ids_ref[...]
    tokens = ids.shape[0]
    lanes = lax.broadcasted_iota(jnp.int32, (tokens, 128), 1)
    hot = [(ids[:, k : k + 1] == lanes).astype(jnp.float32) for k in range(2)]
    later = lax.broadcasted_iota(jnp.int32, (tokens, tokens), 0)
    earlier = lax.broadcasted_iota(jnp.int32, (tokens, tokens), 1)
    lower = (later > earlier).astype(jnp.bfloat16)
    before = dot(lower, (hot[0] + hot[1]).astype(jnp.bfloat16))
    me = me_ref[0]
    pos = []
    for k in range(2):
        slot = jnp.sum(hot[k] * before, axis=1, keepdims=True).astype(jnp.int32)
        pos.append((ids[:, k : k + 1] ^ me) * capacity + slot)
    pair = lax.broadcasted_iota(jnp.int32, (tokens, 2), 1)
    pos = jnp.where(pair == 0, pos[0], pos[1])
    pos_ref[...] = pos
    pick = choosers(pos, slots)
    grad = grad_ref[...].astype(jnp.float32)
    gates = gates_ref[...]
    placed = 0.0
    for k in range(2):
        rows = (gates[:, k : k + 1] * grad).astype(jnp.bfloat16)
        placed = placed + dot(pick[k], rows, TN)
    store_units(placed, unit_refs)


def store_units(placed, unit_refs):
    placed = placed.astype(jnp.bfloat16)
    rows = unit_refs[0].shape[0]
    for n, ref in enumerate(unit_refs):
        ref[...] = placed[n * rows : (n + 1) * rows]


def attend_kernel(pieces, *refs):
    query_ref = refs[0]
    key_refs = refs[1 : 1 + pieces]
    value_refs = refs[1 + pieces : 1 + 2 * pieces]
    token_ref, proj_ref, scale_ref, shift_ref, pos_ref = refs[1 + 2 * pieces : 6 + 2 * pieces]
    mixed_ref = refs[6 + 2 * pieces]
    unit_refs = refs[7 + 2 * pieces : -1]
    attended_ref = refs[-1]
    for head in range(HEADS):
        cols = slice(head * HD, (head + 1) * HD)
        query = query_ref[:, cols]
        scores = [dot(query, ref[:, cols], NT) * (HD ** (-0.5)) for ref in key_refs]
        top = functools.reduce(
            jnp.maximum, [jnp.max(piece, axis=1, keepdims=True) for piece in scores]
        )
        weights = [jnp.exp(piece - top) for piece in scores]
        total = functools.reduce(
            jnp.add, [jnp.sum(piece, axis=1, keepdims=True) for piece in weights]
        )
        accum = functools.reduce(
            jnp.add,
            [
                dot(piece.astype(jnp.bfloat16), ref[:, cols])
                for piece, ref in zip(weights, value_refs)
            ],
        )
        attended_ref[:, cols] = (accum / total).astype(jnp.bfloat16)
    mixed = token_ref[...].astype(jnp.float32) + dot(attended_ref[...], proj_ref[...])
    mixed_ref[...] = mixed
    mean_square = jnp.mean(mixed * mixed, axis=1, keepdims=True)
    normed = mixed * lax.rsqrt(mean_square + 1e-06) * (1.0 + scale_ref[...]) + shift_ref[...]
    normed = normed.astype(jnp.bfloat16)
    slots = len(unit_refs) * unit_refs[0].shape[0]
    pick = choosers(pos_ref[...], slots)
    store_units(dot(pick[0] + pick[1], normed, TN), unit_refs)


def load_rows(block_refs, rows_ref, sem):
    copies = []
    for n, ref in enumerate(block_refs):
        rows = ref.shape[0]
        copies.append(
            pltpu.make_async_copy(ref, rows_ref.at[pl.ds(n * rows, rows)], sem.at[n])
        )
    for copy in copies:
        copy.start()
    return copies


def forward_kernel(count, *refs):
    blocks = refs[:count]
    gate_ref, up_ref, down_ref, keep_ref, send_ref, gate_pre_ref, up_pre_ref, rows_ref, sem = refs[
        count:
    ]
    for copy in load_rows(blocks, rows_ref, sem):
        copy.wait()
    rows = rows_ref[...]
    gate_pre = dot(rows, gate_ref[...], NT)
    up_pre = dot(rows, up_ref[...], NT)
    gate_pre_ref[...] = gate_pre
    up_pre_ref[...] = up_pre
    hidden = (gate_pre * jax.nn.sigmoid(gate_pre) * up_pre).astype(jnp.bfloat16)
    half = rows.shape[0] // 2
    send_ref[...] = dot(hidden[half:], down_ref[...]).astype(jnp.bfloat16)
    keep_ref[...] = dot(hidden[:half], down_ref[...]).astype(jnp.bfloat16)


def forward(blocks, w_gate, w_up, w_down):
    rows = sum(block.shape[0] for block in blocks)
    fs, width = w_gate.shape
    half = jax.ShapeDtypeStruct((rows // 2, width), jnp.bfloat16)
    pre = jax.ShapeDtypeStruct((rows, fs), jnp.float32)
    return pl.pallas_call(
        functools.partial(forward_kernel, len(blocks)),
        out_shape=(half, half, pre, pre),
        in_specs=[ANY()] * len(blocks) + [VMEM()] * 3,
        out_specs=[VMEM()] * 4,
        scratch_shapes=[
            pltpu.VMEM((rows, width), jnp.bfloat16),
            pltpu.SemaphoreType.DMA((len(blocks),)),
        ],
        compiler_params=params(),
        cost_estimate=pl.CostEstimate(
            flops=6 * rows * fs * width, bytes_accessed=8 * rows * width, transcendentals=0
        ),
        name="forward",
    )(*blocks, w_gate, w_up, w_down)


def backward_kernel(chunks, count, *refs):
    gate_pre_refs = refs[:chunks]
    up_pre_refs = refs[chunks : 2 * chunks]
    rows_in = refs[2 * chunks : 2 * chunks + count]
    cots_in = refs[2 * chunks + count : 2 * chunks + 2 * count]
    down_ref, gate_out, up_out, down_out, rows_ref, cots_ref, side_ref, sem, cot_sem = refs[
        2 * chunks + 2 * count :
    ]
    row_copies = load_rows(rows_in, rows_ref, sem)
    cot_copies = load_rows(cots_in, cots_ref, cot_sem)
    for copy in cot_copies:
        copy.wait()
    done = 0
    for n in range(chunks):
        rows = gate_pre_refs[n].shape[0]
        part = pl.ds(done, rows)
        done += rows
        gate_pre = gate_pre_refs[n][...]
        up_pre = up_pre_refs[n][...]
        hidden_grad = dot(cots_ref[part], down_ref[...], NT)
        sigmoid = jax.nn.sigmoid(gate_pre)
        active = gate_pre * sigmoid
        side_ref[0, part] = (active * up_pre).astype(jnp.bfloat16)
        side_ref[1, part] = (
            hidden_grad * up_pre * sigmoid * (1.0 + gate_pre * (1.0 - sigmoid))
        ).astype(jnp.bfloat16)
        side_ref[2, part] = (hidden_grad * active).astype(jnp.bfloat16)
    down_out[...] = dot(side_ref[0], cots_ref[...], TN).astype(jnp.bfloat16)
    for copy in row_copies:
        copy.wait()
    gate_out[...] = dot(side_ref[1], rows_ref[...], TN).astype(jnp.bfloat16)
    up_out[...] = dot(side_ref[2], rows_ref[...], TN).astype(jnp.bfloat16)


def backward(gate_pres, up_pres, rows_in, cots_in, w_down):
    rows = sum(block.shape[0] for block in rows_in)
    fs, width = w_down.shape
    count = len(rows_in)
    out = jax.ShapeDtypeStruct((fs, width), jnp.bfloat16)
    return pl.pallas_call(
        functools.partial(backward_kernel, len(gate_pres), count),
        out_shape=(out, out, out),
        in_specs=[VMEM()] * (2 * len(gate_pres)) + [ANY()] * (2 * count) + [VMEM()],
        out_specs=[VMEM()] * 3,
        scratch_shapes=[
            pltpu.VMEM((rows, width), jnp.bfloat16),
            pltpu.VMEM((rows, width), jnp.bfloat16),
            pltpu.VMEM((3, rows, fs), jnp.bfloat16),
            pltpu.SemaphoreType.DMA((count,)),
            pltpu.SemaphoreType.DMA((count,)),
        ],
        compiler_params=params(),
        cost_estimate=pl.CostEstimate(
            flops=8 * rows * fs * width, bytes_accessed=6 * rows * width, transcendentals=0
        ),
        name="backward",
    )(*gate_pres, *up_pres, *rows_in, *cots_in, w_down)


def combine_kernel(count, *refs):
    mixed_ref, gates_ref, pos_ref = refs[:3]
    units = refs[3 : 3 + count]
    out_ref, rows_ref = refs[3 + count :]
    size = units[0].shape[0]
    for n, ref in enumerate(units):
        rows_ref[n * size : (n + 1) * size] = ref[...]
    pick = choosers(pos_ref[...], count * size)
    gates = gates_ref[...]
    rows = rows_ref[...]
    total = gates[:, 0:1] * dot(pick[0], rows) + gates[:, 1:2] * dot(pick[1], rows)
    out_ref[...] = (mixed_ref[...] + total).astype(jnp.bfloat16)


def per_device(
    tokens,
    queries,
    keys,
    values,
    out_proj,
    mod_scale,
    mod_shift,
    expert_ids,
    gates,
    w_gate,
    w_up,
    w_down,
    out_grad,
):
    n_ctx = lax.axis_size("ctx")
    n_exp = lax.axis_size("exp")
    groups = n_exp // SHARDS
    experts = n_ctx * groups
    local = tokens.shape[1]
    width = tokens.shape[2]
    capacity = 3 * local // experts
    slots = experts * capacity
    bundle = max(1, UNIT // capacity)
    units = experts // bundle
    unit_rows = bundle * capacity
    assert n_ctx & (n_ctx - 1) == 0 and groups & (groups - 1) == 0

    def shifted(value, ctx=0, group=0, shard=0):
        moves = []
        for c in range(n_ctx):
            for e in range(n_exp):
                moves.append((c * n_exp + e, (c ^ ctx) * n_exp + (e ^ (group * SHARDS + shard))))
        return lax.ppermute(value, AXES, moves)

    def exchanged(blocks):
        got = []
        for n, block in enumerate(blocks):
            parts = []
            for m in range(bundle):
                offset = n * bundle + m
                part = block if bundle == 1 else block[m * capacity : (m + 1) * capacity]
                if offset:
                    part = shifted(part, offset // groups, offset % groups)
                parts.append(part)
            got.append(parts[0] if bundle == 1 else jnp.concatenate(parts, axis=0))
        return got

    def spread(block):
        across = shifted(block, shard=2)
        return [block, across, shifted(block, shard=1), shifted(across, shard=1)]

    key_pieces = [keys[0]]
    value_pieces = [values[0]]
    for step in range(1, n_ctx):
        key_pieces.append(shifted(keys[0], ctx=step))
        value_pieces.append(shifted(values[0], ctx=step))

    me = lax.axis_index("ctx") * groups + lax.axis_index("exp") // SHARDS
    me = me.astype(jnp.int32).reshape(1)
    unit_shape = [jax.ShapeDtypeStruct((unit_rows, width), jnp.bfloat16)] * units
    pos, *cot_units = pl.pallas_call(
        functools.partial(slot_kernel, capacity, slots),
        out_shape=[jax.ShapeDtypeStruct((local, 2), jnp.int32)] + unit_shape,
        in_specs=[SMEM()] + [VMEM()] * 3,
        out_specs=[VMEM()] * (1 + units),
        compiler_params=params(),
        name="slots",
    )(me, expert_ids[0], gates[0], out_grad[0])

    cots = [spread(block) for block in exchanged(cot_units)]

    mixed, *row_units = pl.pallas_call(
        functools.partial(attend_kernel, n_ctx),
        out_shape=[jax.ShapeDtypeStruct((local, width), jnp.float32)] + unit_shape,
        in_specs=[VMEM()] * (6 + 2 * n_ctx),
        out_specs=[VMEM()] * (1 + units),
        scratch_shapes=[pltpu.VMEM((local, HEADS * HD), jnp.bfloat16)],
        compiler_params=params(),
        name="attend",
    )(
        queries[0],
        *key_pieces,
        *value_pieces,
        tokens[0],
        out_proj,
        mod_scale,
        mod_shift,
        pos,
    )

    rows = [spread(block) for block in exchanged(row_units)]

    per_chunk = 2
    gate_pres, up_pres, row_blocks, cot_blocks, results = [], [], [], [], []
    for first in range(0, units, per_chunk):
        some = range(first, first + per_chunk)
        order = [(k, n) for k in range(SHARDS) for n in some]
        blocks = [rows[n][k] for k, n in order]
        keep, send, gate_pre, up_pre = forward(blocks, w_gate, w_up, w_down)
        row_blocks += blocks
        cot_blocks += [cots[n][k] for k, n in order]
        gate_pres.append(gate_pre)
        up_pres.append(up_pre)
        other = shifted(send, shard=1)
        half = keep.shape[0] // 2
        mine = keep[:half].astype(jnp.float32) + other[:half].astype(jnp.float32)
        theirs = keep[half:].astype(jnp.float32) + other[half:].astype(jnp.float32)
        across = shifted(theirs.astype(jnp.bfloat16), shard=2)
        sums = (mine + across.astype(jnp.float32)).astype(jnp.bfloat16)
        results += [sums[n * unit_rows : (n + 1) * unit_rows] for n in range(per_chunk)]
    returned = exchanged(results)

    grad_gate, grad_up, grad_down = backward(gate_pres, up_pres, row_blocks, cot_blocks, w_down)

    layer_out = pl.pallas_call(
        functools.partial(combine_kernel, units),
        out_shape=jax.ShapeDtypeStruct((local, width), jnp.bfloat16),
        in_specs=[VMEM()] * (3 + units),
        out_specs=VMEM(),
        scratch_shapes=[pltpu.VMEM((slots, width), jnp.bfloat16)],
        compiler_params=params(),
        name="combine",
    )(mixed, gates[0], pos, *returned)
    return (layer_out[None], grad_gate, grad_up, grad_down)


def solution(mesh):
    placed = (
        P("exp", "ctx", None),
        P("exp", "ctx", None),
        P("exp", "ctx", None),
        P("exp", "ctx", None),
        P(),
        P("exp", None),
        P("exp", None),
        P("exp", "ctx", None),
        P("exp", "ctx", None),
        P(("ctx", "exp"), None),
        P(("ctx", "exp"), None),
        P(("ctx", "exp"), None),
        P("exp", "ctx", None),
    )
    return jax.shard_map(
        per_device,
        mesh=mesh,
        in_specs=placed,
        out_specs=(
            P("exp", "ctx", None),
            P(("ctx", "exp"), None),
            P(("ctx", "exp"), None),
            P(("ctx", "exp"), None),
        ),
        check_vma=False,
    )
```

time: 651 us -> 242 us (0.37)
  the two profiles are of different devices: /device:TPU:10 before, /device:TPU:0 now
where the time goes in v1:
time: 242 us
  waiting for transfers between devices  107 us (44%)
  starting transfers between devices  63.3 us (26%)
  Pallas kernels  52.2 us (22%)
  local copies, waits for them, and re-layouts  12.2 us (5%)
  other arithmetic  5.31 us (2%)
    ppermute x79, waiting for transfers between devices, shifted(): return lax.ppermute(value, AXES, moves)  107 us
    ppermute x79, starting transfers between devices, shifted(): return lax.ppermute(value, AXES, moves)  63.3 us
    pallas_call x1, Pallas kernels, backward(): pl.pallas_call(functools.partial(backward_kernel, len(gate_pres), count),...  23.6 us
    pallas_call x4, Pallas kernels, forward(): pl.pallas_call(functools.partial(forward_kernel, len(blocks)), out_shape=...  19.9 us
    unnamed x110, local copies, waits for them, and re-layouts  12.1 us
    pallas_call x1, Pallas kernels, per_device(): pl.pallas_call(functools.partial(attend_kernel, n_ctx), out_shape=[jax.Sh...  5.64 us
  transfers between devices with their start and end apart: 79, of which 25 were waited for; matrix products, arithmetic and copies ran while one was open for 3% of the time, Pallas kernels for 19%

profile of v1, /device:TPU:0, one launch (start us, length us, event | category | flops | bytes accessed | tf_op | source)
XLA Modules:
  0.0 241.5 jit_solution(14479175009202925160)
XLA Ops:
  8.0 3.1 %collective-permute-done.refs_2_ = bf16[128,1024]{1,0:T(8,128)(2,1)S(1)} collective-permute-done((bf16[128,1024]{1,0:T(8,128)(2,1)}, bf16[128,1024]{1,0:T(8,128)(2,1)S(1)}, u32[]{:S(2)}, u32[]{:S(2)}) %collective-permute-start) | collective-permute-done | bytes 262176 | tf_op jit(solution)/shard_map/ppermute | solution.py:269
  11.0 4.8 %collective-permute-done.1.refs_4_ = bf16[128,1024]{1,0:T(8,128)(2,1)S(1)} collective-permute-done((bf16[128,1024]{1,0:T(8,128)(2,1)}, bf16[128,1024]{1,0:T(8,128)(2,1)S(1)}, u32[]{:S(2)}, u32[]{:S(2)}) %collective-permute-start.1) | collective-permute-done | bytes 262176 | tf_op jit(solution)/shard_map/ppermute | solution.py:269
  21.1 5.6 %attend.1 = (f32[128,2048]{1,0:T(8,128)S(1)}, bf16[48,2048]{1,0:T(8,128)(2,1)S(1)}, bf16[48,2048]{1,0:T(8,128)(2,1)S(1)}, bf16[48,2048]{1,0:T(8,128)(2,1)S(1)}, ...) custom-call(bf16[128,1024]{1,0:T(8,128)(2,1)S(1)} %bitcast.13, ...), custom_call_target="tpu_custom_call" | custom-call | tf_op jit(solution)/shard_map/attend/pallas_call | solution.py:308
  35.9 3.7 %collective-permute-start.36 = (bf16[48,2048]{1,0:T(8,128)(2,1)S(1)}, bf16[48,2048]{1,0:T(8,128)(2,1)S(1)}, u32[]{:S(2)}, u32[]{:S(2)}) collective-permute-start(bf16[48,2048]{1,0:T(8,128)(2,1)S(1)} %get-tuple-element.55), channel_id=1, source_target_pairs={{0,24},{1,25},{2,26},{3,27},{4,28},{5,29},{6,30},{7,31},{8,16},{9,... | collective-permute-start | bytes 589832 | tf_op jit(solution)/shard_map/ppermute | solution.py:269
  39.5 7.7 %collective-permute-done.12.refs_0_.refs_16_ = bf16[48,2048]{1,0:T(8,128)(2,1)S(1)} collective-permute-done((bf16[48,2048]{1,0:T(8,128)(2,1)S(1)}, bf16[48,2048]{1,0:T(8,128)(2,1)S(1)}, u32[]{:S(2)}, u32[]{:S(2)}) %collective-permute-start.12) | collective-permute-done | bytes 196640 | tf_op jit(solution)/shard_map/ppermute | solution.py:269
  47.2 3.4 %collective-permute-start.37 = (bf16[48,2048]{1,0:T(8,128)(2,1)S(1)}, bf16[48,2048]{1,0:T(8,128)(2,1)S(1)}, u32[]{:S(2)}, u32[]{:S(2)}) collective-permute-start(bf16[48,2048]{1,0:T(8,128)(2,1)S(1)} %get-tuple-element.56), channel_id=1, source_target_pairs={{0,28},{1,29},{2,30},{3,31},{4,24},{5,25},{6,26},{7,27},{8,20},{9,... | collective-permute-start | bytes 589832 | tf_op jit(solution)/shard_map/ppermute | solution.py:269
  51.7 13.1 %collective-permute-done.36.refs_0_.refs_32_ = bf16[48,2048]{1,0:T(8,128)(2,1)S(1)} collective-permute-done((bf16[48,2048]{1,0:T(8,128)(2,1)S(1)}, bf16[48,2048]{1,0:T(8,128)(2,1)S(1)}, u32[]{:S(2)}, u32[]{:S(2)}) %collective-permute-start.36) | collective-permute-done | bytes 196640 | tf_op jit(solution)/shard_map/ppermute | solution.py:269
  67.9 4.8 %collective-permute-done.14.refs_2_.refs_18_ = bf16[48,2048]{1,0:T(8,128)(2,1)S(1)} collective-permute-done((bf16[48,2048]{1,0:T(8,128)(2,1)S(1)}, bf16[48,2048]{1,0:T(8,128)(2,1)S(1)}, u32[]{:S(2)}, u32[]{:S(2)}) %collective-permute-start.14) | collective-permute-done | bytes 196640 | tf_op jit(solution)/shard_map/ppermute | solution.py:269
  72.6 4.2 %collective-permute-done.15.refs_3_.refs_19_ = bf16[48,2048]{1,0:T(8,128)(2,1)S(1)} collective-permute-done((bf16[48,2048]{1,0:T(8,128)(2,1)S(1)}, bf16[48,2048]{1,0:T(8,128)(2,1)S(1)}, u32[]{:S(2)}, u32[]{:S(2)}) %collective-permute-start.15) | collective-permute-done | bytes 196640 | tf_op jit(solution)/shard_map/ppermute | solution.py:269
  77.9 3.2 %collective-permute-done.26.refs_2_.refs_26_ = bf16[48,2048]{1,0:T(8,128)(2,1)S(1)} collective-permute-done((bf16[48,2048]{1,0:T(8,128)(2,1)S(1)}, bf16[48,2048]{1,0:T(8,128)(2,1)S(1)}, u32[]{:S(2)}, u32[]{:S(2)}) %collective-permute-start.26) | collective-permute-done | bytes 196640 | tf_op jit(solution)/shard_map/ppermute | solution.py:269
  83.1 4.8 %forward.4 = (bf16[192,2048]{1,0:T(8,128)(2,1)S(1)}, bf16[192,2048]{1,0:T(8,128)(2,1)S(1)}, f32[384,256]{1,0:T(8,128)S(1)}, f32[384,256]{1,0:T(8,128)S(1)}) custom-call(bf16[48,2048]{1,0:T(8,128)(2,1)S(1)} %get-tuple-element.43.refs_0_.refs_8_, bf16[48,2048]{1,0:T(8,128)(2,1)S(1)} %collective-permute-done.2.refs_1_.refs_9_, ...), custom_call_target="tpu_custom_call" | custom-call | flops 1207959552 | bytes 6291456 | tf_op jit(solution)/shard_map/forward/pallas_call | solution.py:146
  93.9 5.5 %forward.5 = (bf16[192,2048]{1,0:T(8,128)(2,1)S(1)}, bf16[192,2048]{1,0:T(8,128)(2,1)}, f32[384,256]{1,0:T(8,128)S(1)}, f32[384,256]{1,0:T(8,128)S(1)}) custom-call(bf16[48,2048]{1,0:T(8,128)(2,1)S(1)} %collective-permute-done.12.refs_0_.refs_16_, bf16[48,2048]{1,0:T(8,128)(2,1)S(1)} %collective-permute-done.13.refs_1_.refs_17_, ...), custom_call_target="tpu_custom_call" | custom-call | flops 1207959552 | bytes 6291456 | tf_op jit(solution)/shard_map/forward/pallas_call | solution.py:146
  101.3 4.8 %forward.6 = (bf16[192,2048]{1,0:T(8,128)(2,1)S(1)}, bf16[192,2048]{1,0:T(8,128)(2,1)S(1)}, f32[384,256]{1,0:T(8,128)S(1)}, f32[384,256]{1,0:T(8,128)S(1)}) custom-call(bf16[48,2048]{1,0:T(8,128)(2,1)S(1)} %collective-permute-done.24.refs_0_.refs_24_, bf16[48,2048]{1,0:T(8,128)(2,1)S(1)} %collective-permute-done.25.refs_1_.refs_25_, ...), custom_call_target="tpu_custom_call" | custom-call | flops 1207959552 | bytes 6291456 | tf_op jit(solution)/shard_map/forward/pallas_call | solution.py:146
  108.3 4.8 %forward.7 = (bf16[192,2048]{1,0:T(8,128)(2,1)S(1)}, bf16[192,2048]{1,0:T(8,128)(2,1)S(1)}, f32[384,256]{1,0:T(8,128)S(1)}, f32[384,256]{1,0:T(8,128)S(1)}) custom-call(bf16[48,2048]{1,0:T(8,128)(2,1)S(1)} %collective-permute-done.36.refs_0_.refs_32_, bf16[48,2048]{1,0:T(8,128)(2,1)S(1)} %collective-permute-done.37.refs_1_.refs_33_, ...), custom_call_target="tpu_custom_call" | custom-call | flops 1207959552 | bytes 6291456 | tf_op jit(solution)/shard_map/forward/pallas_call | solution.py:146
  120.1 9.7 %collective-permute-done.10 = bf16[96,2048]{1,0:T(8,128)(2,1)S(1)} collective-permute-done((bf16[96,2048]{1,0:T(8,128)(2,1)S(1)}, bf16[96,2048]{1,0:T(8,128)(2,1)S(1)}, u32[]{:S(2)}, u32[]{:S(2)}) %collective-permute-start.10) | collective-permute-done | bytes 393248 | tf_op jit(solution)/shard_map/ppermute | solution.py:269
  132.2 7.8 %collective-permute-done.21 = bf16[96,2048]{1,0:T(8,128)(2,1)S(1)} collective-permute-done((bf16[96,2048]{1,0:T(8,128)(2,1)S(1)}, bf16[96,2048]{1,0:T(8,128)(2,1)S(1)}, u32[]{:S(2)}, u32[]{:S(2)}) %collective-permute-start.21) | collective-permute-done | bytes 393248 | tf_op jit(solution)/shard_map/ppermute | solution.py:269
  155.4 10.6 %collective-permute-done.71.refs_64_ = bf16[48,2048]{1,0:T(8,128)(2,1)S(1)} collective-permute-done((bf16[48,2048]{1,0:T(8,128)(2,1)S(1)}, bf16[48,2048]{1,0:T(8,128)(2,1)S(1)}, u32[]{:S(2)}, u32[]{:S(2)}) %collective-permute-start.71) | collective-permute-done | bytes 196640 | tf_op jit(solution)/shard_map/ppermute | solution.py:269
  169.5 4.3 %collective-permute-done.57.refs_50_ = bf16[48,2048]{1,0:T(8,128)(2,1)S(1)} collective-permute-done((bf16[48,2048]{1,0:T(8,128)(2,1)S(1)}, bf16[48,2048]{1,0:T(8,128)(2,1)S(1)}, u32[]{:S(2)}, u32[]{:S(2)}) %collective-permute-start.57) | collective-permute-done | bytes 196640 | tf_op jit(solution)/shard_map/ppermute | solution.py:269
  174.7 3.3 %collective-permute-done.58.refs_51_ = bf16[48,2048]{1,0:T(8,128)(2,1)S(1)} collective-permute-done((bf16[48,2048]{1,0:T(8,128)(2,1)S(1)}, bf16[48,2048]{1,0:T(8,128)(2,1)S(1)}, u32[]{:S(2)}, u32[]{:S(2)}) %collective-permute-start.58) | collective-permute-done | bytes 196640 | tf_op jit(solution)/shard_map/ppermute | solution.py:269
  182.2 4.2 %collective-permute-done.66.refs_59_ = bf16[48,2048]{1,0:T(8,128)(2,1)S(1)} collective-permute-done((bf16[48,2048]{1,0:T(8,128)(2,1)S(1)}, bf16[48,2048]{1,0:T(8,128)(2,1)S(1)}, u32[]{:S(2)}, u32[]{:S(2)}) %collective-permute-start.66) | collective-permute-done | bytes 196640 | tf_op jit(solution)/shard_map/ppermute | solution.py:269
  190.7 3.7 %collective-permute-done.74.refs_67_ = bf16[48,2048]{1,0:T(8,128)(2,1)S(1)} collective-permute-done((bf16[48,2048]{1,0:T(8,128)(2,1)S(1)}, bf16[48,2048]{1,0:T(8,128)(2,1)S(1)}, u32[]{:S(2)}, u32[]{:S(2)}) %collective-permute-start.74) | collective-permute-done | bytes 196640 | tf_op jit(solution)/shard_map/ppermute | solution.py:269
  201.9 4.8 %collective-permute-done.11.refs_4_ = bf16[48,2048]{1,0:T(8,128)(2,1)S(1)} collective-permute-done((bf16[48,2048]{1,0:T(8,128)(2,1)S(1)}, bf16[48,2048]{1,0:T(8,128)(2,1)S(1)}, u32[]{:S(2)}, u32[]{:S(2)}) %collective-permute-start.11) | collective-permute-done | bytes 196640 | tf_op jit(solution)/shard_map/ppermute | solution.py:269
  207.5 5.7 %collective-permute-done.22.refs_5_ = bf16[48,2048]{1,0:T(8,128)(2,1)S(1)} collective-permute-done((bf16[48,2048]{1,0:T(8,128)(2,1)S(1)}, bf16[48,2048]{1,0:T(8,128)(2,1)S(1)}, u32[]{:S(2)}, u32[]{:S(2)}) %collective-permute-start.22) | collective-permute-done | bytes 196640 | tf_op jit(solution)/shard_map/ppermute | solution.py:269
  216.3 23.6 %backward.1 = (bf16[256,2048]{1,0:T(8,128)(2,1)}, bf16[256,2048]{1,0:T(8,128)(2,1)}, bf16[256,2048]{1,0:T(8,128)(2,1)}) custom-call(f32[384,256]{1,0:T(8,128)} %copy-done.11, f32[384,256]{1,0:T(8,128)} %copy-done.13, f32[384,256]{1,0:T(8,128)} %copy-done.15, f32[384,256]{1,0:T(8,128)} %copy-done.17, f32[384,256]{1,0:T(8,128)} %copy-done.12, ...), custom_call_target="tpu_custom_call" | custom-call | flops 6442450944 | bytes 18874368 | tf_op jit(solution)/shard_map/backward/pallas_call | solution.py:202
  (264 shorter events, 88.8 us)
Async XLA Ops:
  30.1 17.1 %collective-permute-start.12 = (bf16[48,2048]{1,0:T(8,128)(2,1)S(1)}, bf16[48,2048]{1,0:T(8,128)(2,1)S(1)}, u32[]{:S(2)}, u32[]{:S(2)}) collective-permute-start(bf16[48,2048]{1,0:T(8,128)(2,1)S(1)} %get-tuple-element.47), channel_id=1, source_target_pairs={{0,8},{1,9},{2,10},{3,11},{4,12},{5,13},{6,14},{7,15},{8,0},{9,1},... | collective-permute-start | bytes 589832 | tf_op jit(solution)/shard_map/ppermute | solution.py:269
  32.7 17.9 %collective-permute-start.13 = (bf16[48,2048]{1,0:T(8,128)(2,1)S(1)}, bf16[48,2048]{1,0:T(8,128)(2,1)S(1)}, u32[]{:S(2)}, u32[]{:S(2)}) collective-permute-start(bf16[48,2048]{1,0:T(8,128)(2,1)S(1)} %get-tuple-element.48), channel_id=1, source_target_pairs={{0,12},{1,13},{2,14},{3,15},{4,8},{5,9},{6,10},{7,11},{8,4},{9,5},... | collective-permute-start | bytes 589832 | tf_op jit(solution)/shard_map/ppermute | solution.py:269
  32.9 18.3 %collective-permute-start.24 = (bf16[48,2048]{1,0:T(8,128)(2,1)S(1)}, bf16[48,2048]{1,0:T(8,128)(2,1)S(1)}, u32[]{:S(2)}, u32[]{:S(2)}) collective-permute-start(bf16[48,2048]{1,0:T(8,128)(2,1)S(1)} %get-tuple-element.51), channel_id=1, source_target_pairs={{0,16},{1,17},{2,18},{3,19},{4,20},{5,21},{6,22},{7,23},{8,24},{9,... | collective-permute-start | bytes 589832 | tf_op jit(solution)/shard_map/ppermute | solution.py:269
  34.5 16.8 %collective-permute-start.25 = (bf16[48,2048]{1,0:T(8,128)(2,1)S(1)}, bf16[48,2048]{1,0:T(8,128)(2,1)S(1)}, u32[]{:S(2)}, u32[]{:S(2)}) collective-permute-start(bf16[48,2048]{1,0:T(8,128)(2,1)S(1)} %get-tuple-element.52), channel_id=1, source_target_pairs={{0,20},{1,21},{2,22},{3,23},{4,16},{5,17},{6,18},{7,19},{8,28},{9,... | collective-permute-start | bytes 589832 | tf_op jit(solution)/shard_map/ppermute | solution.py:269
  35.9 28.9 %collective-permute-start.36 = (bf16[48,2048]{1,0:T(8,128)(2,1)S(1)}, bf16[48,2048]{1,0:T(8,128)(2,1)S(1)}, u32[]{:S(2)}, u32[]{:S(2)}) collective-permute-start(bf16[48,2048]{1,0:T(8,128)(2,1)S(1)} %get-tuple-element.55), channel_id=1, source_target_pairs={{0,24},{1,25},{2,26},{3,27},{4,28},{5,29},{6,30},{7,31},{8,16},{9,... | collective-permute-start | bytes 589832 | tf_op jit(solution)/shard_map/ppermute | solution.py:269
  47.2 18.1 %collective-permute-start.37 = (bf16[48,2048]{1,0:T(8,128)(2,1)S(1)}, bf16[48,2048]{1,0:T(8,128)(2,1)S(1)}, u32[]{:S(2)}, u32[]{:S(2)}) collective-permute-start(bf16[48,2048]{1,0:T(8,128)(2,1)S(1)} %get-tuple-element.56), channel_id=1, source_target_pairs={{0,28},{1,29},{2,30},{3,31},{4,24},{5,25},{6,26},{7,27},{8,20},{9,... | collective-permute-start | bytes 589832 | tf_op jit(solution)/shard_map/ppermute | solution.py:269
  50.6 16.2 %collective-permute-start.4 = (bf16[48,2048]{1,0:T(8,128)(2,1)S(1)}, bf16[48,2048]{1,0:T(8,128)(2,1)S(1)}, u32[]{:S(2)}, u32[]{:S(2)}) collective-permute-start(bf16[48,2048]{1,0:T(8,128)(2,1)S(1)} %collective-permute-done.2.refs_1_.refs_9_), channel_id=1, source_target_pairs={{0,2},{1,3},{2,0},{3,1},{4,6},{5,7},{6,4},{7,5},{8,10},{9,11},{10,... | collective-permute-start | bytes 589832 | tf_op jit(solution)/shard_map/ppermute | solution.py:269
  51.2 15.6 %collective-permute-start.6 = (bf16[48,2048]{1,0:T(8,128)(2,1)S(1)}, bf16[48,2048]{1,0:T(8,128)(2,1)S(1)}, u32[]{:S(2)}, u32[]{:S(2)}) collective-permute-start(bf16[48,2048]{1,0:T(8,128)(2,1)S(1)} %collective-permute-done.2.refs_1_.refs_9_), channel_id=1, source_target_pairs={{0,1},{1,0},{2,3},{3,2},{4,5},{5,4},{6,7},{7,6},{8,9},{9,8},{10,11... | collective-permute-start | bytes 589832 | tf_op jit(solution)/shard_map/ppermute | solution.py:269
  51.2 16.1 %collective-permute-start.7 = (bf16[48,2048]{1,0:T(8,128)(2,1)S(1)}, bf16[48,2048]{1,0:T(8,128)(2,1)S(1)}, u32[]{:S(2)}, u32[]{:S(2)}) collective-permute-start(bf16[48,2048]{1,0:T(8,128)(2,1)S(1)} %collective-permute-done.3.refs_2_.refs_10_), channel_id=1, source_target_pairs={{0,1},{1,0},{2,3},{3,2},{4,5},{5,4},{6,7},{7,6},{8,9},{9,8},{10,11... | collective-permute-start | bytes 589832 | tf_op jit(solution)/shard_map/ppermute | solution.py:269
  89.4 23.8 %collective-permute-start.9 = (bf16[192,2048]{1,0:T(8,128)(2,1)S(1)}, bf16[192,2048]{1,0:T(8,128)(2,1)}, u32[]{:S(2)}, u32[]{:S(2)}) collective-permute-start(bf16[192,2048]{1,0:T(8,128)(2,1)S(1)} %get-tuple-element.46), channel_id=1, source_target_pairs={{0,1},{1,0},{2,3},{3,2},{4,5},{5,4},{6,7},{7,6},{8,9},{9,8},{10,11... | collective-permute-start | bytes 2359304 | tf_op jit(solution)/shard_map/ppermute | solution.py:269
  92.9 14.5 %collective-permute-start.42 = (bf16[48,2048]{1,0:T(8,128)(2,1)S(1)}, bf16[48,2048]{1,0:T(8,128)(2,1)S(1)}, u32[]{:S(2)}, u32[]{:S(2)}) collective-permute-start(bf16[48,2048]{1,0:T(8,128)(2,1)S(1)} %collective-permute-done.38.refs_2_.refs_34_), channel_id=1, source_target_pairs={{0,1},{1,0},{2,3},{3,2},{4,5},{5,4},{6,7},{7,6},{8,9},{9,8},{10,11... | collective-permute-start | bytes 589832 | tf_op jit(solution)/shard_map/ppermute | solution.py:269
  106.9 37.1 %collective-permute-start.49 = (bf16[48,2048]{1,0:T(8,128)(2,1)S(1)}, bf16[48,2048]{1,0:T(8,128)(2,1)}, u32[]{:S(2)}, u32[]{:S(2)}) collective-permute-start(bf16[48,2048]{1,0:T(8,128)(2,1)S(1)} %get-tuple-element.67.refs_40_), channel_id=1, source_target_pairs={{0,2},{1,3},{2,0},{3,1},{4,6},{5,7},{6,4},{7,5},{8,10},{9,11},{10,... | collective-permute-start | bytes 589832 | tf_op jit(solution)/shard_map/ppermute | solution.py:269
  107.4 37.0 %collective-permute-start.51 = (bf16[48,2048]{1,0:T(8,128)(2,1)S(1)}, bf16[48,2048]{1,0:T(8,128)(2,1)}, u32[]{:S(2)}, u32[]{:S(2)}) collective-permute-start(bf16[48,2048]{1,0:T(8,128)(2,1)S(1)} %get-tuple-element.67.refs_40_), channel_id=1, source_target_pairs={{0,1},{1,0},{2,3},{3,2},{4,5},{5,4},{6,7},{7,6},{8,9},{9,8},{10,11... | collective-permute-start | bytes 589832 | tf_op jit(solution)/shard_map/ppermute | solution.py:269
  107.8 34.6 %collective-permute-start.48 = (bf16[48,2048]{1,0:T(8,128)(2,1)}, bf16[48,2048]{1,0:T(8,128)(2,1)}, u32[]{:S(2)}, u32[]{:S(2)}) collective-permute-start(bf16[48,2048]{1,0:T(8,128)(2,1)} %copy-done.25), channel_id=1, source_target_pairs={{0,4},{1,5},{2,6},{3,7},{4,0},{5,1},{6,2},{7,3},{8,12},{9,13},{10,... | collective-permute-start | bytes 589832 | tf_op jit(solution)/shard_map/ppermute | solution.py:269
  116.1 29.5 %collective-permute-start.55 = (bf16[48,2048]{1,0:T(8,128)(2,1)}, bf16[48,2048]{1,0:T(8,128)(2,1)S(1)}, u32[]{:S(2)}, u32[]{:S(2)}) collective-permute-start(bf16[48,2048]{1,0:T(8,128)(2,1)} %copy-done.24), channel_id=1, source_target_pairs={{0,8},{1,9},{2,10},{3,11},{4,12},{5,13},{6,14},{7,15},{8,0},{9,1},... | collective-permute-start | bytes 589832 | tf_op jit(solution)/shard_map/ppermute | solution.py:269
  145.6 20.4 %collective-permute-start.71 = (bf16[48,2048]{1,0:T(8,128)(2,1)S(1)}, bf16[48,2048]{1,0:T(8,128)(2,1)S(1)}, u32[]{:S(2)}, u32[]{:S(2)}) collective-permute-start(bf16[48,2048]{1,0:T(8,128)(2,1)S(1)} %get-tuple-element.73), channel_id=1, source_target_pairs={{0,24},{1,25},{2,26},{3,27},{4,28},{5,29},{6,30},{7,31},{8,16},{9,... | collective-permute-start | bytes 589832 | tf_op jit(solution)/shard_map/ppermute | solution.py:269
  149.4 16.7 %collective-permute-start.45 = (bf16[96,2048]{1,0:T(8,128)(2,1)S(1)}, bf16[96,2048]{1,0:T(8,128)(2,1)S(1)}, u32[]{:S(2)}, u32[]{:S(2)}) collective-permute-start(bf16[96,2048]{1,0:T(8,128)(2,1)S(1)} %add_convert_fusion.1), channel_id=1, source_target_pairs={{0,2},{1,3},{2,0},{3,1},{4,6},{5,7},{6,4},{7,5},{8,10},{9,11},{10,... | collective-permute-start | bytes 1179656 | tf_op jit(solution)/shard_map/ppermute | solution.py:269
  152.2 14.9 %collective-permute-start.72 = (bf16[48,2048]{1,0:T(8,128)(2,1)S(1)}, bf16[48,2048]{1,0:T(8,128)(2,1)S(1)}, u32[]{:S(2)}, u32[]{:S(2)}) collective-permute-start(bf16[48,2048]{1,0:T(8,128)(2,1)S(1)} %get-tuple-element.74), channel_id=1, source_target_pairs={{0,28},{1,29},{2,30},{3,31},{4,24},{5,25},{6,26},{7,27},{8,20},{9,... | collective-permute-start | bytes 589832 | tf_op jit(solution)/shard_map/ppermute | solution.py:269
  196.1 17.1 %collective-permute-start.22 = (bf16[48,2048]{1,0:T(8,128)(2,1)S(1)}, bf16[48,2048]{1,0:T(8,128)(2,1)S(1)}, u32[]{:S(2)}, u32[]{:S(2)}) collective-permute-start(bf16[48,2048]{1,0:T(8,128)(2,1)S(1)} %get-tuple-element.83), channel_id=1, source_target_pairs={{0,8},{1,9},{2,10},{3,11},{4,12},{5,13},{6,14},{7,15},{8,0},{9,1},... | collective-permute-start | bytes 589832 | tf_op jit(solution)/shard_map/ppermute | solution.py:269
  197.9 42.0 %collective-permute-start.23 = (bf16[48,2048]{1,0:T(8,128)(2,1)S(1)}, bf16[48,2048]{1,0:T(8,128)(2,1)S(1)}, u32[]{:S(2)}, u32[]{:S(2)}) collective-permute-start(bf16[48,2048]{1,0:T(8,128)(2,1)S(1)} %get-tuple-element.82), channel_id=1, source_target_pairs={{0,12},{1,13},{2,14},{3,15},{4,8},{5,9},{6,10},{7,11},{8,4},{9,5},... | collective-permute-start | bytes 589832 | tf_op jit(solution)/shard_map/ppermute | solution.py:269
  200.4 39.5 %collective-permute-start.34 = (bf16[48,2048]{1,0:T(8,128)(2,1)S(1)}, bf16[48,2048]{1,0:T(8,128)(2,1)S(1)}, u32[]{:S(2)}, u32[]{:S(2)}) collective-permute-start(bf16[48,2048]{1,0:T(8,128)(2,1)S(1)} %get-tuple-element.81), channel_id=1, source_target_pairs={{0,16},{1,17},{2,18},{3,19},{4,20},{5,21},{6,22},{7,23},{8,24},{9,... | collective-permute-start | bytes 589832 | tf_op jit(solution)/shard_map/ppermute | solution.py:269
  201.9 38.0 %collective-permute-start.35 = (bf16[48,2048]{1,0:T(8,128)(2,1)S(1)}, bf16[48,2048]{1,0:T(8,128)(2,1)S(1)}, u32[]{:S(2)}, u32[]{:S(2)}) collective-permute-start(bf16[48,2048]{1,0:T(8,128)(2,1)S(1)} %get-tuple-element.80), channel_id=1, source_target_pairs={{0,20},{1,21},{2,22},{3,23},{4,16},{5,17},{6,18},{7,19},{8,28},{9,... | collective-permute-start | bytes 589832 | tf_op jit(solution)/shard_map/ppermute | solution.py:269
  206.7 33.2 %collective-permute-start.46 = (bf16[48,2048]{1,0:T(8,128)(2,1)S(1)}, bf16[48,2048]{1,0:T(8,128)(2,1)S(1)}, u32[]{:S(2)}, u32[]{:S(2)}) collective-permute-start(bf16[48,2048]{1,0:T(8,128)(2,1)S(1)} %get-tuple-element.79), channel_id=1, source_target_pairs={{0,24},{1,25},{2,26},{3,27},{4,28},{5,29},{6,30},{7,31},{8,16},{9,... | collective-permute-start | bytes 589832 | tf_op jit(solution)/shard_map/ppermute | solution.py:269
  213.3 26.7 %collective-permute-start.47 = (bf16[48,2048]{1,0:T(8,128)(2,1)S(1)}, bf16[48,2048]{1,0:T(8,128)(2,1)S(1)}, u32[]{:S(2)}, u32[]{:S(2)}) collective-permute-start(bf16[48,2048]{1,0:T(8,128)(2,1)S(1)} %get-tuple-element.78), channel_id=1, source_target_pairs={{0,28},{1,29},{2,30},{3,31},{4,24},{5,25},{6,26},{7,27},{8,20},{9,... | collective-permute-start | bytes 589832 | tf_op jit(solution)/shard_map/ppermute | solution.py:269
  (109 other events, 2058.1 us)

commit v2 on v1

--- a/solution.py
+++ b/solution.py
@@ -10,9 +10,9 @@
 HEADS = 8
 HD = 128
 SHARDS = 4
-UNIT = 48
+PIECE = 16
 VMEM_LIMIT = 48 * 1024 * 1024
-AXES = ("ctx", "exp")
+EXP = ("group", "side", "core")
 
 NT = (((1,), (1,)), ((), ()))
 TN = (((0,), (0,)), ((), ()))
@@ -37,7 +37,7 @@
     return [(pos[:, k : k + 1] == line).astype(jnp.bfloat16) for k in range(2)]
 
 
-def slot_kernel(capacity, slots, me_ref, ids_ref, gates_ref, grad_ref, pos_ref, *unit_refs):
+def slot_kernel(capacity, piece, ids_ref, gates_ref, grad_ref, pos_ref, *chunk_refs):
     ids = ids_ref[...]
     tokens = ids.shape[0]
     lanes = lax.broadcasted_iota(jnp.int32, (tokens, 128), 1)
@@ -46,22 +46,23 @@
     earlier = lax.broadcasted_iota(jnp.int32, (tokens, tokens), 1)
     lower = (later > earlier).astype(jnp.bfloat16)
     before = dot(lower, (hot[0] + hot[1]).astype(jnp.bfloat16))
-    me = me_ref[0]
+    block = chunk_refs[0].shape[0]
     pos = []
     for k in range(2):
         slot = jnp.sum(hot[k] * before, axis=1, keepdims=True).astype(jnp.int32)
-        pos.append((ids[:, k : k + 1] ^ me) * capacity + slot)
+        chunk = slot // piece
+        pos.append(chunk * block + ids[:, k : k + 1] * piece + (slot - chunk * piece))
     pair = lax.broadcasted_iota(jnp.int32, (tokens, 2), 1)
     pos = jnp.where(pair == 0, pos[0], pos[1])
     pos_ref[...] = pos
-    pick = choosers(pos, slots)
+    pick = choosers(pos, block * len(chunk_refs))
     grad = grad_ref[...].astype(jnp.float32)
     gates = gates_ref[...]
     placed = 0.0
     for k in range(2):
         rows = (gates[:, k : k + 1] * grad).astype(jnp.bfloat16)
         placed = placed + dot(pick[k], rows, TN)
-    store_units(placed, unit_refs)
+    store_units(placed, chunk_refs)
 
 
 def store_units(placed, unit_refs):
@@ -249,67 +250,51 @@
     out_grad,
 ):
     n_ctx = lax.axis_size("ctx")
-    n_exp = lax.axis_size("exp")
-    groups = n_exp // SHARDS
-    experts = n_ctx * groups
+    experts = n_ctx * lax.axis_size("group")
     local = tokens.shape[1]
     width = tokens.shape[2]
     capacity = 3 * local // experts
     slots = experts * capacity
-    bundle = max(1, UNIT // capacity)
-    units = experts // bundle
-    unit_rows = bundle * capacity
-    assert n_ctx & (n_ctx - 1) == 0 and groups & (groups - 1) == 0
-
-    def shifted(value, ctx=0, group=0, shard=0):
-        moves = []
-        for c in range(n_ctx):
-            for e in range(n_exp):
-                moves.append((c * n_exp + e, (c ^ ctx) * n_exp + (e ^ (group * SHARDS + shard))))
-        return lax.ppermute(value, AXES, moves)
-
-    def exchanged(blocks):
-        got = []
-        for n, block in enumerate(blocks):
-            parts = []
-            for m in range(bundle):
-                offset = n * bundle + m
-                part = block if bundle == 1 else block[m * capacity : (m + 1) * capacity]
-                if offset:
-                    part = shifted(part, offset // groups, offset % groups)
-                parts.append(part)
-            got.append(parts[0] if bundle == 1 else jnp.concatenate(parts, axis=0))
-        return got
-
-    def spread(block):
-        across = shifted(block, shard=2)
-        return [block, across, shifted(block, shard=1), shifted(across, shard=1)]
+    piece = PIECE if capacity % PIECE == 0 else capacity
+    chunks = capacity // piece
+    block = experts * piece
+
+    def swapped(value, axis, step=1):
+        size = lax.axis_size(axis)
+        return lax.ppermute(value, axis, [(n, n ^ step) for n in range(size)])
+
+    def exchanged(value):
+        shaped = value.reshape(experts, piece, width)
+        moved = lax.all_to_all(shaped, ("ctx", "group"), split_axis=0, concat_axis=0, tiled=True)
+        return moved.reshape(block, width)
+
+    def spread(value):
+        across = swapped(value, "side")
+        return [value, across, swapped(value, "core"), swapped(across, "core")]
 
     key_pieces = [keys[0]]
     value_pieces = [values[0]]
     for step in range(1, n_ctx):
-        key_pieces.append(shifted(keys[0], ctx=step))
-        value_pieces.append(shifted(values[0], ctx=step))
-
-    me = lax.axis_index("ctx") * groups + lax.axis_index("exp") // SHARDS
-    me = me.astype(jnp.int32).reshape(1)
-    unit_shape = [jax.ShapeDtypeStruct((unit_rows, width), jnp.bfloat16)] * units
-    pos, *cot_units = pl.pallas_call(
-        functools.partial(slot_kernel, capacity, slots),
-        out_shape=[jax.ShapeDtypeStruct((local, 2), jnp.int32)] + unit_shape,
-        in_specs=[SMEM()] + [VMEM()] * 3,
-        out_specs=[VMEM()] * (1 + units),
+        key_pieces.append(swapped(keys[0], "ctx", step))
+        value_pieces.append(swapped(values[0], "ctx", step))
+
+    chunk_shape = [jax.ShapeDtypeStruct((block, width), jnp.bfloat16)] * chunks
+    pos, *cot_chunks = pl.pallas_call(
+        functools.partial(slot_kernel, capacity, piece),
+        out_shape=[jax.ShapeDtypeStruct((local, 2), jnp.int32)] + chunk_shape,
+        in_specs=[VMEM()] * 3,
+        out_specs=[VMEM()] * (1 + chunks),
         compiler_params=params(),
         name="slots",
-    )(me, expert_ids[0], gates[0], out_grad[0])
-
-    cots = [spread(block) for block in exchanged(cot_units)]
-
-    mixed, *row_units = pl.pallas_call(
+    )(expert_ids[0], gates[0], out_grad[0])
+
+    cots = [spread(exchanged(value)) for value in cot_chunks]
+
+    mixed, *row_chunks = pl.pallas_call(
         functools.partial(attend_kernel, n_ctx),
-        out_shape=[jax.ShapeDtypeStruct((local, width), jnp.float32)] + unit_shape,
+        out_shape=[jax.ShapeDtypeStruct((local, width), jnp.float32)] + chunk_shape,
         in_specs=[VMEM()] * (6 + 2 * n_ctx),
-        out_specs=[VMEM()] * (1 + units),
+        out_specs=[VMEM()] * (1 + chunks),
         scratch_shapes=[pltpu.VMEM((local, HEADS * HD), jnp.bfloat16)],
         compiler_params=params(),
         name="attend",
@@ -324,34 +309,25 @@
         pos,
     )
 
-    rows = [spread(block) for block in exchanged(row_units)]
-
-    per_chunk = 2
-    gate_pres, up_pres, row_blocks, cot_blocks, results = [], [], [], [], []
-    for first in range(0, units, per_chunk):
-        some = range(first, first + per_chunk)
-        order = [(k, n) for k in range(SHARDS) for n in some]
-        blocks = [rows[n][k] for k, n in order]
+    rows = [spread(exchanged(value)) for value in row_chunks]
+
+    gate_pres, up_pres, returned = [], [], []
+    for blocks in rows:
         keep, send, gate_pre, up_pre = forward(blocks, w_gate, w_up, w_down)
-        row_blocks += blocks
-        cot_blocks += [cots[n][k] for k, n in order]
         gate_pres.append(gate_pre)
         up_pres.append(up_pre)
-        other = shifted(send, shard=1)
-        half = keep.shape[0] // 2
-        mine = keep[:half].astype(jnp.float32) + other[:half].astype(jnp.float32)
-        theirs = keep[half:].astype(jnp.float32) + other[half:].astype(jnp.float32)
-        across = shifted(theirs.astype(jnp.bfloat16), shard=2)
-        sums = (mine + across.astype(jnp.float32)).astype(jnp.bfloat16)
-        results += [sums[n * unit_rows : (n + 1) * unit_rows] for n in range(per_chunk)]
-    returned = exchanged(results)
-
-    grad_gate, grad_up, grad_down = backward(gate_pres, up_pres, row_blocks, cot_blocks, w_down)
+        other = swapped(send, "core")
+        mine = keep[:block].astype(jnp.float32) + other[:block].astype(jnp.float32)
+        theirs = keep[block:].astype(jnp.float32) + other[block:].astype(jnp.float32)
+        across = swapped(theirs.astype(jnp.bfloat16), "side")
+        returned.append(exchanged((mine + across.astype(jnp.float32)).astype(jnp.bfloat16)))
+
+    grad_gate, grad_up, grad_down = backward(gate_pres, up_pres, sum(rows, []), sum(cots, []), w_down)
 
     layer_out = pl.pallas_call(
-        functools.partial(combine_kernel, units),
+        functools.partial(combine_kernel, chunks),
         out_shape=jax.ShapeDtypeStruct((local, width), jnp.bfloat16),
-        in_specs=[VMEM()] * (3 + units),
+        in_specs=[VMEM()] * (3 + chunks),
         out_specs=VMEM(),
         scratch_shapes=[pltpu.VMEM((slots, width), jnp.bfloat16)],
         compiler_params=params(),
@@ -361,30 +337,33 @@
 
 
 def solution(mesh):
+    n_ctx = mesh.shape["ctx"]
+    cut = (n_ctx, mesh.shape["exp"] // SHARDS, SHARDS // 2, 2)
+    mesh = jax.sharding.Mesh(mesh.devices.reshape(cut), ("ctx",) + EXP)
     placed = (
-        P("exp", "ctx", None),
-        P("exp", "ctx", None),
-        P("exp", "ctx", None),
-        P("exp", "ctx", None),
+        P(EXP, "ctx", None),
+        P(EXP, "ctx", None),
+        P(EXP, "ctx", None),
+        P(EXP, "ctx", None),
         P(),
-        P("exp", None),
-        P("exp", None),
-        P("exp", "ctx", None),
-        P("exp", "ctx", None),
-        P(("ctx", "exp"), None),
-        P(("ctx", "exp"), None),
-        P(("ctx", "exp"), None),
-        P("exp", "ctx", None),
+        P(EXP, None),
+        P(EXP, None),
+        P(EXP, "ctx", None),
+        P(EXP, "ctx", None),
+        P(("ctx",) + EXP, None),
+        P(("ctx",) + EXP, None),
+        P(("ctx",) + EXP, None),
+        P(EXP, "ctx", None),
     )
     return jax.shard_map(
         per_device,
         mesh=mesh,
         in_specs=placed,
         out_specs=(
-            P("exp", "ctx", None),
-            P(("ctx", "exp"), None),
-            P(("ctx", "exp"), None),
-            P(("ctx", "exp"), None),
+            P(EXP, "ctx", None),
+            P(("ctx",) + EXP, None),
+            P(("ctx",) + EXP, None),
+            P(("ctx",) + EXP, None),
         ),
         check_vma=False,
     )

time: 242 us -> 230 us (0.950)
  waiting for transfers between devices: 107 us -> 72.2 us
  blocking collectives: 0 us -> 20.4 us
  local copies, waits for them, and re-layouts: 12.2 us -> 25.1 us
  Pallas kernels: 52.2 us -> 41.1 us
  other arithmetic: 5.31 us -> 12.9 us
  starting transfers between devices: 63.3 us -> 55.8 us
    ppermute x79 -> x26, waiting for transfers between devices: 107 us -> 40.7 us  [swapped(): return lax.ppermute(value, axis, [(n, n ^ step) for n in range(size)])]
    ppermute x79 -> x26, starting transfers between devices: 63.3 us -> 18.4 us  [swapped(): return lax.ppermute(value, axis, [(n, n ^ step) for n in range(size)])]
    all_to_all x0 -> x8, starting transfers between devices: none -> 37.4 us  [exchanged(): lax.all_to_all(shaped, ('ctx', 'group'), split_axis=0, concat_axis=0, til...]
    all_to_all x0 -> x8, waiting for transfers between devices: none -> 31.5 us  [exchanged(): lax.all_to_all(shaped, ('ctx', 'group'), split_axis=0, concat_axis=0, til...]
    all_to_all x0 -> x1, blocking collectives: none -> 20.4 us  [exchanged(): lax.all_to_all(shaped, ('ctx', 'group'), split_axis=0, concat_axis=0, til...]
    unnamed x110 -> x68, local copies, waits for them, and re-layouts: 12.1 us -> 25.1 us
    pallas_call x1, Pallas kernels: 23.6 us -> 14 us  [backward(): pl.pallas_call(functools.partial(backward_kernel, len(gate_pres), count),...]
    convert_element_type x8 -> x6, other arithmetic: 5.31 us -> 12.9 us  [the longest x3 6.86 us: per_device(): (mine + across.astype(jnp.float32)).astype(jnp.bfloat16)]
  transfers between devices with their start and end apart: 79 -> 34, of which waited for: 25 -> 11; matrix products, arithmetic and copies ran while one was open for 3% -> 6% of each run, Pallas kernels for 19% -> 14%
where the time goes in v2:
time: 230 us; the launch traced here: 228 us
  waiting for transfers between devices  72.2 us (31%)
  starting transfers between devices  55.8 us (24%)
  Pallas kernels  41.1 us (18%)
  local copies, waits for them, and re-layouts  25.1 us (11%)
  blocking collectives  20.4 us (9%)
  other arithmetic  12.9 us (6%)
    ppermute x26, waiting for transfers between devices, swapped(): return lax.ppermute(value, axis, [(n, n ^ step) for n in range(size)])  40.7 us
    all_to_all x8, starting transfers between devices, exchanged(): lax.all_to_all(shaped, ('ctx', 'group'), split_axis=0, concat_axis=0, til...  37.4 us
    all_to_all x8, waiting for transfers between devices, exchanged(): lax.all_to_all(shaped, ('ctx', 'group'), split_axis=0, concat_axis=0, til...  31.5 us
    unnamed x68, local copies, waits for them, and re-layouts  25.1 us
    all_to_all x1, blocking collectives, exchanged(): lax.all_to_all(shaped, ('ctx', 'group'), split_axis=0, concat_axis=0, til...  20.4 us
    ppermute x26, starting transfers between devices, swapped(): return lax.ppermute(value, axis, [(n, n ^ step) for n in range(size)])  18.4 us
    pallas_call x3, Pallas kernels, forward(): pl.pallas_call(functools.partial(forward_kernel, len(blocks)), out_shape=...  16.7 us
    pallas_call x1, Pallas kernels, backward(): pl.pallas_call(functools.partial(backward_kernel, len(gate_pres), count),...  14 us
  transfers between devices with their start and end apart: 34, of which 11 were waited for; matrix products, arithmetic and copies ran while one was open for 6% of the time, Pallas kernels for 14%

profile of v2, /device:TPU:0, one launch (start us, length us, event | category | flops | bytes accessed | tf_op | source)
XLA Modules:
  0.0 228.5 jit_solution(7809455825174049149)
XLA Ops:
  0.6 3.0 %collective-permute-start = (bf16[128,1024]{1,0:T(8,128)(2,1)}, bf16[128,1024]{1,0:T(8,128)(2,1)S(1)}, u32[]{:S(2)}, u32[]{:S(2)}) collective-permute-start(bf16[128,1024]{1,0:T(8,128)(2,1)} %bitcast.45), channel_id=1, source_target_pairs={{0,16},{16,0},{1,17},{17,1},{2,18},{18,2},{3,19},{19,3},{4,20},{20... | collective-permute-start | bytes 786440 | tf_op jit(solution)/shard_map/ppermute | solution.py:264
  11.0 4.8 %collective-permute-done.1.refs_4_ = bf16[128,1024]{1,0:T(8,128)(2,1)S(1)} collective-permute-done((bf16[128,1024]{1,0:T(8,128)(2,1)}, bf16[128,1024]{1,0:T(8,128)(2,1)S(1)}, u32[]{:S(2)}, u32[]{:S(2)}) %collective-permute-start.1) | collective-permute-done | bytes 262176 | tf_op jit(solution)/shard_map/ppermute | solution.py:264
  21.1 6.6 %attend.1 = (f32[128,2048]{1,0:T(8,128)S(1)}, bf16[128,2048]{1,0:T(8,128)(2,1)S(1)}, bf16[128,2048]{1,0:T(8,128)(2,1)}, bf16[128,2048]{1,0:T(8,128)(2,1)}) custom-call(bf16[128,1024]{1,0:T(8,128)(2,1)S(1)} %bitcast.44, bf16[128,1024]{1,0:T(8,128)(2,1)S(1)} %bitcast.46, bf16[128,1024]{1,0:T(8,128)(2,1)S(1)} %collective-permute-done.refs_2_, ...), custom_call_target="tpu_custom_call" | custom-call | tf_op jit(solution)/shard_map/attend/pallas_call | solution.py:293
  27.7 20.4 %all_to_all.45 = bf16[8,16,2048]{2,1,0:T(8,128)(2,1)S(1)} all-to-all(bf16[8,16,2048]{2,1,0:T(8,128)(2,1)S(1)} %bitcast.43), channel_id=1, replica_groups=mesh['ctx'=2,'group'=4,'side'=2,'core'=2] {'ctx','group'}, dimensions={0} | all-to-all | bytes 1048576 | tf_op jit(solution)/shard_map/all_to_all | solution.py:268
  48.0 3.5 %all-to-all-start.2 = ((bf16[8,16,2048]{2,1,0:T(8,128)(2,1)}), bf16[8,16,2048]{2,1,0:T(8,128)(2,1)S(1)}, u32[]{:S(2)}, u32[]{:S(2)}) async-start(bf16[8,16,2048]{2,1,0:T(8,128)(2,1)} %bitcast.11), calls=%async_computation.2 | async-start | bytes 1048576 | tf_op jit(solution)/shard_map/all_to_all | solution.py:268
  53.1 11.6 %all-to-all-done.2 = bf16[8,16,2048]{2,1,0:T(8,128)(2,1)S(1)} async-done(((bf16[8,16,2048]{2,1,0:T(8,128)(2,1)}), bf16[8,16,2048]{2,1,0:T(8,128)(2,1)S(1)}, u32[]{:S(2)}, u32[]{:S(2)}) %all-to-all-start.2) | async-done | bytes 524320 | tf_op jit(solution)/shard_map/all_to_all | solution.py:268
  64.7 4.1 %all-to-all-start.4 = ((bf16[8,16,2048]{2,1,0:T(8,128)(2,1)}), bf16[8,16,2048]{2,1,0:T(8,128)(2,1)}, u32[]{:S(2)}, u32[]{:S(2)}) async-start(bf16[8,16,2048]{2,1,0:T(8,128)(2,1)} %bitcast.15), calls=%async_computation.4 | async-start | bytes 1048576 | tf_op jit(solution)/shard_map/all_to_all | solution.py:268
  70.9 10.6 %all-to-all-done.4 = bf16[8,16,2048]{2,1,0:T(8,128)(2,1)} async-done(((bf16[8,16,2048]{2,1,0:T(8,128)(2,1)}), bf16[8,16,2048]{2,1,0:T(8,128)(2,1)}, u32[]{:S(2)}, u32[]{:S(2)}) %all-to-all-start.4) | async-done | bytes 524320 | tf_op jit(solution)/shard_map/all_to_all | solution.py:268
  81.5 4.1 %all-to-all-start.6 = ((bf16[8,16,2048]{2,1,0:T(8,128)(2,1)}), bf16[8,16,2048]{2,1,0:T(8,128)(2,1)}, u32[]{:S(2)}, u32[]{:S(2)}) async-start(bf16[8,16,2048]{2,1,0:T(8,128)(2,1)} %bitcast.20), calls=%async_computation.6 | async-start | bytes 1048576 | tf_op jit(solution)/shard_map/all_to_all | solution.py:268
  87.5 5.8 %forward.3 = (bf16[256,2048]{1,0:T(8,128)(2,1)S(1)}, bf16[256,2048]{1,0:T(8,128)(2,1)}, f32[512,256]{1,0:T(8,128)S(1)}, f32[512,256]{1,0:T(8,128)S(1)}) custom-call(bf16[128,2048]{1,0:T(8,128)(2,1)S(1)} %bitcast.35, bf16[128,2048]{1,0:T(8,128)(2,1)S(1)} %collective-permute-done.2.refs_1_.refs_7_, bf16[128,2048]{1,0:T(8,128)(2,1)} %collective-permute-done.3.refs_2_.refs_8_, ...), custom_call_target="tpu_custom_call" | custom-call | flops 1610612736 | bytes 8388608 | tf_op jit(solution)/shard_map/forward/pallas_call | solution.py:147
  95.6 4.8 %collective-permute-done.12.refs_1_.refs_15_ = bf16[128,2048]{1,0:T(8,128)(2,1)} collective-permute-done((bf16[128,2048]{1,0:T(8,128)(2,1)}, bf16[128,2048]{1,0:T(8,128)(2,1)}, u32[]{:S(2)}, u32[]{:S(2)}) %collective-permute-start.12) | collective-permute-done | bytes 524320 | tf_op jit(solution)/shard_map/ppermute | solution.py:264
  101.7 4.8 %forward.4 = (bf16[256,2048]{1,0:T(8,128)(2,1)S(1)}, bf16[256,2048]{1,0:T(8,128)(2,1)}, f32[512,256]{1,0:T(8,128)S(1)}, f32[512,256]{1,0:T(8,128)S(1)}) custom-call(bf16[128,2048]{1,0:T(8,128)(2,1)S(1)} %bitcast.39, bf16[128,2048]{1,0:T(8,128)(2,1)S(1)} %copy-done.18, bf16[128,2048]{1,0:T(8,128)(2,1)S(1)} %collective-permute-done.8.refs_2_.refs_12_, ...), custom_call_target="tpu_custom_call" | custom-call | flops 1610612736 | bytes 8388608 | tf_op jit(solution)/shard_map/forward/pallas_call | solution.py:147
  108.7 5.8 %all-to-all-start.7 = ((bf16[8,16,2048]{2,1,0:T(8,128)(2,1)}), bf16[8,16,2048]{2,1,0:T(8,128)(2,1)}, u32[]{:S(2)}, u32[]{:S(2)}) async-start(bf16[8,16,2048]{2,1,0:T(8,128)(2,1)} %bitcast.42), calls=%async_computation.7 | async-start | bytes 1048576 | tf_op jit(solution)/shard_map/all_to_all | solution.py:268
  114.6 6.1 %forward.5 = (bf16[256,2048]{1,0:T(8,128)(2,1)S(1)}, bf16[256,2048]{1,0:T(8,128)(2,1)}, f32[512,256]{1,0:T(8,128)S(1)}, f32[512,256]{1,0:T(8,128)S(1)}) custom-call(bf16[128,2048]{1,0:T(8,128)(2,1)} %bitcast.16.refs_0_.refs_14_, bf16[128,2048]{1,0:T(8,128)(2,1)} %collective-permute-done.12.refs_1_.refs_15_, ...), custom_call_target="tpu_custom_call" | custom-call | flops 1610612736 | bytes 8388608 | tf_op jit(solution)/shard_map/forward/pallas_call | solution.py:147
  126.4 3.8 %all-to-all-done.7 = bf16[8,16,2048]{2,1,0:T(8,128)(2,1)} async-done(((bf16[8,16,2048]{2,1,0:T(8,128)(2,1)}), bf16[8,16,2048]{2,1,0:T(8,128)(2,1)}, u32[]{:S(2)}, u32[]{:S(2)}) %all-to-all-start.7) | async-done | bytes 524320 | tf_op jit(solution)/shard_map/all_to_all | solution.py:268
  130.2 4.3 %all-to-all-start.8 = ((bf16[8,16,2048]{2,1,0:T(8,128)(2,1)}), bf16[8,16,2048]{2,1,0:T(8,128)(2,1)}, u32[]{:S(2)}, u32[]{:S(2)}) async-start(bf16[8,16,2048]{2,1,0:T(8,128)(2,1)} %bitcast.41), calls=%async_computation.8 | async-start | bytes 1048576 | tf_op jit(solution)/shard_map/all_to_all | solution.py:268
  140.9 2.4 %add_convert_fusion.4 = bf16[128,2048]{1,0:T(8,128)(2,1)} fusion(bf16[128,2048]{1,0:T(8,128)(2,1)} %collective-permute-done.6, bf16[256,2048]{1,0:T(8,128)(2,1)} %collective-permute-done.5, bf16[256,2048]{1,0:T(8,128)(2,1)} %copy-done.1), kind=kLoop, calls=%fused_computation.4 | loop fusion | flops 1572864 | bytes 2097152 | tf_op jit(solution)/shard_map/convert_element_type | solution.py:323
  143.3 5.5 %all-to-all-done.8 = bf16[8,16,2048]{2,1,0:T(8,128)(2,1)} async-done(((bf16[8,16,2048]{2,1,0:T(8,128)(2,1)}), bf16[8,16,2048]{2,1,0:T(8,128)(2,1)}, u32[]{:S(2)}, u32[]{:S(2)}) %all-to-all-start.8) | async-done | bytes 524320 | tf_op jit(solution)/shard_map/all_to_all | solution.py:268
  148.8 3.5 %all-to-all-start.1 = ((bf16[8,16,2048]{2,1,0:T(8,128)(2,1)}), bf16[8,16,2048]{2,1,0:T(8,128)(2,1)S(1)}, u32[]{:S(2)}, u32[]{:S(2)}) async-start(bf16[8,16,2048]{2,1,0:T(8,128)(2,1)} %bitcast.9), calls=%async_computation.1 | async-start | bytes 1048576 | tf_op jit(solution)/shard_map/all_to_all | solution.py:268
  155.8 17.2 %collective-permute-done.11 = bf16[128,2048]{1,0:T(8,128)(2,1)S(1)} collective-permute-done((bf16[128,2048]{1,0:T(8,128)(2,1)}, bf16[128,2048]{1,0:T(8,128)(2,1)S(1)}, u32[]{:S(2)}, u32[]{:S(2)}) %collective-permute-start.11) | collective-permute-done | bytes 524320 | tf_op jit(solution)/shard_map/ppermute | solution.py:264
  176.8 6.0 %all-to-all-start.3 = ((bf16[8,16,2048]{2,1,0:T(8,128)(2,1)}), bf16[8,16,2048]{2,1,0:T(8,128)(2,1)S(1)}, u32[]{:S(2)}, u32[]{:S(2)}) async-start(bf16[8,16,2048]{2,1,0:T(8,128)(2,1)} %bitcast.51), calls=%async_computation.3 | async-start | bytes 1048576 | tf_op jit(solution)/shard_map/all_to_all | solution.py:268
  184.4 10.8 %collective-permute-done.16 = bf16[128,2048]{1,0:T(8,128)(2,1)} collective-permute-done((bf16[128,2048]{1,0:T(8,128)(2,1)}, bf16[128,2048]{1,0:T(8,128)(2,1)}, u32[]{:S(2)}, u32[]{:S(2)}) %collective-permute-start.16) | collective-permute-done | bytes 524320 | tf_op jit(solution)/shard_map/ppermute | solution.py:264
  197.5 6.0 %all-to-all-start.5 = ((bf16[8,16,2048]{2,1,0:T(8,128)(2,1)}), bf16[8,16,2048]{2,1,0:T(8,128)(2,1)S(1)}, u32[]{:S(2)}, u32[]{:S(2)}) async-start(bf16[8,16,2048]{2,1,0:T(8,128)(2,1)} %bitcast.50), calls=%async_computation.5 | async-start | bytes 1048576 | tf_op jit(solution)/shard_map/all_to_all | solution.py:268
  212.9 14.0 %backward.1 = (bf16[256,2048]{1,0:T(8,128)(2,1)}, bf16[256,2048]{1,0:T(8,128)(2,1)}, bf16[256,2048]{1,0:T(8,128)(2,1)}) custom-call(f32[512,256]{1,0:T(8,128)S(1)} %copy-done.22, f32[512,256]{1,0:T(8,128)S(1)} %copy-done.26, f32[512,256]{1,0:T(8,128)S(1)} %copy-done.30, f32[512,256]{1,0:T(8,128)S(1)} %copy-done.24, f32[512,256]{1,0:T(8,128)S(1)} %copy-done.28, ...), custom_call_target="tpu_custom_call" | custom-call | flops 6442450944 | bytes 18874368 | tf_op jit(solution)/shard_map/backward/pallas_call | solution.py:203
  (126 shorter events, 57.9 us)
Async XLA Ops:
  51.5 18.9 %collective-permute-start.2 = (bf16[128,2048]{1,0:T(8,128)(2,1)S(1)}, bf16[128,2048]{1,0:T(8,128)(2,1)S(1)}, u32[]{:S(2)}, u32[]{:S(2)}) collective-permute-start(bf16[128,2048]{1,0:T(8,128)(2,1)S(1)} %bitcast.33), channel_id=1, source_target_pairs={{0,2},{2,0},{1,3},{3,1},{4,6},{6,4},{5,7},{7,5},{8,10},{10,8},{9,1... | collective-permute-start | bytes 1572872 | tf_op jit(solution)/shard_map/ppermute | solution.py:264
  68.9 18.4 %collective-permute-start.7 = (bf16[128,2048]{1,0:T(8,128)(2,1)S(1)}, bf16[128,2048]{1,0:T(8,128)(2,1)S(1)}, u32[]{:S(2)}, u32[]{:S(2)}) collective-permute-start(bf16[128,2048]{1,0:T(8,128)(2,1)S(1)} %bitcast.37), channel_id=1, source_target_pairs={{0,2},{2,0},{1,3},{3,1},{4,6},{6,4},{5,7},{7,5},{8,10},{10,8},{9,1... | collective-permute-start | bytes 1572872 | tf_op jit(solution)/shard_map/ppermute | solution.py:264
  70.4 17.1 %collective-permute-start.3 = (bf16[128,2048]{1,0:T(8,128)(2,1)S(1)}, bf16[128,2048]{1,0:T(8,128)(2,1)}, u32[]{:S(2)}, u32[]{:S(2)}) collective-permute-start(bf16[128,2048]{1,0:T(8,128)(2,1)S(1)} %bitcast.34), channel_id=1, source_target_pairs={{0,1},{1,0},{2,3},{3,2},{4,5},{5,4},{6,7},{7,6},{8,9},{9,8},{10,11... | collective-permute-start | bytes 1572872 | tf_op jit(solution)/shard_map/ppermute | solution.py:264
  70.4 17.1 %collective-permute-start.4 = (bf16[128,2048]{1,0:T(8,128)(2,1)S(1)}, bf16[128,2048]{1,0:T(8,128)(2,1)}, u32[]{:S(2)}, u32[]{:S(2)}) collective-permute-start(bf16[128,2048]{1,0:T(8,128)(2,1)S(1)} %collective-permute-done.2.refs_1_.refs_7_), channel_id=1, source_target_pairs={{0,1},{1,0},{2,3},{3,2},{4,5},{5,4},{6,7},{7,6},{8,9},{9,8},{10,11... | collective-permute-start | bytes 1572872 | tf_op jit(solution)/shard_map/ppermute | solution.py:264
  81.5 27.2 %all-to-all-start.6 = ((bf16[8,16,2048]{2,1,0:T(8,128)(2,1)}), bf16[8,16,2048]{2,1,0:T(8,128)(2,1)}, u32[]{:S(2)}, u32[]{:S(2)}) async-start(bf16[8,16,2048]{2,1,0:T(8,128)(2,1)} %bitcast.20), calls=%async_computation.6 | async-start | bytes 1048576 | tf_op jit(solution)/shard_map/all_to_all | solution.py:268
  95.1 27.2 %collective-permute-start.5 = (bf16[256,2048]{1,0:T(8,128)(2,1)}, bf16[256,2048]{1,0:T(8,128)(2,1)}, u32[]{:S(2)}, u32[]{:S(2)}) collective-permute-start(bf16[256,2048]{1,0:T(8,128)(2,1)} %get-tuple-element.31), channel_id=1, source_target_pairs={{0,1},{1,0},{2,3},{3,2},{4,5},{5,4},{6,7},{7,6},{8,9},{9,8},{10,11... | collective-permute-start | bytes 3145736 | tf_op jit(solution)/shard_map/ppermute | solution.py:264
  95.4 19.2 %collective-permute-start.13 = (bf16[128,2048]{1,0:T(8,128)(2,1)}, bf16[128,2048]{1,0:T(8,128)(2,1)}, u32[]{:S(2)}, u32[]{:S(2)}) collective-permute-start(bf16[128,2048]{1,0:T(8,128)(2,1)} %bitcast.16.refs_0_.refs_14_), channel_id=1, source_target_pairs={{0,1},{1,0},{2,3},{3,2},{4,5},{5,4},{6,7},{7,6},{8,9},{9,8},{10,11... | collective-permute-start | bytes 1572872 | tf_op jit(solution)/shard_map/ppermute | solution.py:264
  108.1 26.4 %collective-permute-start.10 = (bf16[256,2048]{1,0:T(8,128)(2,1)}, bf16[256,2048]{1,0:T(8,128)(2,1)}, u32[]{:S(2)}, u32[]{:S(2)}) collective-permute-start(bf16[256,2048]{1,0:T(8,128)(2,1)} %get-tuple-element.34), channel_id=1, source_target_pairs={{0,1},{1,0},{2,3},{3,2},{4,5},{5,4},{6,7},{7,6},{8,9},{9,8},{10,11... | collective-permute-start | bytes 3145736 | tf_op jit(solution)/shard_map/ppermute | solution.py:264
  108.7 21.5 %all-to-all-start.7 = ((bf16[8,16,2048]{2,1,0:T(8,128)(2,1)}), bf16[8,16,2048]{2,1,0:T(8,128)(2,1)}, u32[]{:S(2)}, u32[]{:S(2)}) async-start(bf16[8,16,2048]{2,1,0:T(8,128)(2,1)} %bitcast.42), calls=%async_computation.7 | async-start | bytes 1048576 | tf_op jit(solution)/shard_map/all_to_all | solution.py:268
  122.3 30.1 %collective-permute-start.15 = (bf16[256,2048]{1,0:T(8,128)(2,1)}, bf16[256,2048]{1,0:T(8,128)(2,1)}, u32[]{:S(2)}, u32[]{:S(2)}) collective-permute-start(bf16[256,2048]{1,0:T(8,128)(2,1)} %get-tuple-element.37), channel_id=1, source_target_pairs={{0,1},{1,0},{2,3},{3,2},{4,5},{5,4},{6,7},{7,6},{8,9},{9,8},{10,11... | collective-permute-start | bytes 3145736 | tf_op jit(solution)/shard_map/ppermute | solution.py:264
  125.9 56.9 %collective-permute-start.17 = (bf16[128,2048]{1,0:T(8,128)(2,1)}, bf16[128,2048]{1,0:T(8,128)(2,1)}, u32[]{:S(2)}, u32[]{:S(2)}) collective-permute-start(bf16[128,2048]{1,0:T(8,128)(2,1)} %bitcast.21.refs_18_), channel_id=1, source_target_pairs={{0,2},{2,0},{1,3},{3,1},{4,6},{6,4},{5,7},{7,5},{8,10},{10,8},{9,1... | collective-permute-start | bytes 1572872 | tf_op jit(solution)/shard_map/ppermute | solution.py:264
  126.4 56.4 %collective-permute-start.18 = (bf16[128,2048]{1,0:T(8,128)(2,1)}, bf16[128,2048]{1,0:T(8,128)(2,1)}, u32[]{:S(2)}, u32[]{:S(2)}) collective-permute-start(bf16[128,2048]{1,0:T(8,128)(2,1)} %bitcast.21.refs_18_), channel_id=1, source_target_pairs={{0,1},{1,0},{2,3},{3,2},{4,5},{5,4},{6,7},{7,6},{8,9},{9,8},{10,11... | collective-permute-start | bytes 1572872 | tf_op jit(solution)/shard_map/ppermute | solution.py:264
  130.2 18.6 %all-to-all-start.8 = ((bf16[8,16,2048]{2,1,0:T(8,128)(2,1)}), bf16[8,16,2048]{2,1,0:T(8,128)(2,1)}, u32[]{:S(2)}, u32[]{:S(2)}) async-start(bf16[8,16,2048]{2,1,0:T(8,128)(2,1)} %bitcast.41), calls=%async_computation.8 | async-start | bytes 1048576 | tf_op jit(solution)/shard_map/all_to_all | solution.py:268
  134.6 48.7 %collective-permute-start.20 = (bf16[128,2048]{1,0:T(8,128)(2,1)}, bf16[128,2048]{1,0:T(8,128)(2,1)}, u32[]{:S(2)}, u32[]{:S(2)}) collective-permute-start(bf16[128,2048]{1,0:T(8,128)(2,1)} %bitcast.23.refs_22_), channel_id=1, source_target_pairs={{0,2},{2,0},{1,3},{3,1},{4,6},{6,4},{5,7},{7,5},{8,10},{10,8},{9,1... | collective-permute-start | bytes 1572872 | tf_op jit(solution)/shard_map/ppermute | solution.py:264
  139.4 33.6 %collective-permute-start.11 = (bf16[128,2048]{1,0:T(8,128)(2,1)}, bf16[128,2048]{1,0:T(8,128)(2,1)S(1)}, u32[]{:S(2)}, u32[]{:S(2)}) collective-permute-start(bf16[128,2048]{1,0:T(8,128)(2,1)} %add_convert_fusion.3), channel_id=1, source_target_pairs={{0,2},{2,0},{1,3},{3,1},{4,6},{6,4},{5,7},{7,5},{8,10},{10,8},{9,1... | collective-permute-start | bytes 1572872 | tf_op jit(solution)/shard_map/ppermute | solution.py:264
  148.8 27.9 %all-to-all-start.1 = ((bf16[8,16,2048]{2,1,0:T(8,128)(2,1)}), bf16[8,16,2048]{2,1,0:T(8,128)(2,1)S(1)}, u32[]{:S(2)}, u32[]{:S(2)}) async-start(bf16[8,16,2048]{2,1,0:T(8,128)(2,1)} %bitcast.9), calls=%async_computation.1 | async-start | bytes 1048576 | tf_op jit(solution)/shard_map/all_to_all | solution.py:268
  152.3 32.0 %collective-permute-start.23 = (bf16[128,2048]{1,0:T(8,128)(2,1)}, bf16[128,2048]{1,0:T(8,128)(2,1)}, u32[]{:S(2)}, u32[]{:S(2)}) collective-permute-start(bf16[128,2048]{1,0:T(8,128)(2,1)} %bitcast.25.refs_26_), channel_id=1, source_target_pairs={{0,2},{2,0},{1,3},{3,1},{4,6},{6,4},{5,7},{7,5},{8,10},{10,8},{9,1... | collective-permute-start | bytes 1572872 | tf_op jit(solution)/shard_map/ppermute | solution.py:264
  173.0 22.2 %collective-permute-start.16 = (bf16[128,2048]{1,0:T(8,128)(2,1)}, bf16[128,2048]{1,0:T(8,128)(2,1)}, u32[]{:S(2)}, u32[]{:S(2)}) collective-permute-start(bf16[128,2048]{1,0:T(8,128)(2,1)} %add_convert_fusion.1), channel_id=1, source_target_pairs={{0,2},{2,0},{1,3},{3,1},{4,6},{6,4},{5,7},{7,5},{8,10},{10,8},{9,1... | collective-permute-start | bytes 1572872 | tf_op jit(solution)/shard_map/ppermute | solution.py:264
  176.8 20.7 %all-to-all-start.3 = ((bf16[8,16,2048]{2,1,0:T(8,128)(2,1)}), bf16[8,16,2048]{2,1,0:T(8,128)(2,1)S(1)}, u32[]{:S(2)}, u32[]{:S(2)}) async-start(bf16[8,16,2048]{2,1,0:T(8,128)(2,1)} %bitcast.51), calls=%async_computation.3 | async-start | bytes 1048576 | tf_op jit(solution)/shard_map/all_to_all | solution.py:268
  182.7 20.7 %collective-permute-start.21 = (bf16[128,2048]{1,0:T(8,128)(2,1)}, bf16[128,2048]{1,0:T(8,128)(2,1)}, u32[]{:S(2)}, u32[]{:S(2)}) collective-permute-start(bf16[128,2048]{1,0:T(8,128)(2,1)} %bitcast.23.refs_22_), channel_id=1, source_target_pairs={{0,1},{1,0},{2,3},{3,2},{4,5},{5,4},{6,7},{7,6},{8,9},{9,8},{10,11... | collective-permute-start | bytes 1572872 | tf_op jit(solution)/shard_map/ppermute | solution.py:264
  182.8 20.6 %collective-permute-start.24 = (bf16[128,2048]{1,0:T(8,128)(2,1)}, bf16[128,2048]{1,0:T(8,128)(2,1)}, u32[]{:S(2)}, u32[]{:S(2)}) collective-permute-start(bf16[128,2048]{1,0:T(8,128)(2,1)} %bitcast.25.refs_26_), channel_id=1, source_target_pairs={{0,1},{1,0},{2,3},{3,2},{4,5},{5,4},{6,7},{7,6},{8,9},{9,8},{10,11... | collective-permute-start | bytes 1572872 | tf_op jit(solution)/shard_map/ppermute | solution.py:264
  183.3 20.1 %collective-permute-start.19 = (bf16[128,2048]{1,0:T(8,128)(2,1)}, bf16[128,2048]{1,0:T(8,128)(2,1)}, u32[]{:S(2)}, u32[]{:S(2)}) collective-permute-start(bf16[128,2048]{1,0:T(8,128)(2,1)} %collective-permute-done.17.refs_19_), channel_id=1, source_target_pairs={{0,1},{1,0},{2,3},{3,2},{4,5},{5,4},{6,7},{7,6},{8,9},{9,8},{10,11... | collective-permute-start | bytes 1572872 | tf_op jit(solution)/shard_map/ppermute | solution.py:264
  184.4 19.1 %collective-permute-start.22 = (bf16[128,2048]{1,0:T(8,128)(2,1)}, bf16[128,2048]{1,0:T(8,128)(2,1)}, u32[]{:S(2)}, u32[]{:S(2)}) collective-permute-start(bf16[128,2048]{1,0:T(8,128)(2,1)} %collective-permute-done.20.refs_23_), channel_id=1, source_target_pairs={{0,1},{1,0},{2,3},{3,2},{4,5},{5,4},{6,7},{7,6},{8,9},{9,8},{10,11... | collective-permute-start | bytes 1572872 | tf_op jit(solution)/shard_map/ppermute | solution.py:264
  197.5 29.5 %all-to-all-start.5 = ((bf16[8,16,2048]{2,1,0:T(8,128)(2,1)}), bf16[8,16,2048]{2,1,0:T(8,128)(2,1)S(1)}, u32[]{:S(2)}, u32[]{:S(2)}) async-start(bf16[8,16,2048]{2,1,0:T(8,128)(2,1)} %bitcast.50), calls=%async_computation.5 | async-start | bytes 1048576 | tf_op jit(solution)/shard_map/all_to_all | solution.py:268
  (43 other events, 345.0 us)

commit v3 on v0

v3 whole, which is shorter than its diff:
```python
import functools

import jax
import jax.numpy as jnp
from jax import lax
from jax.experimental import pallas as pl
from jax.experimental.pallas import tpu as pltpu
from jax.sharding import PartitionSpec as P

HEADS = 8
HD = 128
SHARDS = 4
UNIT = 48
PER_CHUNK = 2
VMEM_LIMIT = 40 * 1024 * 1024
EXP = ("group", "side", "core")

NT = (((1,), (1,)), ((), ()))
TN = (((0,), (0,)), ((), ()))

VMEM = pl.BlockSpec(memory_space=pltpu.VMEM)
SMEM = pl.BlockSpec(memory_space=pltpu.SMEM)
ANY = pl.BlockSpec(memory_space=pl.ANY)


def dot(a, b, dims=(((1,), (0,)), ((), ()))):
    return lax.dot_general(a, b, dims, preferred_element_type=jnp.float32)


def shape_of(rows, cols, dtype=jnp.bfloat16):
    return jax.ShapeDtypeStruct((rows, cols), dtype)


def call(body, name, small, large, outs, buffers, flops=0, after=()):
    flat = [value for group in large for value in group]
    count = len(flat)
    n_small, n_outs, n_after = len(small), len(outs), len(after)
    group_shapes = [
        pltpu.VMEM((sum(v.shape[0] for v in group), group[0].shape[1]), group[0].dtype)
        for group in large
    ]

    def kernel(*refs):
        small_refs = refs[:n_small]
        sources = refs[n_small : n_small + count]
        out_refs = refs[n_small + count + n_after : n_small + count + n_after + n_outs]
        rest = refs[n_small + count + n_after + n_outs :]
        targets = rest[: len(large)]
        own = rest[len(large) : -1]
        sem = rest[-1]
        waits, at = [], 0
        for group, target in zip(large, targets):
            copies, row = [], 0
            for value in group:
                size = value.shape[0]
                copies.append(
                    pltpu.make_async_copy(sources[at], target.at[pl.ds(row, size)], sem.at[at])
                )
                row += size
                at += 1
            waits.append(copies)
        for copies in waits:
            for copy in copies:
                copy.start()

        def ready(n):
            for copy in waits[n]:
                copy.wait()
            return targets[n]

        body(small_refs, ready, out_refs, own)

    moved = sum(v.size * v.dtype.itemsize for v in flat)
    return pl.pallas_call(
        kernel,
        out_shape=tuple(outs),
        in_specs=[spec for spec, _ in small] + [ANY] * (count + n_after),
        out_specs=(VMEM,) * n_outs,
        scratch_shapes=group_shapes + list(buffers) + [pltpu.SemaphoreType.DMA((count,))],
        compiler_params=pltpu.CompilerParams(vmem_limit_bytes=VMEM_LIMIT),
        cost_estimate=pl.CostEstimate(flops=flops, bytes_accessed=moved, transcendentals=0),
        name=name,
    )(*[value for _, value in small], *flat, *after)


def column(row):
    size = row.shape[1]
    across = lax.broadcasted_iota(jnp.int32, (size, size), 0)
    along = lax.broadcasted_iota(jnp.int32, (size, size), 1)
    return jnp.sum(jnp.where(across == along, row, jnp.zeros_like(row)), axis=1, keepdims=True)


def choosers(pos, slots):
    line = lax.broadcasted_iota(jnp.int32, (pos[0].shape[0], slots), 1)
    return [(place == line).astype(jnp.bfloat16) for place in pos]


def store_units(placed, unit_refs):
    placed = placed.astype(jnp.bfloat16)
    rows = unit_refs[0].shape[0]
    for n, ref in enumerate(unit_refs):
        ref[...] = placed[n * rows : (n + 1) * rows]


def slots_body(n_ctx, groups, capacity, small, ready, outs, own):
    me_ref, ids_ref, gates_ref = small
    pos_ref, *unit_refs = outs
    ids = [column(ids_ref[k : k + 1]) for k in range(2)]
    gates = [column(gates_ref[k : k + 1]) for k in range(2)]
    tokens = ids[0].shape[0]
    lanes = lax.broadcasted_iota(jnp.int32, (tokens, 128), 1)
    hot = [(ids[k] == lanes).astype(jnp.float32) for k in range(2)]
    later = lax.broadcasted_iota(jnp.int32, (tokens, tokens), 0)
    earlier = lax.broadcasted_iota(jnp.int32, (tokens, tokens), 1)
    lower = (later > earlier).astype(jnp.bfloat16)
    before = dot(lower, (hot[0] + hot[1]).astype(jnp.bfloat16))
    shift = groups.bit_length() - 1
    pos = []
    for k in range(2):
        slot = jnp.sum(hot[k] * before, axis=1, keepdims=True).astype(jnp.int32)
        ctx = ((ids[k] >> shift) - me_ref[0]) & (n_ctx - 1)
        group = ((ids[k] & (groups - 1)) - me_ref[1]) & (groups - 1)
        pos.append((group * n_ctx + ctx) * capacity + slot)
    pair = lax.broadcasted_iota(jnp.int32, (tokens, 2), 1)
    pos_ref[...] = jnp.where(pair == 0, pos[0], pos[1])
    pick = choosers(pos, len(unit_refs) * unit_refs[0].shape[0])
    grad = ready(0)[...].astype(jnp.float32)
    placed = 0.0
    for k in range(2):
        placed = placed + dot(pick[k], (gates[k] * grad).astype(jnp.bfloat16), TN)
    store_units(placed, unit_refs)


def attend_body(pieces, small, ready, outs, own):
    scale_ref, shift_ref, pos_ref = small
    mixed_ref, *unit_refs = outs
    (attended_ref,) = own
    query_ref, key_ref, value_ref = ready(0), ready(1), ready(2)
    for head in range(HEADS):
        cols = slice(head * HD, (head + 1) * HD)
        scores = dot(query_ref[:, cols], key_ref[:, cols], NT) * (HD ** (-0.5))
        weights = jnp.exp(scores - jnp.max(scores, axis=1, keepdims=True))
        total = jnp.sum(weights, axis=1, keepdims=True)
        accum = dot(weights.astype(jnp.bfloat16), value_ref[:, cols])
        attended_ref[:, cols] = (accum / total).astype(jnp.bfloat16)
    token_ref, proj_ref = ready(3), ready(4)
    mixed = token_ref[...].astype(jnp.float32) + dot(attended_ref[...], proj_ref[...])
    mixed_ref[...] = mixed
    mean_square = jnp.mean(mixed * mixed, axis=1, keepdims=True)
    normed = mixed * lax.rsqrt(mean_square + 1e-06) * (1.0 + scale_ref[...]) + shift_ref[...]
    slots = len(unit_refs) * unit_refs[0].shape[0]
    pick = choosers([pos_ref[:, 0:1], pos_ref[:, 1:2]], slots)
    store_units(dot(pick[0] + pick[1], normed.astype(jnp.bfloat16), TN), unit_refs)


def forward_body(small, ready, outs, own):
    keep_ref, send_ref, gate_pre_ref, up_pre_ref = outs
    rows = ready(0)[...]
    gate_pre = dot(rows, ready(1)[...], NT)
    gate_pre_ref[...] = gate_pre
    up_pre = dot(rows, ready(2)[...], NT)
    up_pre_ref[...] = up_pre
    hidden = (gate_pre * jax.nn.sigmoid(gate_pre) * up_pre).astype(jnp.bfloat16)
    half = rows.shape[0] // 2
    partial = dot(hidden, ready(3)[...]).astype(jnp.bfloat16)
    keep_ref[...] = partial[:half]
    send_ref[...] = partial[half:]


def add_body(small, ready, outs, own):
    total = ready(0)[...].astype(jnp.float32) + ready(1)[...].astype(jnp.float32)
    store_units(total, outs)


def backward_body(small, ready, outs, own):
    side_refs = outs[:3]
    cot_ref, down_ref = ready(0), ready(1)
    hidden_grad = dot(cot_ref[...], down_ref[...], NT)
    gate_pre = ready(2)[...]
    up_pre = ready(3)[...]
    sigmoid = jax.nn.sigmoid(gate_pre)
    active = gate_pre * sigmoid
    side_refs[0][...] = (
        hidden_grad * up_pre * sigmoid * (1.0 + gate_pre * (1.0 - sigmoid))
    ).astype(jnp.bfloat16)
    side_refs[1][...] = (hidden_grad * active).astype(jnp.bfloat16)
    side_refs[2][...] = (active * up_pre).astype(jnp.bfloat16)
    row_ref = ready(4)
    half = side_refs[0].shape[1] // 2
    for side_ref, with_ref, out_ref in zip(side_refs, (row_ref, row_ref, cot_ref), outs[3:]):
        out_ref[...] = dot(side_ref[:, half:], with_ref[...], TN).astype(jnp.bfloat16)


def finish_body(small, ready, outs, own):
    row_ref, cot_ref = ready(0), ready(1)
    for n, (with_ref, out_ref) in enumerate(zip((row_ref, row_ref, cot_ref), outs)):
        side_ref = ready(2 + n)
        half = side_ref.shape[1] // 2
        grad = dot(side_ref[:, :half], with_ref[...], TN)
        out_ref[...] = (grad + ready(5 + n)[...].astype(jnp.float32)).astype(jnp.bfloat16)


def combine_body(small, ready, outs, own):
    gates_ref, pos_ref = small
    rows_ref, mixed_ref = ready(0), ready(1)
    rows = rows_ref[...]
    pick = choosers([pos_ref[:, 0:1], pos_ref[:, 1:2]], rows.shape[0])
    total = mixed_ref[...]
    for k in range(2):
        total = total + column(gates_ref[k : k + 1]) * dot(pick[k], rows)
    outs[0][...] = total.astype(jnp.bfloat16)


def per_device(
    tokens,
    queries,
    keys,
    values,
    out_proj,
    mod_scale,
    mod_shift,
    expert_ids,
    gates,
    w_gate,
    w_up,
    w_down,
    out_grad,
):
    n_ctx = lax.axis_size("ctx")
    groups = lax.axis_size("group")
    experts = n_ctx * groups
    local = tokens.shape[1]
    width = tokens.shape[2]
    hidden = w_gate.shape[0]
    capacity = 3 * local // experts
    slots = experts * capacity
    bundle = max(1, UNIT // capacity)
    units = experts // bundle
    unit_rows = bundle * capacity
    assert n_ctx & (n_ctx - 1) == 0 and groups & (groups - 1) == 0

    def swapped(value, axis):
        return lax.ppermute(value, axis, [(n, n ^ 1) for n in range(lax.axis_size(axis))])

    def shifted(value, offset, sign):
        group, ctx = offset // n_ctx * sign, offset % n_ctx * sign
        moves = []
        for c in range(n_ctx):
            for g in range(groups):
                target = (c + ctx) % n_ctx * groups + (g + group) % groups
                moves.append((c * groups + g, target))
        return lax.ppermute(value, ("ctx", "group"), moves)

    def exchanged(unit, n, sign):
        parts = []
        for m in range(bundle):
            offset = n * bundle + m
            part = unit if bundle == 1 else unit[m * capacity : (m + 1) * capacity]
            parts.append(shifted(part, offset, sign) if offset else part)
        return parts[0] if bundle == 1 else jnp.concatenate(parts, axis=0)

    key_pieces = [keys[0]]
    value_pieces = [values[0]]
    for step in range(1, n_ctx):
        key_pieces.append(shifted(keys[0], step, 1))
        value_pieces.append(shifted(values[0], step, 1))

    ids_rows = jnp.transpose(expert_ids[0])
    gate_rows = jnp.transpose(gates[0])
    me = jnp.stack([lax.axis_index("ctx"), lax.axis_index("group")]).astype(jnp.int32)
    unit_shape = [shape_of(unit_rows, width)] * units
    pos, *cot_units = call(
        functools.partial(slots_body, n_ctx, groups, capacity),
        "slots",
        [(SMEM, me), (VMEM, ids_rows), (VMEM, gate_rows)],
        [[out_grad[0]]],
        [shape_of(local, 2, jnp.int32)] + unit_shape,
        [],
        flops=8 * slots * local * width,
    )
    cots = [exchanged(unit, n, 1) for n, unit in enumerate(cot_units)]
    cots_across = [swapped(unit, "side") for unit in cots]

    mixed, *row_units = call(
        functools.partial(attend_body, n_ctx),
        "attend",
        [(VMEM, mod_scale), (VMEM, mod_shift), (VMEM, pos)],
        [[queries[0]], key_pieces, value_pieces, [tokens[0]], [out_proj]],
        [shape_of(local, width, jnp.float32)] + unit_shape,
        [pltpu.VMEM((local, HEADS * HD), jnp.bfloat16)],
        flops=4 * local * HEADS * HD * width,
        after=cots[2:4],
    )
    rows = [exchanged(unit, n, 1) for n, unit in enumerate(row_units)]
    rows_across = [swapped(unit, "side") for unit in rows]

    weights = [[weight, swapped(weight, "core")] for weight in (w_gate, w_up, w_down)]
    ahead = {0: cots_across[0:4], PER_CHUNK: cots_across[6:8]}
    gate_pres, up_pres, row_order, cot_order, returned = [], [], [], [], []
    for first in range(0, units, PER_CHUNK):
        last = first + PER_CHUNK
        blocks = rows[first:last] + rows_across[first:last]
        row_order += blocks
        cot_order += cots[first:last] + cots_across[first:last]
        half = PER_CHUNK * unit_rows
        keep, send, gate_pre, up_pre = call(
            forward_body,
            "forward",
            [],
            [blocks] + weights,
            [shape_of(half, width)] * 2 + [shape_of(2 * half, 2 * hidden, jnp.float32)] * 2,
            [],
            flops=24 * half * hidden * width,
            after=ahead.get(first, ()),
        )
        gate_pres.append(gate_pre)
        up_pres.append(up_pre)
        sums = call(
            add_body,
            "add",
            [],
            [[keep], [swapped(send, "side")]],
            [shape_of(unit_rows, width)] * PER_CHUNK,
            [],
        )
        returned += [exchanged(unit, first + n, -1) for n, unit in enumerate(sums)]

    total_rows = 2 * slots
    side = [shape_of(total_rows, 2 * hidden)] * 3
    grad = [shape_of(hidden, width)] * 3
    *sides, other_gate, other_up, other_down = call(
        backward_body,
        "backward",
        [],
        [cot_order, weights[2], gate_pres, up_pres, row_order],
        side + grad,
        [],
        flops=10 * total_rows * hidden * width,
    )
    others = [swapped(value, "core") for value in (other_gate, other_up, other_down)]
    grad_gate, grad_up, grad_down = call(
        finish_body,
        "finish",
        [],
        [row_order, cot_order] + [[value] for value in sides] + [[value] for value in others],
        grad,
        [],
        flops=6 * total_rows * hidden * width,
    )

    (layer_out,) = call(
        combine_body,
        "combine",
        [(VMEM, gate_rows), (VMEM, pos)],
        [returned, [mixed]],
        [shape_of(local, width)],
        [],
    )
    return (layer_out[None], grad_gate, grad_up, grad_down)


def solution(mesh):
    n_ctx = mesh.shape["ctx"]
    cut = (n_ctx, mesh.shape["exp"] // SHARDS, SHARDS // 2, 2)
    mesh = jax.sharding.Mesh(mesh.devices.reshape(cut), ("ctx",) + EXP)
    rows = P(EXP, "ctx", None)
    weight = P(("ctx",) + EXP, None)
    return jax.shard_map(
        per_device,
        mesh=mesh,
        in_specs=(rows, rows, rows, rows, P(), P(EXP, None), P(EXP, None), rows, rows)
        + (weight, weight, weight, rows),
        out_specs=(rows, weight, weight, weight),
        check_vma=False,
    )
```

time: 651 us -> 237 us (0.36)
  the two profiles are of different devices: /device:TPU:10 before, /device:TPU:0 now
where the time goes in v3:
time: 237 us; the launch traced here: 236 us
  waiting for transfers between devices  102 us (43%)
  starting transfers between devices  63.9 us (27%)
  Pallas kernels  59 us (25%)
  local copies, waits for them, and re-layouts  9.89 us (4%)
    ppermute x23, waiting for transfers between devices, shifted(): return lax.ppermute(value, ('ctx', 'group'), moves)  72.8 us
    pallas_call x13, Pallas kernels, call(): pl.pallas_call(kernel, out_shape=tuple(outs), in_specs=[spec for spec, _...  59 us
    ppermute x23, starting transfers between devices, shifted(): return lax.ppermute(value, ('ctx', 'group'), moves)  39 us
    ppermute x26, waiting for transfers between devices, swapped(): lax.ppermute(value, axis, [(n, n ^ 1) for n in range(lax.axis_size(axis))])  29.6 us
    ppermute x26, starting transfers between devices, swapped(): lax.ppermute(value, axis, [(n, n ^ 1) for n in range(lax.axis_size(axis))])  24.9 us
    unnamed x30, local copies, waits for them, and re-layouts  9.89 us
  transfers between devices with their start and end apart: 49, of which 27 were waited for; matrix products, arithmetic and copies ran while one was open for 0% of the time, Pallas kernels for 18%

profile of v3, /device:TPU:0, one launch (start us, length us, event | category | flops | bytes accessed | tf_op | source)
XLA Modules:
  0.0 236.4 jit_solution(4318932693865750094)
XLA Ops:
  17.0 4.4 %collective-permute-done.3.refs_11_.refs_5_.refs_21_ = bf16[48,2048]{1,0:T(8,128)(2,1)S(1)} collective-permute-done((bf16[48,2048]{1,0:T(8,128)(2,1)S(1)}, bf16[48,2048]{1,0:T(8,128)(2,1)S(1)}, u32[]{:S(2)}, u32[]{:S(2)}) %collective-permute-start.3) | collective-permute-done | bytes 196640 | tf_op jit(solution)/shard_map/ppermute | solution.py:252
  21.4 15.5 %collective-permute-start.43 = (bf16[48,2048]{1,0:T(8,128)(2,1)S(1)}, bf16[48,2048]{1,0:T(8,128)(2,1)S(1)}, u32[]{:S(2)}, u32[]{:S(2)}) collective-permute-start(bf16[48,2048]{1,0:T(8,128)(2,1)S(1)} %get-tuple-element.88), channel_id=1, source_target_pairs={{0,24},{4,28},{8,16},{12,20},{16,8},{20,12},{24,0},{28,4},{1,25},{... | collective-permute-start | bytes 589832 | tf_op jit(solution)/shard_map/ppermute | solution.py:252
  41.0 4.7 %collective-permute-done.43.refs_9_.refs_25_ = bf16[48,2048]{1,0:T(8,128)(2,1)S(1)} collective-permute-done((bf16[48,2048]{1,0:T(8,128)(2,1)S(1)}, bf16[48,2048]{1,0:T(8,128)(2,1)S(1)}, u32[]{:S(2)}, u32[]{:S(2)}) %collective-permute-start.43) | collective-permute-done | bytes 196640 | tf_op jit(solution)/shard_map/ppermute | solution.py:252
  66.5 5.6 %collective-permute-done.4.refs_1_.refs_27_ = bf16[48,2048]{1,0:T(8,128)(2,1)S(1)} collective-permute-done((bf16[48,2048]{1,0:T(8,128)(2,1)S(1)}, bf16[48,2048]{1,0:T(8,128)(2,1)S(1)}, u32[]{:S(2)}, u32[]{:S(2)}) %collective-permute-start.4) | collective-permute-done | bytes 196640 | tf_op jit(solution)/shard_map/ppermute | solution.py:252
  72.1 4.0 %collective-permute-done.17.refs_0_.refs_30_.refs_4_ = bf16[48,2048]{1,0:T(8,128)(2,1)S(1)} collective-permute-done((bf16[48,2048]{1,0:T(8,128)(2,1)S(1)}, bf16[48,2048]{1,0:T(8,128)(2,1)S(1)}, u32[]{:S(2)}, u32[]{:S(2)}) %collective-permute-start.17) | collective-permute-done | bytes 196640 | tf_op jit(solution)/shard_map/ppermute | solution.py:252
  76.2 11.9 %collective-permute-done.28.refs_0_.refs_34_.refs_8_ = bf16[48,2048]{1,0:T(8,128)(2,1)S(1)} collective-permute-done((bf16[48,2048]{1,0:T(8,128)(2,1)S(1)}, bf16[48,2048]{1,0:T(8,128)(2,1)S(1)}, u32[]{:S(2)}, u32[]{:S(2)}) %collective-permute-start.28) | collective-permute-done | bytes 196640 | tf_op jit(solution)/shard_map/ppermute | solution.py:252
  92.7 3.8 %collective-permute-done.35.refs_0_.refs_38_.refs_12_ = bf16[48,2048]{1,0:T(8,128)(2,1)S(1)} collective-permute-done((bf16[48,2048]{1,0:T(8,128)(2,1)S(1)}, bf16[48,2048]{1,0:T(8,128)(2,1)S(1)}, u32[]{:S(2)}, u32[]{:S(2)}) %collective-permute-start.35) | collective-permute-done | bytes 196640 | tf_op jit(solution)/shard_map/ppermute | solution.py:252
  103.7 3.7 %collective-permute-done.38.refs_3_.refs_41_.refs_15_ = bf16[48,2048]{1,0:T(8,128)(2,1)S(1)} collective-permute-done((bf16[48,2048]{1,0:T(8,128)(2,1)S(1)}, bf16[48,2048]{1,0:T(8,128)(2,1)S(1)}, u32[]{:S(2)}, u32[]{:S(2)}) %collective-permute-start.38) | collective-permute-done | bytes 196640 | tf_op jit(solution)/shard_map/ppermute | solution.py:243
  111.5 3.9 %forward.7 = (bf16[96,2048]{1,0:T(8,128)(2,1)S(1)}, bf16[96,2048]{1,0:T(8,128)(2,1)S(1)}, f32[192,512]{1,0:T(8,128)S(1)}, f32[192,512]{1,0:T(8,128)S(1)}) custom-call(bf16[48,2048]{1,0:T(8,128)(2,1)S(1)} %collective-permute-done.35.refs_0_.refs_38_.refs_12_, bf16[48,2048]{1,0:T(8,128)(2,1)S(1)} %collective-permute-done.36.refs_1_.refs_39_.refs_13_, ...), custom_call_target="tpu_custom_call" | custom-call | flops 1207959552 | bytes 7077888 | tf_op jit(solution)/shard_map/forward/pallas_call | solution.py:74
  121.0 3.8 %forward.6 = (bf16[96,2048]{1,0:T(8,128)(2,1)S(1)}, bf16[96,2048]{1,0:T(8,128)(2,1)S(1)}, f32[192,512]{1,0:T(8,128)S(1)}, f32[192,512]{1,0:T(8,128)S(1)}) custom-call(bf16[48,2048]{1,0:T(8,128)(2,1)S(1)} %collective-permute-done.28.refs_0_.refs_34_.refs_8_, bf16[48,2048]{1,0:T(8,128)(2,1)S(1)} %collective-permute-done.29.refs_1_.refs_35_.refs_9_, ...), custom_call_target="tpu_custom_call" | custom-call | flops 1207959552 | bytes 7077888 | tf_op jit(solution)/shard_map/forward/pallas_call | solution.py:74
  129.4 4.7 %forward.4 = (bf16[96,2048]{1,0:T(8,128)(2,1)S(1)}, bf16[96,2048]{1,0:T(8,128)(2,1)}, f32[192,512]{1,0:T(8,128)S(1)}, f32[192,512]{1,0:T(8,128)S(1)}) custom-call(bf16[48,2048]{1,0:T(8,128)(2,1)S(1)} %get-tuple-element.58.refs_0_.refs_26_, bf16[48,2048]{1,0:T(8,128)(2,1)S(1)} %collective-permute-done.4.refs_1_.refs_27_, ...), custom_call_target="tpu_custom_call" | custom-call | flops 1207959552 | bytes 7077888 | tf_op jit(solution)/shard_map/forward/pallas_call | solution.py:74
  142.1 3.8 %forward.5 = (bf16[96,2048]{1,0:T(8,128)(2,1)S(1)}, bf16[96,2048]{1,0:T(8,128)(2,1)S(1)}, f32[192,512]{1,0:T(8,128)S(1)}, f32[192,512]{1,0:T(8,128)S(1)}) custom-call(bf16[48,2048]{1,0:T(8,128)(2,1)S(1)} %collective-permute-done.17.refs_0_.refs_30_.refs_4_, bf16[48,2048]{1,0:T(8,128)(2,1)S(1)} %collective-permute-done.18.refs_1_.refs_31_.refs_5_, ...), custom_call_target="tpu_custom_call" | custom-call | flops 1207959552 | bytes 7077888 | tf_op jit(solution)/shard_map/forward/pallas_call | solution.py:74
  149.0 17.8 %backward.1 = (bf16[768,512]{1,0:T(8,128)(2,1)S(1)}, bf16[768,512]{1,0:T(8,128)(2,1)S(1)}, bf16[768,512]{1,0:T(8,128)(2,1)S(1)}, bf16[256,2048]{1,0:T(8,128)(2,1...) custom-call(bf16[48,2048]{1,0:T(8,128)(2,1)S(1)} %get-tuple-element.60.refs_0_.refs_16_, ...), custom_call_target="tpu_custom_call" | custom-call | flops 4026531840 | bytes 11534336 | tf_op jit(solution)/shard_map/backward/pallas_call | solution.py:74
  169.5 4.8 %collective-permute-done.32.refs_1_ = bf16[96,2048]{1,0:T(8,128)(2,1)S(1)} collective-permute-done((bf16[96,2048]{1,0:T(8,128)(2,1)S(1)}, bf16[96,2048]{1,0:T(8,128)(2,1)S(1)}, u32[]{:S(2)}, u32[]{:S(2)}) %collective-permute-start.32) | collective-permute-done | bytes 393248 | tf_op jit(solution)/shard_map/ppermute | solution.py:243
  175.2 5.9 %collective-permute-done.25.refs_1_ = bf16[96,2048]{1,0:T(8,128)(2,1)S(1)} collective-permute-done((bf16[96,2048]{1,0:T(8,128)(2,1)S(1)}, bf16[96,2048]{1,0:T(8,128)(2,1)S(1)}, u32[]{:S(2)}, u32[]{:S(2)}) %collective-permute-start.25) | collective-permute-done | bytes 393248 | tf_op jit(solution)/shard_map/ppermute | solution.py:243
  182.8 7.9 %collective-permute-done.40.refs_8_ = bf16[48,2048]{1,0:T(8,128)(2,1)S(1)} collective-permute-done((bf16[48,2048]{1,0:T(8,128)(2,1)S(1)}, bf16[48,2048]{1,0:T(8,128)(2,1)S(1)}, u32[]{:S(2)}, u32[]{:S(2)}) %collective-permute-start.40) | collective-permute-done | bytes 196640 | tf_op jit(solution)/shard_map/ppermute | solution.py:252
  190.8 4.2 %collective-permute-done.41.refs_9_ = bf16[48,2048]{1,0:T(8,128)(2,1)S(1)} collective-permute-done((bf16[48,2048]{1,0:T(8,128)(2,1)S(1)}, bf16[48,2048]{1,0:T(8,128)(2,1)S(1)}, u32[]{:S(2)}, u32[]{:S(2)}) %collective-permute-start.41) | collective-permute-done | bytes 196640 | tf_op jit(solution)/shard_map/ppermute | solution.py:252
  195.0 4.9 %collective-permute-start.34 = (bf16[48,2048]{1,0:T(8,128)(2,1)S(1)}, bf16[48,2048]{1,0:T(8,128)(2,1)S(1)}, u32[]{:S(2)}, u32[]{:S(2)}) collective-permute-start(bf16[48,2048]{1,0:T(8,128)(2,1)S(1)} %get-tuple-element.79), channel_id=1, source_target_pairs={{0,24},{4,28},{8,16},{12,20},{16,8},{20,12},{24,0},{28,4},{1,25},{... | collective-permute-start | bytes 589832 | tf_op jit(solution)/shard_map/ppermute | solution.py:252
  200.4 4.6 %collective-permute-done.33.refs_6_ = bf16[48,2048]{1,0:T(8,128)(2,1)S(1)} collective-permute-done((bf16[48,2048]{1,0:T(8,128)(2,1)S(1)}, bf16[48,2048]{1,0:T(8,128)(2,1)S(1)}, u32[]{:S(2)}, u32[]{:S(2)}) %collective-permute-start.33) | collective-permute-done | bytes 196640 | tf_op jit(solution)/shard_map/ppermute | solution.py:252
  205.0 4.5 %collective-permute-done.34.refs_7_ = bf16[48,2048]{1,0:T(8,128)(2,1)S(1)} collective-permute-done((bf16[48,2048]{1,0:T(8,128)(2,1)S(1)}, bf16[48,2048]{1,0:T(8,128)(2,1)S(1)}, u32[]{:S(2)}, u32[]{:S(2)}) %collective-permute-start.34) | collective-permute-done | bytes 196640 | tf_op jit(solution)/shard_map/ppermute | solution.py:252
  209.5 3.9 %collective-permute-done.26.refs_4_ = bf16[48,2048]{1,0:T(8,128)(2,1)S(1)} collective-permute-done((bf16[48,2048]{1,0:T(8,128)(2,1)S(1)}, bf16[48,2048]{1,0:T(8,128)(2,1)S(1)}, u32[]{:S(2)}, u32[]{:S(2)}) %collective-permute-start.26) | collective-permute-done | bytes 196640 | tf_op jit(solution)/shard_map/ppermute | solution.py:252
  213.4 4.4 %collective-permute-done.27.refs_5_ = bf16[48,2048]{1,0:T(8,128)(2,1)S(1)} collective-permute-done((bf16[48,2048]{1,0:T(8,128)(2,1)S(1)}, bf16[48,2048]{1,0:T(8,128)(2,1)S(1)}, u32[]{:S(2)}, u32[]{:S(2)}) %collective-permute-start.27) | collective-permute-done | bytes 196640 | tf_op jit(solution)/shard_map/ppermute | solution.py:252
  217.8 3.7 %combine.1 = bf16[128,2048]{1,0:T(8,128)(2,1)} custom-call(f32[2,128]{1,0:T(2,128)S(1)} %bitcast.21, s32[128,2]{1,0:T(8,128)S(1)} %get-tuple-element.55.refs_2_.refs_1_, bf16[48,2048]{1,0:T(8,128)(2,1)S(1)} %get-tuple-element.64.refs_2_, bf16[48,2048]{1,0:T(8,128)(2,1)S(1)} %collective-permute-done.16.refs_3_, ...), custom_call_target="tpu_custom_call" | custom-call | bytes 2621440 | tf_op jit(solution)/shard_map/combine/pallas_call | solution.py:74
  221.6 14.6 %finish.1 = (bf16[256,2048]{1,0:T(8,128)(2,1)}, bf16[256,2048]{1,0:T(8,128)(2,1)}, bf16[256,2048]{1,0:T(8,128)(2,1)}) custom-call(bf16[48,2048]{1,0:T(8,128)(2,1)S(1)} %get-tuple-element.58.refs_0_.refs_26_, bf16[48,2048]{1,0:T(8,128)(2,1)S(1)} %collective-permute-done.4.refs_1_.refs_27_, bf16[48,2048]{1,0:T(8,128)(2,1)S(1)} %collective-permute-done.5.refs_2_.refs_28_, ...), custom_call_target="tpu_custom_call" | custom-call | flops 2415919104 | bytes 11796480 | tf_op jit(solution)/shard_map/finish/pallas_call | solution.py:74
  (118 shorter events, 84.2 us)
Async XLA Ops:
  10.7 26.2 %collective-permute-start.11 = (bf16[48,2048]{1,0:T(8,128)(2,1)S(1)}, bf16[48,2048]{1,0:T(8,128)(2,1)S(1)}, u32[]{:S(2)}, u32[]{:S(2)}) collective-permute-start(bf16[48,2048]{1,0:T(8,128)(2,1)S(1)} %get-tuple-element.61), channel_id=1, source_target_pairs={{0,16},{4,20},{8,24},{12,28},{16,0},{20,4},{24,8},{28,12},{1,17},{... | collective-permute-start | bytes 589832 | tf_op jit(solution)/shard_map/ppermute | solution.py:252
  11.2 27.2 %collective-permute-start.21 = (bf16[48,2048]{1,0:T(8,128)(2,1)S(1)}, bf16[48,2048]{1,0:T(8,128)(2,1)S(1)}, u32[]{:S(2)}, u32[]{:S(2)}) collective-permute-start(bf16[48,2048]{1,0:T(8,128)(2,1)S(1)} %get-tuple-element.68), channel_id=1, source_target_pairs={{0,12},{4,0},{8,4},{12,8},{16,28},{20,16},{24,20},{28,24},{1,13},{... | collective-permute-start | bytes 589832 | tf_op jit(solution)/shard_map/ppermute | solution.py:252
  13.5 25.5 %collective-permute-start.23 = (bf16[48,2048]{1,0:T(8,128)(2,1)S(1)}, bf16[48,2048]{1,0:T(8,128)(2,1)S(1)}, u32[]{:S(2)}, u32[]{:S(2)}) collective-permute-start(bf16[48,2048]{1,0:T(8,128)(2,1)S(1)} %get-tuple-element.69), channel_id=1, source_target_pairs={{0,28},{4,16},{8,20},{12,24},{16,12},{20,0},{24,4},{28,8},{1,29},{... | collective-permute-start | bytes 589832 | tf_op jit(solution)/shard_map/ppermute | solution.py:252
  16.1 24.4 %collective-permute-start.42 = (bf16[48,2048]{1,0:T(8,128)(2,1)S(1)}, bf16[48,2048]{1,0:T(8,128)(2,1)S(1)}, u32[]{:S(2)}, u32[]{:S(2)}) collective-permute-start(bf16[48,2048]{1,0:T(8,128)(2,1)S(1)} %get-tuple-element.87), channel_id=1, source_target_pairs={{0,8},{4,12},{8,0},{12,4},{16,24},{20,28},{24,16},{28,20},{1,9},{5... | collective-permute-start | bytes 589832 | tf_op jit(solution)/shard_map/ppermute | solution.py:252
  21.4 24.3 %collective-permute-start.43 = (bf16[48,2048]{1,0:T(8,128)(2,1)S(1)}, bf16[48,2048]{1,0:T(8,128)(2,1)S(1)}, u32[]{:S(2)}, u32[]{:S(2)}) collective-permute-start(bf16[48,2048]{1,0:T(8,128)(2,1)S(1)} %get-tuple-element.88), channel_id=1, source_target_pairs={{0,24},{4,28},{8,16},{12,20},{16,8},{20,12},{24,0},{28,4},{1,25},{... | collective-permute-start | bytes 589832 | tf_op jit(solution)/shard_map/ppermute | solution.py:252
  47.2 61.8 %collective-permute-start.7 = (bf16[256,2048]{1,0:T(8,128)(2,1)}, bf16[256,2048]{1,0:T(8,128)(2,1)S(1)}, u32[]{:S(2)}, u32[]{:S(2)}) collective-permute-start(bf16[256,2048]{1,0:T(8,128)(2,1)} %refs_4_.7), channel_id=1, source_target_pairs={{0,1},{1,0},{2,3},{3,2},{4,5},{5,4},{6,7},{7,6},{8,9},{9,8},{10,11... | collective-permute-start | bytes 3145736 | tf_op jit(solution)/shard_map/ppermute | solution.py:243
  47.7 16.0 %collective-permute-start.12 = (bf16[48,2048]{1,0:T(8,128)(2,1)S(1)}, bf16[48,2048]{1,0:T(8,128)(2,1)S(1)}, u32[]{:S(2)}, u32[]{:S(2)}) collective-permute-start(bf16[48,2048]{1,0:T(8,128)(2,1)S(1)} %collective-permute-done.11.refs_1_.refs_17_), channel_id=1, source_target_pairs={{0,2},{2,0},{1,3},{3,1},{4,6},{6,4},{5,7},{7,5},{8,10},{10,8},{9,1... | collective-permute-start | bytes 589832 | tf_op jit(solution)/shard_map/ppermute | solution.py:243
  50.6 16.0 %collective-permute-start.22 = (bf16[48,2048]{1,0:T(8,128)(2,1)S(1)}, bf16[48,2048]{1,0:T(8,128)(2,1)S(1)}, u32[]{:S(2)}, u32[]{:S(2)}) collective-permute-start(bf16[48,2048]{1,0:T(8,128)(2,1)S(1)} %collective-permute-done.21.refs_12_.refs_28_), channel_id=1, source_target_pairs={{0,2},{2,0},{1,3},{3,1},{4,6},{6,4},{5,7},{7,5},{8,10},{10,8},{9,1... | collective-permute-start | bytes 589832 | tf_op jit(solution)/shard_map/ppermute | solution.py:243
  52.0 57.5 %collective-permute-start.8 = (bf16[256,2048]{1,0:T(8,128)(2,1)}, bf16[256,2048]{1,0:T(8,128)(2,1)S(1)}, u32[]{:S(2)}, u32[]{:S(2)}) collective-permute-start(bf16[256,2048]{1,0:T(8,128)(2,1)} %refs_6_.7), channel_id=1, source_target_pairs={{0,1},{1,0},{2,3},{3,2},{4,5},{5,4},{6,7},{7,6},{8,9},{9,8},{10,11... | collective-permute-start | bytes 3145736 | tf_op jit(solution)/shard_map/ppermute | solution.py:243
  53.5 57.5 %collective-permute-start.9 = (bf16[256,2048]{1,0:T(8,128)(2,1)}, bf16[256,2048]{1,0:T(8,128)(2,1)S(1)}, u32[]{:S(2)}, u32[]{:S(2)}) collective-permute-start(bf16[256,2048]{1,0:T(8,128)(2,1)} %refs_16_.1), channel_id=1, source_target_pairs={{0,1},{1,0},{2,3},{3,2},{4,5},{5,4},{6,7},{7,6},{8,9},{9,8},{10,11... | collective-permute-start | bytes 3145736 | tf_op jit(solution)/shard_map/ppermute | solution.py:243
  72.1 16.0 %collective-permute-start.28 = (bf16[48,2048]{1,0:T(8,128)(2,1)S(1)}, bf16[48,2048]{1,0:T(8,128)(2,1)S(1)}, u32[]{:S(2)}, u32[]{:S(2)}) collective-permute-start(bf16[48,2048]{1,0:T(8,128)(2,1)S(1)} %get-tuple-element.74), channel_id=1, source_target_pairs={{0,8},{4,12},{8,0},{12,4},{16,24},{20,28},{24,16},{28,20},{1,9},{5... | collective-permute-start | bytes 589832 | tf_op jit(solution)/shard_map/ppermute | solution.py:252
  76.1 16.0 %collective-permute-start.29 = (bf16[48,2048]{1,0:T(8,128)(2,1)S(1)}, bf16[48,2048]{1,0:T(8,128)(2,1)S(1)}, u32[]{:S(2)}, u32[]{:S(2)}) collective-permute-start(bf16[48,2048]{1,0:T(8,128)(2,1)S(1)} %get-tuple-element.75), channel_id=1, source_target_pairs={{0,24},{4,28},{8,16},{12,20},{16,8},{20,12},{24,0},{28,4},{1,25},{... | collective-permute-start | bytes 589832 | tf_op jit(solution)/shard_map/ppermute | solution.py:252
  111.0 16.9 %collective-permute-start.6 = (bf16[48,2048]{1,0:T(8,128)(2,1)S(1)}, bf16[48,2048]{1,0:T(8,128)(2,1)S(1)}, u32[]{:S(2)}, u32[]{:S(2)}) collective-permute-start(bf16[48,2048]{1,0:T(8,128)(2,1)S(1)} %collective-permute-done.4.refs_1_.refs_27_), channel_id=1, source_target_pairs={{0,2},{2,0},{1,3},{3,1},{4,6},{6,4},{5,7},{7,5},{8,10},{10,8},{9,1... | collective-permute-start | bytes 589832 | tf_op jit(solution)/shard_map/ppermute | solution.py:243
  115.4 18.7 %collective-permute-start.24 = (bf16[48,2048]{1,0:T(8,128)(2,1)S(1)}, bf16[48,2048]{1,0:T(8,128)(2,1)S(1)}, u32[]{:S(2)}, u32[]{:S(2)}) collective-permute-start(bf16[48,2048]{1,0:T(8,128)(2,1)S(1)} %collective-permute-done.23.refs_13_.refs_29_), channel_id=1, source_target_pairs={{0,2},{2,0},{1,3},{3,1},{4,6},{6,4},{5,7},{7,5},{8,10},{10,8},{9,1... | collective-permute-start | bytes 589832 | tf_op jit(solution)/shard_map/ppermute | solution.py:243
  117.0 19.4 %collective-permute-start.19 = (bf16[48,2048]{1,0:T(8,128)(2,1)S(1)}, bf16[48,2048]{1,0:T(8,128)(2,1)S(1)}, u32[]{:S(2)}, u32[]{:S(2)}) collective-permute-start(bf16[48,2048]{1,0:T(8,128)(2,1)S(1)} %collective-permute-done.17.refs_0_.refs_30_.refs_4_), channel_id=1, source_target_pairs={{0,2},{2,0},{1,3},{3,1},{4,6},{6,4},{5,7},{7,5},{8,10},{10,8},{9,1... | collective-permute-start | bytes 589832 | tf_op jit(solution)/shard_map/ppermute | solution.py:243
  119.5 21.1 %collective-permute-start.20 = (bf16[48,2048]{1,0:T(8,128)(2,1)S(1)}, bf16[48,2048]{1,0:T(8,128)(2,1)S(1)}, u32[]{:S(2)}, u32[]{:S(2)}) collective-permute-start(bf16[48,2048]{1,0:T(8,128)(2,1)S(1)} %collective-permute-done.18.refs_1_.refs_31_.refs_5_), channel_id=1, source_target_pairs={{0,2},{2,0},{1,3},{3,1},{4,6},{6,4},{5,7},{7,5},{8,10},{10,8},{9,1... | collective-permute-start | bytes 589832 | tf_op jit(solution)/shard_map/ppermute | solution.py:243
  124.9 21.1 %collective-permute-start.44 = (bf16[48,2048]{1,0:T(8,128)(2,1)S(1)}, bf16[48,2048]{1,0:T(8,128)(2,1)S(1)}, u32[]{:S(2)}, u32[]{:S(2)}) collective-permute-start(bf16[48,2048]{1,0:T(8,128)(2,1)S(1)} %collective-permute-done.42.refs_8_.refs_24_), channel_id=1, source_target_pairs={{0,2},{2,0},{1,3},{3,1},{4,6},{6,4},{5,7},{7,5},{8,10},{10,8},{9,1... | collective-permute-start | bytes 589832 | tf_op jit(solution)/shard_map/ppermute | solution.py:243
  128.0 21.1 %collective-permute-start.45 = (bf16[48,2048]{1,0:T(8,128)(2,1)S(1)}, bf16[48,2048]{1,0:T(8,128)(2,1)S(1)}, u32[]{:S(2)}, u32[]{:S(2)}) collective-permute-start(bf16[48,2048]{1,0:T(8,128)(2,1)S(1)} %collective-permute-done.43.refs_9_.refs_25_), channel_id=1, source_target_pairs={{0,2},{2,0},{1,3},{3,1},{4,6},{6,4},{5,7},{7,5},{8,10},{10,8},{9,1... | collective-permute-start | bytes 589832 | tf_op jit(solution)/shard_map/ppermute | solution.py:243
  134.1 33.3 %collective-permute-start.15 = (bf16[96,2048]{1,0:T(8,128)(2,1)}, bf16[96,2048]{1,0:T(8,128)(2,1)S(1)}, u32[]{:S(2)}, u32[]{:S(2)}) collective-permute-start(bf16[96,2048]{1,0:T(8,128)(2,1)} %get-tuple-element.63), channel_id=1, source_target_pairs={{0,2},{2,0},{1,3},{3,1},{4,6},{6,4},{5,7},{7,5},{8,10},{10,8},{9,1... | collective-permute-start | bytes 1179656 | tf_op jit(solution)/shard_map/ppermute | solution.py:243
  136.4 31.1 %collective-permute-start.39 = (bf16[96,2048]{1,0:T(8,128)(2,1)S(1)}, bf16[96,2048]{1,0:T(8,128)(2,1)S(1)}, u32[]{:S(2)}, u32[]{:S(2)}) collective-permute-start(bf16[96,2048]{1,0:T(8,128)(2,1)S(1)} %get-tuple-element.83), channel_id=1, source_target_pairs={{0,2},{2,0},{1,3},{3,1},{4,6},{6,4},{5,7},{7,5},{8,10},{10,8},{9,1... | collective-permute-start | bytes 1179656 | tf_op jit(solution)/shard_map/ppermute | solution.py:243
  140.6 33.7 %collective-permute-start.32 = (bf16[96,2048]{1,0:T(8,128)(2,1)S(1)}, bf16[96,2048]{1,0:T(8,128)(2,1)S(1)}, u32[]{:S(2)}, u32[]{:S(2)}) collective-permute-start(bf16[96,2048]{1,0:T(8,128)(2,1)S(1)} %get-tuple-element.77), channel_id=1, source_target_pairs={{0,2},{2,0},{1,3},{3,1},{4,6},{6,4},{5,7},{7,5},{8,10},{10,8},{9,1... | collective-permute-start | bytes 1179656 | tf_op jit(solution)/shard_map/ppermute | solution.py:243
  166.8 54.7 %collective-permute-start.46 = (bf16[256,2048]{1,0:T(8,128)(2,1)S(1)}, bf16[256,2048]{1,0:T(8,128)(2,1)S(1)}, u32[]{:S(2)}, u32[]{:S(2)}) collective-permute-start(bf16[256,2048]{1,0:T(8,128)(2,1)S(1)} %get-tuple-element.100), channel_id=1, source_target_pairs={{0,1},{1,0},{2,3},{3,2},{4,5},{5,4},{6,7},{7,6},{8,9},{9,8},{10,11... | collective-permute-start | bytes 3145736 | tf_op jit(solution)/shard_map/ppermute | solution.py:243
  166.9 54.6 %collective-permute-start.47 = (bf16[256,2048]{1,0:T(8,128)(2,1)S(1)}, bf16[256,2048]{1,0:T(8,128)(2,1)S(1)}, u32[]{:S(2)}, u32[]{:S(2)}) collective-permute-start(bf16[256,2048]{1,0:T(8,128)(2,1)S(1)} %get-tuple-element.101), channel_id=1, source_target_pairs={{0,1},{1,0},{2,3},{3,2},{4,5},{5,4},{6,7},{7,6},{8,9},{9,8},{10,11... | collective-permute-start | bytes 3145736 | tf_op jit(solution)/shard_map/ppermute | solution.py:243
  167.4 54.2 %collective-permute-start.48 = (bf16[256,2048]{1,0:T(8,128)(2,1)}, bf16[256,2048]{1,0:T(8,128)(2,1)S(1)}, u32[]{:S(2)}, u32[]{:S(2)}) collective-permute-start(bf16[256,2048]{1,0:T(8,128)(2,1)} %get-tuple-element.102), channel_id=1, source_target_pairs={{0,1},{1,0},{2,3},{3,2},{4,5},{5,4},{6,7},{7,6},{8,9},{9,8},{10,11... | collective-permute-start | bytes 3145736 | tf_op jit(solution)/shard_map/ppermute | solution.py:243
  (40 other events, 695.2 us)

commit v4 on v3

v4 whole, which is shorter than its diff:
```python
import functools

import jax
import jax.numpy as jnp
from jax import lax
from jax.experimental import pallas as pl
from jax.experimental.pallas import tpu as pltpu
from jax.sharding import PartitionSpec as P

HEADS = 8
HD = 128
SHARDS = 4
PIECE = 16
VMEM_LIMIT = 60 * 1024 * 1024
EXP = ("group", "side", "core")

NT = (((1,), (1,)), ((), ()))
TN = (((0,), (0,)), ((), ()))

VMEM = pl.BlockSpec(memory_space=pltpu.VMEM)
ANY = pl.BlockSpec(memory_space=pl.ANY)


def dot(a, b, dims=(((1,), (0,)), ((), ()))):
    return lax.dot_general(a, b, dims, preferred_element_type=jnp.float32)


def shape_of(*shape, dtype=jnp.bfloat16):
    return jax.ShapeDtypeStruct(shape, dtype)


def call(body, name, operands, outs, flops=0, after=()):
    pieces = [piece for group, _ in operands for piece in group]
    values = []
    for value, _, _ in pieces:
        if not any(value is known for known in values):
            values.append(value)
    where = [[value is known for known in values].index(True) for value, _, _ in pieces]
    n_in, n_outs = len(values) + len(after), len(outs)

    def kernel(*refs):
        out_refs = refs[n_in : n_in + n_outs]
        targets = refs[n_in + n_outs : -1]
        sem = refs[-1]
        waits, at = [], 0
        for (group, _), target in zip(operands, targets):
            copies = []
            for _, source_index, target_index in group:
                source = refs[where[at]]
                copies.append(
                    pltpu.make_async_copy(
                        source if source_index is None else source.at[source_index],
                        target if target_index is None else target.at[target_index],
                        sem.at[at],
                    )
                )
                at += 1
            waits.append(copies)
        for copies in waits:
            for copy in copies:
                copy.start()

        def ready(n):
            for copy in waits[n]:
                copy.wait()
            return targets[n]

        body(ready, out_refs)

    moved = sum(v.size * v.dtype.itemsize for v in values)
    return pl.pallas_call(
        kernel,
        out_shape=tuple(outs),
        in_specs=[ANY] * n_in,
        out_specs=(VMEM,) * n_outs,
        scratch_shapes=[pltpu.VMEM(shape, group[0][0].dtype) for group, shape in operands]
        + [pltpu.SemaphoreType.DMA((len(pieces),))],
        compiler_params=pltpu.CompilerParams(vmem_limit_bytes=VMEM_LIMIT),
        cost_estimate=pl.CostEstimate(flops=flops, bytes_accessed=moved, transcendentals=0),
        name=name,
    )(*values, *after)


def whole(value):
    return [(value, None, None)], value.shape


def rows_of(values):
    pieces, row = [], 0
    for value in values:
        pieces.append((value, None, pl.ds(row, value.shape[0])))
        row += value.shape[0]
    return pieces, (row, values[0].shape[1])


def column(row):
    size = row.shape[1]
    across = lax.broadcasted_iota(jnp.int32, (size, size), 0)
    along = lax.broadcasted_iota(jnp.int32, (size, size), 1)
    return jnp.sum(jnp.where(across == along, row, jnp.zeros_like(row)), axis=1, keepdims=True)


def choosers(pos, slots):
    line = lax.broadcasted_iota(jnp.int32, (pos[0].shape[0], slots), 1)
    return [(place == line).astype(jnp.bfloat16) for place in pos]


def positions(capacity, ids):
    tokens = ids[0].shape[0]
    lanes = lax.broadcasted_iota(jnp.int32, (tokens, 128), 1)
    hot = [(ids[k] == lanes).astype(jnp.float32) for k in range(2)]
    later = lax.broadcasted_iota(jnp.int32, (tokens, tokens), 0)
    earlier = lax.broadcasted_iota(jnp.int32, (tokens, tokens), 1)
    lower = (later > earlier).astype(jnp.bfloat16)
    before = dot(lower, (hot[0] + hot[1]).astype(jnp.bfloat16))
    pos = []
    for k in range(2):
        slot = jnp.sum(hot[k] * before, axis=1, keepdims=True).astype(jnp.int32)
        pos.append(ids[k] * capacity + slot)
    return pos


def chunk_position(pos, capacity, first, count):
    expert = pos // capacity
    slot = pos - expert * capacity - first
    return jnp.where((slot >= 0) & (slot < count), expert * count + slot, -1)


def place_cots(capacity, first, ready, grad_at, gates, pos, out_ref):
    blocks, count, _ = out_ref.shape
    piece = count if blocks > 1 else capacity
    pick = choosers(
        [chunk_position(place, capacity, first, piece) for place in pos], blocks * count
    )
    grad = ready(grad_at)[...].astype(jnp.float32)
    placed = 0.0
    for k in range(2):
        placed = placed + dot(pick[k], (gates[k] * grad).astype(jnp.bfloat16), TN)
    out_ref[...] = placed.astype(jnp.bfloat16).reshape(out_ref.shape)


def slots_body(capacity, ready, outs):
    pos_ref, cot_ref = outs
    ids_ref = ready(0)
    pos = positions(capacity, [column(ids_ref[k : k + 1]) for k in range(2)])
    pair = lax.broadcasted_iota(jnp.int32, (pos[0].shape[0], 2), 1)
    pos_ref[...] = jnp.where(pair == 0, pos[0], pos[1])
    gates_ref = ready(1)
    gates = [column(gates_ref[k : k + 1]) for k in range(2)]
    place_cots(capacity, 0, ready, 2, gates, pos, cot_ref)


def late_slots_body(capacity, first, ready, outs):
    pos_ref, gates_ref = ready(0), ready(1)
    gates = [column(gates_ref[k : k + 1]) for k in range(2)]
    pos = [pos_ref[:, k : k + 1] for k in range(2)]
    place_cots(capacity, first, ready, 2, gates, pos, outs[0])


def attend_body(ready, outs):
    mixed_ref, normed_ref = outs
    query_ref, key_ref, value_ref = ready(0), ready(1), ready(2)
    parts = []
    for head in range(HEADS):
        cols = slice(head * HD, (head + 1) * HD)
        scores = dot(query_ref[:, cols], key_ref[:, cols], NT) * (HD ** (-0.5))
        weights = jnp.exp(scores - jnp.max(scores, axis=1, keepdims=True))
        total = jnp.sum(weights, axis=1, keepdims=True)
        accum = dot(weights.astype(jnp.bfloat16), value_ref[:, cols])
        parts.append((accum / total).astype(jnp.bfloat16))
    attended = jnp.concatenate(parts, axis=1)
    token_ref, proj_ref = ready(3), ready(4)
    mixed = token_ref[...].astype(jnp.float32) + dot(attended, proj_ref[...])
    mixed_ref[...] = mixed
    mean_square = jnp.mean(mixed * mixed, axis=1, keepdims=True)
    scale_ref, shift_ref = ready(5), ready(6)
    normed = mixed * lax.rsqrt(mean_square + 1e-06) * (1.0 + scale_ref[...]) + shift_ref[...]
    normed_ref[...] = normed.astype(jnp.bfloat16)


def place_body(capacity, firsts, ready, outs):
    pos_ref = ready(0)
    pos = [pos_ref[:, k : k + 1] for k in range(2)]
    normed = ready(1)[...]
    for first, out_ref in zip(firsts, outs):
        blocks, count, _ = out_ref.shape
        piece = count if blocks > 1 else capacity
        pick = choosers(
            [chunk_position(place, capacity, first, piece) for place in pos], blocks * count
        )
        placed = dot(pick[0] + pick[1], normed, TN).astype(jnp.bfloat16)
        out_ref[...] = placed.reshape(out_ref.shape)


def forward_body(ready, outs):
    keep_ref, send_ref, gate_pre_ref, up_pre_ref = outs
    row_ref = ready(0)
    rows = row_ref[...].reshape(-1, row_ref.shape[-1])
    gate_pre = dot(ready(1)[...], rows, NT)
    gate_pre_ref[...] = gate_pre
    up_pre = dot(ready(2)[...], rows, NT)
    up_pre_ref[...] = up_pre
    hidden = (gate_pre * jax.nn.sigmoid(gate_pre) * up_pre).astype(jnp.bfloat16)
    half = rows.shape[0] // 2
    partial = dot(hidden, ready(3)[...], TN).astype(jnp.bfloat16)
    keep_ref[...] = partial[:half]
    send_ref[...] = partial[half:]


def add_body(ready, outs):
    for n, out_ref in enumerate(outs):
        total = ready(2 * n)[...].astype(jnp.float32) + ready(2 * n + 1)[...].astype(jnp.float32)
        out_ref[...] = total.astype(jnp.bfloat16).reshape(out_ref.shape)


def backward_body(ready, outs):
    kept, sent = outs[:3], outs[3:]
    cot_ref, down_ref = ready(0), ready(1)
    cots = cot_ref[...]
    hidden_grad = dot(down_ref[...], cots, NT)
    gate_pre = ready(2)[...]
    up_pre = ready(3)[...]
    sigmoid = jax.nn.sigmoid(gate_pre)
    active = gate_pre * sigmoid
    gate_cot = hidden_grad * up_pre * sigmoid * (1.0 + gate_pre * (1.0 - sigmoid))
    up_cot = hidden_grad * active
    half = kept[0].shape[0]
    both = jnp.concatenate([gate_cot.astype(jnp.bfloat16), up_cot.astype(jnp.bfloat16)], axis=0)
    grads = dot(both, ready(4)[...])
    for n in range(2):
        kept[n][...] = grads[2 * n * half : (2 * n + 1) * half]
        sent[n][...] = grads[(2 * n + 1) * half : (2 * n + 2) * half].astype(jnp.bfloat16)
    grads = dot((active * up_pre).astype(jnp.bfloat16), cots)
    kept[2][...] = grads[:half]
    sent[2][...] = grads[half:].astype(jnp.bfloat16)


def combine_body(ready, outs):
    pos_ref, gates_ref = ready(0), ready(1)
    row_ref = ready(2)
    rows = row_ref[...].reshape(-1, row_ref.shape[-1])
    pick = choosers([pos_ref[:, 0:1], pos_ref[:, 1:2]], rows.shape[0])
    picked = dot(jnp.concatenate(pick, axis=0), rows)
    total = ready(3)[...]
    tokens = total.shape[0]
    for k in range(2):
        total = total + column(gates_ref[k : k + 1]) * picked[k * tokens : (k + 1) * tokens]
    outs[0][...] = total.astype(jnp.bfloat16)


def per_device(
    tokens,
    queries,
    keys,
    values,
    out_proj,
    mod_scale,
    mod_shift,
    expert_ids,
    gates,
    w_gate,
    w_up,
    w_down,
    out_grad,
):
    n_ctx = lax.axis_size("ctx")
    experts = n_ctx * lax.axis_size("group")
    local = tokens.shape[1]
    width = tokens.shape[2]
    hidden = w_gate.shape[0]
    capacity = 3 * local // experts
    slots = experts * capacity
    if capacity % PIECE == 0 and capacity > PIECE:
        blocks, height = experts, capacity
        row_cuts = [(0, capacity - PIECE), (capacity - PIECE, PIECE)]
        cot_cuts = [(0, PIECE), (PIECE, capacity - PIECE)]
    else:
        blocks, height = 1, slots
        row_cuts = cot_cuts = [(0, slots)]

    def swapped(value, axis):
        return lax.ppermute(value, axis, [(n, n ^ 1) for n in range(lax.axis_size(axis))])

    def exchanged(value):
        shaped = value if blocks > 1 else value.reshape(experts, capacity, width)
        moved = lax.all_to_all(shaped, ("ctx", "group"), split_axis=0, concat_axis=0, tiled=True)
        return moved.reshape(value.shape)

    def turned(value, step):
        size = lax.axis_size("ctx")
        return lax.ppermute(value, "ctx", [(n, (n + step) % size) for n in range(size)])

    def chunk_shapes(cuts):
        return [shape_of(blocks, count, width) for _, count in cuts]

    key_pieces = [keys[0]] + [turned(keys[0], step) for step in range(1, n_ctx)]
    value_pieces = [values[0]] + [turned(values[0], step) for step in range(1, n_ctx)]

    ids_rows = jnp.transpose(expert_ids[0])
    gate_rows = jnp.transpose(gates[0])
    pos, first_cots = call(
        functools.partial(slots_body, capacity),
        "slots",
        [whole(ids_rows), whole(gate_rows), whole(out_grad[0])],
        [shape_of(local, 2, dtype=jnp.int32)] + chunk_shapes(cot_cuts[:1]),
        flops=4 * slots * local * width,
    )
    cots = [exchanged(first_cots)]
    cots_across = [swapped(cots[0], "side")]

    mixed, normed = call(
        attend_body,
        "attend",
        [
            whole(queries[0]),
            rows_of(key_pieces),
            rows_of(value_pieces),
            whole(tokens[0]),
            whole(out_proj),
            whole(mod_scale),
            whole(mod_shift),
        ],
        [shape_of(local, width, dtype=jnp.float32), shape_of(local, width)],
        flops=4 * local * HEADS * HD * width,
    )
    placed = call(
        functools.partial(place_body, capacity, [first for first, _ in row_cuts]),
        "place",
        [whole(pos), whole(normed)],
        chunk_shapes(row_cuts),
        flops=2 * slots * local * width,
        after=cots,
    )
    rows = [exchanged(value) for value in placed]
    rows_across = [swapped(value, "side") for value in rows]

    for first, count in cot_cuts[1:]:
        (late_cots,) = call(
            functools.partial(late_slots_body, capacity, first),
            "late_slots",
            [whole(pos), whole(gate_rows), whole(out_grad[0])],
            [shape_of(blocks, count, width)],
            flops=4 * slots * local * width,
            after=rows,
        )
        cots.append(exchanged(late_cots))
        cots_across.append(swapped(cots[-1], "side"))

    pairs = [[weight, swapped(weight, "core")] for weight in (w_gate, w_up, w_down)]
    gate_pres, up_pres, returned = [], [], []
    after = cots_across[:1]
    for (_, count), own, across in zip(row_cuts, rows, rows_across):
        half = blocks * count
        pre = shape_of(2 * hidden, 2 * half, dtype=jnp.float32)
        keep, send, gate_pre, up_pre = call(
            forward_body,
            "forward",
            [([(own, None, 0), (across, None, 1)], (2,) + own.shape)]
            + [rows_of(pair) for pair in pairs],
            [shape_of(half, width)] * 2 + [pre] * 2,
            flops=24 * half * hidden * width,
            after=after,
        )
        after = [keep]
        gate_pres.append(gate_pre)
        up_pres.append(up_pre)
        (sums,) = call(
            add_body,
            "add",
            [whole(keep), whole(swapped(send, "side"))],
            [shape_of(blocks, count, width)],
        )
        returned.append(exchanged(sums))

    total_rows = 2 * slots
    row_pieces, cot_pieces, pre_pieces, line = [], [], [[], []], 0
    for n, (first, count) in enumerate(row_cuts):
        for side, both in enumerate(((rows, cots), (rows_across, cots_across))):
            for block in range(blocks):
                start = line + (side * blocks + block) * count
                row_pieces.append((both[0][n], block, pl.ds(start, count)))
                for (cot_first, cot_count), value in zip(cot_cuts, both[1]):
                    low = max(first, cot_first)
                    high = min(first + count, cot_first + cot_count)
                    if low < high:
                        source = (block, pl.ds(low - cot_first, high - low))
                        cot_pieces.append((value, source, pl.ds(start + low - first, high - low)))
        for pieces, pres in zip(pre_pieces, (gate_pres, up_pres)):
            target = (slice(None), pl.ds(line, 2 * blocks * count))
            pieces.append((pres[n], None, target))
        line += 2 * blocks * count
    grads = call(
        backward_body,
        "backward",
        [
            (cot_pieces, (total_rows, width)),
            rows_of(pairs[2]),
            (pre_pieces[0], (2 * hidden, total_rows)),
            (pre_pieces[1], (2 * hidden, total_rows)),
            (row_pieces, (total_rows, width)),
        ],
        [shape_of(hidden, width, dtype=jnp.float32)] * 3 + [shape_of(hidden, width)] * 3,
        flops=16 * total_rows * hidden * width,
    )
    operands = []
    for kept, sent in zip(grads[:3], grads[3:]):
        operands += [whole(kept), whole(swapped(sent, "core"))]
    grad_gate, grad_up, grad_down = call(
        add_body, "finish", operands, [shape_of(hidden, width)] * 3
    )

    returned_pieces = []
    for (first, count), value in zip(row_cuts, returned):
        returned_pieces.append((value, None, (slice(None), pl.ds(first, count))))
    (layer_out,) = call(
        combine_body,
        "combine",
        [
            whole(pos),
            whole(gate_rows),
            (returned_pieces, (blocks, height, width)),
            whole(mixed),
        ],
        [shape_of(local, width)],
        flops=4 * slots * local * width,
    )
    return (layer_out[None], grad_gate, grad_up, grad_down)


def solution(mesh):
    n_ctx = mesh.shape["ctx"]
    cut = (n_ctx, mesh.shape["exp"] // SHARDS, SHARDS // 2, 2)
    mesh = jax.sharding.Mesh(mesh.devices.reshape(cut), ("ctx",) + EXP)
    rows = P(EXP, "ctx", None)
    weight = P(("ctx",) + EXP, None)
    return jax.shard_map(
        per_device,
        mesh=mesh,
        in_specs=(rows, rows, rows, rows, P(), P(EXP, None), P(EXP, None), rows, rows)
        + (weight, weight, weight, rows),
        out_specs=(rows, weight, weight, weight),
        check_vma=False,
    )
```

time: 237 us -> 216 us (0.911)
  blocking collectives: 0 us -> 30.9 us
  starting transfers between devices: 63.9 us -> 36.7 us
  waiting for transfers between devices: 102 us -> 83.6 us
  Pallas kernels: 59 us -> 55.5 us
    ppermute x23 -> x2, waiting for transfers between devices: 72.8 us -> 17.1 us  [turned(): lax.ppermute(value, 'ctx', [(n, (n + step) % size) for n in range(size)])]
    ppermute x23 -> x2, starting transfers between devices: 39 us -> 2.1 us  [turned(): lax.ppermute(value, 'ctx', [(n, (n + step) % size) for n in range(size)])]
    all_to_all x0 -> x1, blocking collectives: none -> 30.9 us  [exchanged(): lax.all_to_all(shaped, ('ctx', 'group'), split_axis=0, concat_axis=0, til...]
    all_to_all x0 -> x5, starting transfers between devices: none -> 26.2 us  [exchanged(): lax.all_to_all(shaped, ('ctx', 'group'), split_axis=0, concat_axis=0, til...]
    ppermute x26 -> x12, waiting for transfers between devices: 29.6 us -> 54.8 us  [swapped(): lax.ppermute(value, axis, [(n, n ^ 1) for n in range(lax.axis_size(axis))])]
    ppermute x26 -> x12, starting transfers between devices: 24.9 us -> 8.42 us  [swapped(): lax.ppermute(value, axis, [(n, n ^ 1) for n in range(lax.axis_size(axis))])]
    all_to_all x0 -> x5, waiting for transfers between devices: none -> 11.7 us  [exchanged(): lax.all_to_all(shaped, ('ctx', 'group'), split_axis=0, concat_axis=0, til...]
    pallas_call x13 -> x11, Pallas kernels: 59 us -> 55.5 us  [call(): pl.pallas_call(kernel, out_shape=tuple(outs), in_specs=[ANY] * n_in, out_...]
  transfers between devices with their start and end apart: 49 -> 19, of which waited for: 27 -> 10; matrix products, arithmetic and copies ran while one was open for 0% -> 0% of each run, Pallas kernels for 18% -> 21%
where the time goes in v4:
time: 216 us; the launch traced here: 215 us
  waiting for transfers between devices  83.6 us (39%)
  Pallas kernels  55.5 us (26%)
  starting transfers between devices  36.7 us (17%)
  blocking collectives  30.9 us (14%)
  local copies, waits for them, and re-layouts  7.61 us (4%)
    pallas_call x11, Pallas kernels, call(): pl.pallas_call(kernel, out_shape=tuple(outs), in_specs=[ANY] * n_in, out_...  55.5 us
    ppermute x12, waiting for transfers between devices, swapped(): lax.ppermute(value, axis, [(n, n ^ 1) for n in range(lax.axis_size(axis))])  54.8 us
    all_to_all x1, blocking collectives, exchanged(): lax.all_to_all(shaped, ('ctx', 'group'), split_axis=0, concat_axis=0, til...  30.9 us
    all_to_all x5, starting transfers between devices, exchanged(): lax.all_to_all(shaped, ('ctx', 'group'), split_axis=0, concat_axis=0, til...  26.2 us
    ppermute x2, waiting for transfers between devices, turned(): lax.ppermute(value, 'ctx', [(n, (n + step) % size) for n in range(size)])  17.1 us
    all_to_all x5, waiting for transfers between devices, exchanged(): lax.all_to_all(shaped, ('ctx', 'group'), split_axis=0, concat_axis=0, til...  11.7 us
    ppermute x12, starting transfers between devices, swapped(): lax.ppermute(value, axis, [(n, n ^ 1) for n in range(lax.axis_size(axis))])  8.42 us
    unnamed x36, local copies, waits for them, and re-layouts  7.61 us
  transfers between devices with their start and end apart: 19, of which 10 were waited for; matrix products, arithmetic and copies ran while one was open for 0% of the time, Pallas kernels for 21%

profile of v4, /device:TPU:0, one launch (start us, length us, event | category | flops | bytes accessed | tf_op | source)
XLA Modules:
  0.0 215.4 jit_solution(17762394915422223671)
XLA Ops:
  0.7 2.6 %slots.1 = (s32[128,2]{1,0:T(8,128)}, bf16[8,16,2048]{2,1,0:T(8,128)(2,1)}) custom-call(s32[2,128]{1,0:T(2,128)} %bitcast.24, f32[2,128]{1,0:T(2,128)} %bitcast.21, bf16[128,2048]{1,0:T(8,128)(2,1)} %bitcast.13), custom_call_target="tpu_custom_call" | custom-call | flops 402653184 | bytes 526336 | tf_op jit(solution)/shard_map/slots/pallas_call | solution.py:71
  3.2 7.3 %all-to-all-start = ((bf16[8,16,2048]{2,1,0:T(8,128)(2,1)}), bf16[8,16,2048]{2,1,0:T(8,128)(2,1)S(1)}, u32[]{:S(2)}, u32[]{:S(2)}) async-start(bf16[8,16,2048]{2,1,0:T(8,128)(2,1)} %get-tuple-element.29), calls=%async_computation | async-start | bytes 1048576 | tf_op jit(solution)/shard_map/all_to_all | solution.py:286
  12.6 12.3 %collective-permute-done.refs_2_ = bf16[128,1024]{1,0:T(8,128)(2,1)S(1)} collective-permute-done((bf16[128,1024]{1,0:T(8,128)(2,1)S(1)}, bf16[128,1024]{1,0:T(8,128)(2,1)S(1)}, u32[]{:S(2)}, u32[]{:S(2)}) %collective-permute-start) | collective-permute-done | bytes 262176 | tf_op jit(solution)/shard_map/ppermute | solution.py:291
  24.9 4.9 %collective-permute-done.1.refs_4_ = bf16[128,1024]{1,0:T(8,128)(2,1)S(1)} collective-permute-done((bf16[128,1024]{1,0:T(8,128)(2,1)S(1)}, bf16[128,1024]{1,0:T(8,128)(2,1)S(1)}, u32[]{:S(2)}, u32[]{:S(2)}) %collective-permute-start.1) | collective-permute-done | bytes 262176 | tf_op jit(solution)/shard_map/ppermute | solution.py:291
  30.4 4.8 %attend.1 = (f32[128,2048]{1,0:T(8,128)}, bf16[128,2048]{1,0:T(8,128)(2,1)}) custom-call(bf16[128,1024]{1,0:T(8,128)(2,1)} %bitcast.16, bf16[128,1024]{1,0:T(8,128)(2,1)} %bitcast.17, bf16[128,1024]{1,0:T(8,128)(2,1)} %copy-done.15, bf16[128,1024]{1,0:T(8,128)(2,1)} %bitcast.19, bf16[128,1024]{1,0:T(8,128)(2,1)} %copy-done.16, bf16[128,2048]{1,0:T(8,128)(2,1)} %bitcast.12, ...), custom_call_target="tpu_custom_call" | custom-call | flops 1073741824 | bytes 6045696 | tf_op jit(solution)/shard_map/attend/pallas_call | solution.py:71
  36.1 2.8 %place.1 = (bf16[8,32,2048]{2,1,0:T(8,128)(2,1)}, bf16[8,16,2048]{2,1,0:T(8,128)(2,1)}) custom-call(s32[128,2]{1,0:T(8,128)} %get-tuple-element.27.refs_0_, bf16[128,2048]{1,0:T(8,128)(2,1)} %get-tuple-element.28.refs_1_, bf16[8,16,2048]{2,1,0:T(8,128)(2,1)} %copy-done.4), custom_call_target="tpu_custom_call" | custom-call | flops 201326592 | bytes 525312 | tf_op jit(solution)/shard_map/place/pallas_call | solution.py:71
  38.9 30.9 %all_to_all.30.refs_0_.refs_3_.refs_10_ = bf16[8,32,2048]{2,1,0:T(8,128)(2,1)S(1)} all-to-all(bf16[8,32,2048]{2,1,0:T(8,128)(2,1)} %get-tuple-element.30), channel_id=1, replica_groups=mesh['ctx'=2,'group'=4,'side'=2,'core'=2] {'ctx','group'}, dimensions={0} | all-to-all | bytes 2097152 | tf_op jit(solution)/shard_map/all_to_all | solution.py:286
  69.8 3.5 %all-to-all-start.3 = ((bf16[8,16,2048]{2,1,0:T(8,128)(2,1)}), bf16[8,16,2048]{2,1,0:T(8,128)(2,1)S(1)}, u32[]{:S(2)}, u32[]{:S(2)}) async-start(bf16[8,16,2048]{2,1,0:T(8,128)(2,1)} %get-tuple-element.33), calls=%async_computation.3 | async-start | bytes 1048576 | tf_op jit(solution)/shard_map/all_to_all | solution.py:286
  75.5 11.7 %all-to-all-done.3.refs_0_.refs_4_.refs_12_ = bf16[8,16,2048]{2,1,0:T(8,128)(2,1)S(1)} async-done(((bf16[8,16,2048]{2,1,0:T(8,128)(2,1)}), bf16[8,16,2048]{2,1,0:T(8,128)(2,1)S(1)}, u32[]{:S(2)}, u32[]{:S(2)}) %all-to-all-start.3) | async-done | bytes 524320 | tf_op jit(solution)/shard_map/all_to_all | solution.py:286
  88.0 2.9 %late_slots.1 = bf16[8,32,2048]{2,1,0:T(8,128)(2,1)} custom-call(s32[128,2]{1,0:T(8,128)} %get-tuple-element.27.refs_0_, f32[2,128]{1,0:T(2,128)} %bitcast.22, bf16[128,2048]{1,0:T(8,128)(2,1)} %bitcast.14, bf16[8,32,2048]{2,1,0:T(8,128)(2,1)} %copy-done.2, bf16[8,16,2048]{2,1,0:T(8,128)(2,1)} %copy-done), custom_call_target="tpu_custom_call" | custom-call | flops 402653184 | bytes 526336 | tf_op jit(solution)/shard_map/late_slots/pallas_call | solution.py:71
  90.9 3.7 %all-to-all-start.5 = ((bf16[8,32,2048]{2,1,0:T(8,128)(2,1)}), bf16[8,32,2048]{2,1,0:T(8,128)(2,1)S(1)}, u32[]{:S(2)}, u32[]{:S(2)}) async-start(bf16[8,32,2048]{2,1,0:T(8,128)(2,1)} %late_slots.1), calls=%async_computation.5 | async-start | bytes 2097152 | tf_op jit(solution)/shard_map/all_to_all | solution.py:286
  96.7 14.5 %collective-permute-done.6.refs_8_.refs_2_ = bf16[8,16,2048]{2,1,0:T(8,128)(2,1)S(1)} collective-permute-done((bf16[8,16,2048]{2,1,0:T(8,128)(2,1)S(1)}, bf16[8,16,2048]{2,1,0:T(8,128)(2,1)S(1)}, u32[]{:S(2)}, u32[]{:S(2)}) %collective-permute-start.6) | collective-permute-done | bytes 524320 | tf_op jit(solution)/shard_map/ppermute | solution.py:282
  112.0 7.7 %forward.2 = (bf16[256,2048]{1,0:T(8,128)(2,1)}, bf16[256,2048]{1,0:T(8,128)(2,1)}, f32[512,512]{1,0:T(8,128)}, f32[512,512]{1,0:T(8,128)}) custom-call(bf16[8,32,2048]{2,1,0:T(8,128)(2,1)} %copy-done.2, bf16[8,32,2048]{2,1,0:T(8,128)(2,1)} %collective-permute-done.2.refs_1_.refs_11_, bf16[256,2048]{1,0:T(8,128)(2,1)} %refs_2_.3, ...), custom_call_target="tpu_custom_call" | custom-call | flops 3221225472 | bytes 8388608 | tf_op jit(solution)/shard_map/forward/pallas_call | solution.py:71
  119.7 2.3 %collective-permute-done.8.refs_1_.refs_13_ = bf16[8,16,2048]{2,1,0:T(8,128)(2,1)S(1)} collective-permute-done((bf16[8,16,2048]{2,1,0:T(8,128)(2,1)S(1)}, bf16[8,16,2048]{2,1,0:T(8,128)(2,1)S(1)}, u32[]{:S(2)}, u32[]{:S(2)}) %collective-permute-start.8) | collective-permute-done | bytes 524320 | tf_op jit(solution)/shard_map/ppermute | solution.py:282
  122.8 6.3 %forward.3 = (bf16[128,2048]{1,0:T(8,128)(2,1)}, bf16[128,2048]{1,0:T(8,128)(2,1)}, f32[512,256]{1,0:T(8,128)}, f32[512,256]{1,0:T(8,128)}) custom-call(bf16[8,16,2048]{2,1,0:T(8,128)(2,1)} %copy-done, bf16[8,16,2048]{2,1,0:T(8,128)(2,1)} %copy-done.11, bf16[256,2048]{1,0:T(8,128)(2,1)} %refs_2_.3, bf16[256,2048]{1,0:T(8,128)(2,1)} %collective-permute-done.3.refs_3_, ...), custom_call_target="tpu_custom_call" | custom-call | flops 1610612736 | bytes 7340032 | tf_op jit(solution)/shard_map/forward/pallas_call | solution.py:71
  131.2 13.0 %collective-permute-done.9.refs_1_ = bf16[128,2048]{1,0:T(8,128)(2,1)S(1)} collective-permute-done((bf16[128,2048]{1,0:T(8,128)(2,1)}, bf16[128,2048]{1,0:T(8,128)(2,1)S(1)}, u32[]{:S(2)}, u32[]{:S(2)}) %collective-permute-start.9) | collective-permute-done | bytes 524320 | tf_op jit(solution)/shard_map/ppermute | solution.py:282
  147.2 5.9 %all-to-all-start.4 = ((bf16[8,16,2048]{2,1,0:T(8,128)(2,1)}), bf16[8,16,2048]{2,1,0:T(8,128)(2,1)S(1)}, u32[]{:S(2)}, u32[]{:S(2)}) async-start(bf16[8,16,2048]{2,1,0:T(8,128)(2,1)} %add.3), calls=%async_computation.4 | async-start | bytes 1048576 | tf_op jit(solution)/shard_map/all_to_all | solution.py:286
  154.5 12.2 %collective-permute-done.7.refs_1_ = bf16[256,2048]{1,0:T(8,128)(2,1)S(1)} collective-permute-done((bf16[256,2048]{1,0:T(8,128)(2,1)}, bf16[256,2048]{1,0:T(8,128)(2,1)S(1)}, u32[]{:S(2)}, u32[]{:S(2)}) %collective-permute-start.7) | collective-permute-done | bytes 1048608 | tf_op jit(solution)/shard_map/ppermute | solution.py:282
  167.7 2.7 %add.2 = bf16[8,32,2048]{2,1,0:T(8,128)(2,1)} custom-call(bf16[256,2048]{1,0:T(8,128)(2,1)} %get-tuple-element.31.refs_0_.refs_8_, bf16[256,2048]{1,0:T(8,128)(2,1)} %copy-done.9), custom_call_target="tpu_custom_call" | custom-call | bytes 2097152 | tf_op jit(solution)/shard_map/add/pallas_call | solution.py:71
  170.4 5.9 %all-to-all-start.2 = ((bf16[8,32,2048]{2,1,0:T(8,128)(2,1)}), bf16[8,32,2048]{2,1,0:T(8,128)(2,1)S(1)}, u32[]{:S(2)}, u32[]{:S(2)}) async-start(bf16[8,32,2048]{2,1,0:T(8,128)(2,1)} %add.2), calls=%async_computation.2 | async-start | bytes 2097152 | tf_op jit(solution)/shard_map/all_to_all | solution.py:286
  176.3 11.6 %collective-permute-done.10.refs_3_ = bf16[8,32,2048]{2,1,0:T(8,128)(2,1)} collective-permute-done((bf16[8,32,2048]{2,1,0:T(8,128)(2,1)S(1)}, bf16[8,32,2048]{2,1,0:T(8,128)(2,1)}, u32[]{:S(2)}, u32[]{:S(2)}) %collective-permute-start.10) | collective-permute-done | bytes 1048608 | tf_op jit(solution)/shard_map/ppermute | solution.py:282
  187.9 14.9 %backward.1 = (f32[256,2048]{1,0:T(8,128)}, f32[256,2048]{1,0:T(8,128)}, f32[256,2048]{1,0:T(8,128)}, bf16[256,2048]{1,0:T(8,128)(2,1)}, bf16[256,2048]{1,0:T(8,128)(2,1)}, /*index=5*/bf16[256,2048]{1,0:T(8,128)(2,1)}) custom-call(bf16[8,16,2048]{2,1,0:T(8,128)(2,1)} %copy-done.4, bf16[8,32,2048]{2,1,0:T(8,128)(2,1)} %copy-done.10, ...), custom_call_target="tpu_custom_call" | custom-call | flops 6442450944 | bytes 11534336 | tf_op jit(solution)/shard_map/backward/pallas_call | solution.py:71
  204.5 3.3 %combine.1 = bf16[128,2048]{1,0:T(8,128)(2,1)} custom-call(s32[128,2]{1,0:T(8,128)} %get-tuple-element.27.refs_0_, f32[2,128]{1,0:T(2,128)} %bitcast.23, bf16[8,32,2048]{2,1,0:T(8,128)(2,1)} %copy-done.3, bf16[8,16,2048]{2,1,0:T(8,128)(2,1)} %copy-done.6, f32[128,2048]{1,0:T(8,128)} %get-tuple-element.36.refs_4_), custom_call_target="tpu_custom_call" | custom-call | flops 402653184 | bytes 2623488 | tf_op jit(solution)/shard_map/combine/pallas_call | solution.py:71
  209.8 5.4 %finish.1 = (bf16[256,2048]{1,0:T(8,128)(2,1)}, bf16[256,2048]{1,0:T(8,128)(2,1)}, bf16[256,2048]{1,0:T(8,128)(2,1)}) custom-call(f32[256,2048]{1,0:T(8,128)} %get-tuple-element.41.refs_0_, bf16[256,2048]{1,0:T(8,128)(2,1)} %copy-done.7, f32[256,2048]{1,0:T(8,128)} %get-tuple-element.43.refs_2_, bf16[256,2048]{1,0:T(8,128)(2,1)} %copy-done.8, ...), custom_call_target="tpu_custom_call" | custom-call | bytes 9437184 | tf_op jit(solution)/shard_map/finish/pallas_call | solution.py:71
  (62 shorter events, 21.4 us)
Async XLA Ops:
  0.6 11.9 %copy-start.14 = (bf16[1,128,1024]{2,1,0:T(8,128)(2,1)S(1)}, bf16[1,128,1024]{2,1,0:T(8,128)(2,1)}, u32[]{:S(2)}) copy-start(bf16[1,128,1024]{2,1,0:T(8,128)(2,1)} %param.16) | copy-start | bytes 786436
  3.2 32.0 %all-to-all-start = ((bf16[8,16,2048]{2,1,0:T(8,128)(2,1)}), bf16[8,16,2048]{2,1,0:T(8,128)(2,1)S(1)}, u32[]{:S(2)}, u32[]{:S(2)}) async-start(bf16[8,16,2048]{2,1,0:T(8,128)(2,1)} %get-tuple-element.29), calls=%async_computation | async-start | bytes 1048576 | tf_op jit(solution)/shard_map/all_to_all | solution.py:286
  10.5 14.4 %collective-permute-start = (bf16[128,1024]{1,0:T(8,128)(2,1)S(1)}, bf16[128,1024]{1,0:T(8,128)(2,1)S(1)}, u32[]{:S(2)}, u32[]{:S(2)}) collective-permute-start(bf16[128,1024]{1,0:T(8,128)(2,1)S(1)} %bitcast.18), channel_id=1, source_target_pairs={{0,16},{16,0},{1,17},{17,1},{2,18},{18,2},{3,19},{19,3},{4,20},{20... | collective-permute-start | bytes 786440 | tf_op jit(solution)/shard_map/ppermute | solution.py:291
  12.6 17.2 %collective-permute-start.1 = (bf16[128,1024]{1,0:T(8,128)(2,1)S(1)}, bf16[128,1024]{1,0:T(8,128)(2,1)S(1)}, u32[]{:S(2)}, u32[]{:S(2)}) collective-permute-start(bf16[128,1024]{1,0:T(8,128)(2,1)S(1)} %bitcast.20), channel_id=1, source_target_pairs={{0,16},{16,0},{1,17},{17,1},{2,18},{18,2},{3,19},{19,3},{4,20},{20... | collective-permute-start | bytes 786440 | tf_op jit(solution)/shard_map/ppermute | solution.py:291
  69.8 17.3 %copy-start.2 = (bf16[8,32,2048]{2,1,0:T(8,128)(2,1)}, bf16[8,32,2048]{2,1,0:T(8,128)(2,1)S(1)}, u32[]{:S(2)}) copy-start(bf16[8,32,2048]{2,1,0:T(8,128)(2,1)S(1)} %all_to_all.30.refs_0_.refs_3_.refs_10_) | copy-start | bytes 3145732
  69.8 17.3 %all-to-all-start.3 = ((bf16[8,16,2048]{2,1,0:T(8,128)(2,1)}), bf16[8,16,2048]{2,1,0:T(8,128)(2,1)S(1)}, u32[]{:S(2)}, u32[]{:S(2)}) async-start(bf16[8,16,2048]{2,1,0:T(8,128)(2,1)} %get-tuple-element.33), calls=%async_computation.3 | async-start | bytes 1048576 | tf_op jit(solution)/shard_map/all_to_all | solution.py:286
  73.3 21.2 %copy-start.5 = (bf16[8,16,2048]{2,1,0:T(8,128)(2,1)S(1)}, bf16[8,16,2048]{2,1,0:T(8,128)(2,1)}, u32[]{:S(2)}) copy-start(bf16[8,16,2048]{2,1,0:T(8,128)(2,1)} %copy-done.4) | copy-start | bytes 1572868
  73.4 22.8 %collective-permute-start.3 = (bf16[256,2048]{1,0:T(8,128)(2,1)}, bf16[256,2048]{1,0:T(8,128)(2,1)}, u32[]{:S(2)}, u32[]{:S(2)}) collective-permute-start(bf16[256,2048]{1,0:T(8,128)(2,1)} %refs_2_.3), channel_id=1, source_target_pairs={{0,1},{1,0},{2,3},{3,2},{4,5},{5,4},{6,7},{7,6},{8,9},{9,8},{10,11... | collective-permute-start | bytes 3145736 | tf_op jit(solution)/shard_map/ppermute | solution.py:282
  73.4 23.2 %collective-permute-start.4 = (bf16[256,2048]{1,0:T(8,128)(2,1)}, bf16[256,2048]{1,0:T(8,128)(2,1)}, u32[]{:S(2)}, u32[]{:S(2)}) collective-permute-start(bf16[256,2048]{1,0:T(8,128)(2,1)} %refs_4_.4), channel_id=1, source_target_pairs={{0,1},{1,0},{2,3},{3,2},{4,5},{5,4},{6,7},{7,6},{8,9},{9,8},{10,11... | collective-permute-start | bytes 3145736 | tf_op jit(solution)/shard_map/ppermute | solution.py:282
  73.9 22.8 %collective-permute-start.5 = (bf16[256,2048]{1,0:T(8,128)(2,1)}, bf16[256,2048]{1,0:T(8,128)(2,1)}, u32[]{:S(2)}, u32[]{:S(2)}) collective-permute-start(bf16[256,2048]{1,0:T(8,128)(2,1)} %refs_4_.5), channel_id=1, source_target_pairs={{0,1},{1,0},{2,3},{3,2},{4,5},{5,4},{6,7},{7,6},{8,9},{9,8},{10,11... | collective-permute-start | bytes 3145736 | tf_op jit(solution)/shard_map/ppermute | solution.py:282
  74.0 38.0 %collective-permute-start.2 = (bf16[8,32,2048]{2,1,0:T(8,128)(2,1)S(1)}, bf16[8,32,2048]{2,1,0:T(8,128)(2,1)}, u32[]{:S(2)}, u32[]{:S(2)}) collective-permute-start(bf16[8,32,2048]{2,1,0:T(8,128)(2,1)S(1)} %all_to_all.30.refs_0_.refs_3_.refs_10_), channel_id=1, source_target_pairs={{0,2},{2,0},{1,3},{3,1},{4,6},{6,4},{5,7},{7,5},{8,10},{10,8},{9,1... | collective-permute-start | bytes 3145736 | tf_op jit(solution)/shard_map/ppermute | solution.py:282
  90.9 56.3 %all-to-all-start.5 = ((bf16[8,32,2048]{2,1,0:T(8,128)(2,1)}), bf16[8,32,2048]{2,1,0:T(8,128)(2,1)S(1)}, u32[]{:S(2)}, u32[]{:S(2)}) async-start(bf16[8,32,2048]{2,1,0:T(8,128)(2,1)} %late_slots.1), calls=%async_computation.5 | async-start | bytes 2097152 | tf_op jit(solution)/shard_map/all_to_all | solution.py:286
  94.6 16.6 %collective-permute-start.6 = (bf16[8,16,2048]{2,1,0:T(8,128)(2,1)S(1)}, bf16[8,16,2048]{2,1,0:T(8,128)(2,1)S(1)}, u32[]{:S(2)}, u32[]{:S(2)}) collective-permute-start(bf16[8,16,2048]{2,1,0:T(8,128)(2,1)S(1)} %copy-done.5), channel_id=1, source_target_pairs={{0,2},{2,0},{1,3},{3,1},{4,6},{6,4},{5,7},{7,5},{8,10},{10,8},{9,1... | collective-permute-start | bytes 1572872 | tf_op jit(solution)/shard_map/ppermute | solution.py:282
  96.1 25.9 %collective-permute-start.8 = (bf16[8,16,2048]{2,1,0:T(8,128)(2,1)S(1)}, bf16[8,16,2048]{2,1,0:T(8,128)(2,1)S(1)}, u32[]{:S(2)}, u32[]{:S(2)}) collective-permute-start(bf16[8,16,2048]{2,1,0:T(8,128)(2,1)S(1)} %copy-done.1), channel_id=1, source_target_pairs={{0,2},{2,0},{1,3},{3,1},{4,6},{6,4},{5,7},{7,5},{8,10},{10,8},{9,1... | collective-permute-start | bytes 1572872 | tf_op jit(solution)/shard_map/ppermute | solution.py:282
  129.1 15.1 %collective-permute-start.9 = (bf16[128,2048]{1,0:T(8,128)(2,1)}, bf16[128,2048]{1,0:T(8,128)(2,1)S(1)}, u32[]{:S(2)}, u32[]{:S(2)}) collective-permute-start(bf16[128,2048]{1,0:T(8,128)(2,1)} %get-tuple-element.35), channel_id=1, source_target_pairs={{0,2},{2,0},{1,3},{3,1},{4,6},{6,4},{5,7},{7,5},{8,10},{10,8},{9,1... | collective-permute-start | bytes 1572872 | tf_op jit(solution)/shard_map/ppermute | solution.py:282
  130.7 36.0 %collective-permute-start.7 = (bf16[256,2048]{1,0:T(8,128)(2,1)}, bf16[256,2048]{1,0:T(8,128)(2,1)S(1)}, u32[]{:S(2)}, u32[]{:S(2)}) collective-permute-start(bf16[256,2048]{1,0:T(8,128)(2,1)} %get-tuple-element.32), channel_id=1, source_target_pairs={{0,2},{2,0},{1,3},{3,1},{4,6},{6,4},{5,7},{7,5},{8,10},{10,8},{9,1... | collective-permute-start | bytes 3145736 | tf_op jit(solution)/shard_map/ppermute | solution.py:282
  147.2 23.2 %copy-start.10 = (bf16[8,32,2048]{2,1,0:T(8,128)(2,1)}, bf16[8,32,2048]{2,1,0:T(8,128)(2,1)S(1)}, u32[]{:S(2)}) copy-start(bf16[8,32,2048]{2,1,0:T(8,128)(2,1)S(1)} %all-to-all-done.5.refs_1_) | copy-start | bytes 3145732
  147.2 23.2 %all-to-all-start.4 = ((bf16[8,16,2048]{2,1,0:T(8,128)(2,1)}), bf16[8,16,2048]{2,1,0:T(8,128)(2,1)S(1)}, u32[]{:S(2)}, u32[]{:S(2)}) async-start(bf16[8,16,2048]{2,1,0:T(8,128)(2,1)} %add.3), calls=%async_computation.4 | async-start | bytes 1048576 | tf_op jit(solution)/shard_map/all_to_all | solution.py:286
  153.1 34.9 %collective-permute-start.10 = (bf16[8,32,2048]{2,1,0:T(8,128)(2,1)S(1)}, bf16[8,32,2048]{2,1,0:T(8,128)(2,1)}, u32[]{:S(2)}, u32[]{:S(2)}) collective-permute-start(bf16[8,32,2048]{2,1,0:T(8,128)(2,1)S(1)} %all-to-all-done.5.refs_1_), channel_id=1, source_target_pairs={{0,2},{2,0},{1,3},{3,1},{4,6},{6,4},{5,7},{7,5},{8,10},{10,8},{9,1... | collective-permute-start | bytes 3145736 | tf_op jit(solution)/shard_map/ppermute | solution.py:282
  170.4 32.4 %copy-start.6 = (bf16[8,16,2048]{2,1,0:T(8,128)(2,1)}, bf16[8,16,2048]{2,1,0:T(8,128)(2,1)S(1)}, u32[]{:S(2)}) copy-start(bf16[8,16,2048]{2,1,0:T(8,128)(2,1)S(1)} %all-to-all-done.4.refs_3_) | copy-start | bytes 1572868
  170.4 33.1 %all-to-all-start.2 = ((bf16[8,32,2048]{2,1,0:T(8,128)(2,1)}), bf16[8,32,2048]{2,1,0:T(8,128)(2,1)S(1)}, u32[]{:S(2)}, u32[]{:S(2)}) async-start(bf16[8,32,2048]{2,1,0:T(8,128)(2,1)} %add.2), calls=%async_computation.2 | async-start | bytes 2097152 | tf_op jit(solution)/shard_map/all_to_all | solution.py:286
  202.9 4.9 %collective-permute-start.11 = (bf16[256,2048]{1,0:T(8,128)(2,1)}, bf16[256,2048]{1,0:T(8,128)(2,1)S(1)}, u32[]{:S(2)}, u32[]{:S(2)}) collective-permute-start(bf16[256,2048]{1,0:T(8,128)(2,1)} %get-tuple-element.42), channel_id=1, source_target_pairs={{0,1},{1,0},{2,3},{3,2},{4,5},{5,4},{6,7},{7,6},{8,9},{9,8},{10,11... | collective-permute-start | bytes 3145736 | tf_op jit(solution)/shard_map/ppermute | solution.py:282
  202.9 5.9 %collective-permute-start.12 = (bf16[256,2048]{1,0:T(8,128)(2,1)}, bf16[256,2048]{1,0:T(8,128)(2,1)S(1)}, u32[]{:S(2)}, u32[]{:S(2)}) collective-permute-start(bf16[256,2048]{1,0:T(8,128)(2,1)} %get-tuple-element.44), channel_id=1, source_target_pairs={{0,1},{1,0},{2,3},{3,2},{4,5},{5,4},{6,7},{7,6},{8,9},{9,8},{10,11... | collective-permute-start | bytes 3145736 | tf_op jit(solution)/shard_map/ppermute | solution.py:282
  203.4 5.5 %collective-permute-start.13 = (bf16[256,2048]{1,0:T(8,128)(2,1)}, bf16[256,2048]{1,0:T(8,128)(2,1)}, u32[]{:S(2)}, u32[]{:S(2)}) collective-permute-start(bf16[256,2048]{1,0:T(8,128)(2,1)} %get-tuple-element.46), channel_id=1, source_target_pairs={{0,1},{1,0},{2,3},{3,2},{4,5},{5,4},{6,7},{7,6},{8,9},{9,8},{10,11... | collective-permute-start | bytes 3145736 | tf_op jit(solution)/shard_map/ppermute | solution.py:282
  (13 other events, 28.9 us)

commit v5 on v4

--- a/solution.py
+++ b/solution.py
@@ -11,7 +11,7 @@
 HD = 128
 SHARDS = 4
 PIECE = 16
-VMEM_LIMIT = 60 * 1024 * 1024
+VMEM_LIMIT = 63 * 1024 * 1024
 EXP = ("group", "side", "core")
 
 NT = (((1,), (1,)), ((), ()))
@@ -29,7 +29,7 @@
     return jax.ShapeDtypeStruct(shape, dtype)
 
 
-def call(body, name, operands, outs, flops=0, after=()):
+def call(body, name, operands, outs, micros=1, after=()):
     pieces = [piece for group, _ in operands for piece in group]
     values = []
     for value, _, _ in pieces:
@@ -67,7 +67,6 @@
 
         body(ready, out_refs)
 
-    moved = sum(v.size * v.dtype.itemsize for v in values)
     return pl.pallas_call(
         kernel,
         out_shape=tuple(outs),
@@ -76,7 +75,9 @@
         scratch_shapes=[pltpu.VMEM(shape, group[0][0].dtype) for group, shape in operands]
         + [pltpu.SemaphoreType.DMA((len(pieces),))],
         compiler_params=pltpu.CompilerParams(vmem_limit_bytes=VMEM_LIMIT),
-        cost_estimate=pl.CostEstimate(flops=flops, bytes_accessed=moved, transcendentals=0),
+        cost_estimate=pl.CostEstimate(
+            flops=int(micros * 1.15e9), bytes_accessed=0, transcendentals=0
+        ),
         name=name,
     )(*values, *after)
 
@@ -213,8 +214,16 @@
         out_ref[...] = total.astype(jnp.bfloat16).reshape(out_ref.shape)
 
 
+def finish_body(ready, outs):
+    sent_ref = ready(3)
+    size = outs[0].shape[0]
+    for n, out_ref in enumerate(outs):
+        total = ready(n)[...] + sent_ref[n * size : (n + 1) * size].astype(jnp.float32)
+        out_ref[...] = total.astype(jnp.bfloat16)
+
+
 def backward_body(ready, outs):
-    kept, sent = outs[:3], outs[3:]
+    kept, sent_ref = outs[:3], outs[3]
     cot_ref, down_ref = ready(0), ready(1)
     cots = cot_ref[...]
     hidden_grad = dot(down_ref[...], cots, NT)
@@ -229,10 +238,17 @@
     grads = dot(both, ready(4)[...])
     for n in range(2):
         kept[n][...] = grads[2 * n * half : (2 * n + 1) * half]
-        sent[n][...] = grads[(2 * n + 1) * half : (2 * n + 2) * half].astype(jnp.bfloat16)
+        sent = grads[(2 * n + 1) * half : (2 * n + 2) * half].astype(jnp.bfloat16)
+        sent_ref[n * half : (n + 1) * half] = sent
     grads = dot((active * up_pre).astype(jnp.bfloat16), cots)
     kept[2][...] = grads[:half]
-    sent[2][...] = grads[half:].astype(jnp.bfloat16)
+    sent_ref[2 * half :] = grads[half:].astype(jnp.bfloat16)
+
+
+def pack_body(ready, outs):
+    size = outs[0].shape[0] // 3
+    for n in range(3):
+        outs[0][n * size : (n + 1) * size] = ready(n)[...]
 
 
 def combine_body(ready, outs):
@@ -303,10 +319,19 @@
         "slots",
         [whole(ids_rows), whole(gate_rows), whole(out_grad[0])],
         [shape_of(local, 2, dtype=jnp.int32)] + chunk_shapes(cot_cuts[:1]),
-        flops=4 * slots * local * width,
+        3,
     )
     cots = [exchanged(first_cots)]
     cots_across = [swapped(cots[0], "side")]
+
+    (packed,) = call(
+        pack_body,
+        "pack",
+        [whole(w_gate), whole(w_up), whole(w_down)],
+        [shape_of(3 * hidden, width)],
+        3,
+    )
+    other_weights = swapped(packed, "core")
 
     mixed, normed = call(
         attend_body,
@@ -321,15 +346,15 @@
             whole(mod_shift),
         ],
         [shape_of(local, width, dtype=jnp.float32), shape_of(local, width)],
-        flops=4 * local * HEADS * HD * width,
+        60,
     )
     placed = call(
         functools.partial(place_body, capacity, [first for first, _ in row_cuts]),
         "place",
         [whole(pos), whole(normed)],
         chunk_shapes(row_cuts),
-        flops=2 * slots * local * width,
-        after=cots,
+        3,
+        after=cots + [other_weights],
     )
     rows = [exchanged(value) for value in placed]
     rows_across = [swapped(value, "side") for value in rows]
@@ -340,15 +365,18 @@
             "late_slots",
             [whole(pos), whole(gate_rows), whole(out_grad[0])],
             [shape_of(blocks, count, width)],
-            flops=4 * slots * local * width,
-            after=rows,
+            3,
+            after=rows + cots_across[:1],
         )
         cots.append(exchanged(late_cots))
         cots_across.append(swapped(cots[-1], "side"))
 
-    pairs = [[weight, swapped(weight, "core")] for weight in (w_gate, w_up, w_down)]
-    gate_pres, up_pres, returned = [], [], []
-    after = cots_across[:1]
+    pairs = []
+    for n, weight in enumerate((w_gate, w_up, w_down)):
+        second = (other_weights, pl.ds(n * hidden, hidden), pl.ds(hidden, hidden))
+        pairs.append(([(weight, None, pl.ds(0, hidden)), second], (2 * hidden, width)))
+    gate_pres, up_pres, partials = [], [], []
+    after = []
     for (_, count), own, across in zip(row_cuts, rows, rows_across):
         half = blocks * count
         pre = shape_of(2 * hidden, 2 * half, dtype=jnp.float32)
@@ -356,21 +384,28 @@
             forward_body,
             "forward",
             [([(own, None, 0), (across, None, 1)], (2,) + own.shape)]
-            + [rows_of(pair) for pair in pairs],
+            + pairs,
             [shape_of(half, width)] * 2 + [pre] * 2,
-            flops=24 * half * hidden * width,
+            7,
             after=after,
         )
         after = [keep]
         gate_pres.append(gate_pre)
         up_pres.append(up_pre)
+        partials.append((keep, swapped(send, "side"), count))
+
+    def summed(keep, other, count, after):
         (sums,) = call(
             add_body,
             "add",
-            [whole(keep), whole(swapped(send, "side"))],
+            [whole(keep), whole(other)],
             [shape_of(blocks, count, width)],
+            2,
+            after=after,
         )
-        returned.append(exchanged(sums))
+        return sums
+
+    totals = [summed(*partial, []) for partial in partials[:-1]]
 
     total_rows = 2 * slots
     row_pieces, cot_pieces, pre_pieces, line = [], [], [[], []], 0
@@ -389,24 +424,28 @@
             target = (slice(None), pl.ds(line, 2 * blocks * count))
             pieces.append((pres[n], None, target))
         line += 2 * blocks * count
-    grads = call(
+    *kept, sent = call(
         backward_body,
         "backward",
         [
             (cot_pieces, (total_rows, width)),
-            rows_of(pairs[2]),
+            pairs[2],
             (pre_pieces[0], (2 * hidden, total_rows)),
             (pre_pieces[1], (2 * hidden, total_rows)),
             (row_pieces, (total_rows, width)),
         ],
-        [shape_of(hidden, width, dtype=jnp.float32)] * 3 + [shape_of(hidden, width)] * 3,
-        flops=16 * total_rows * hidden * width,
-    )
-    operands = []
-    for kept, sent in zip(grads[:3], grads[3:]):
-        operands += [whole(kept), whole(swapped(sent, "core"))]
+        [shape_of(hidden, width, dtype=jnp.float32)] * 3 + [shape_of(3 * hidden, width)],
+        40,
+        after=totals,
+    )
+    totals.append(summed(*partials[-1], kept[:1] if totals else []))
+    returned = [exchanged(total) for total in totals]
     grad_gate, grad_up, grad_down = call(
-        add_body, "finish", operands, [shape_of(hidden, width)] * 3
+        finish_body,
+        "finish",
+        [whole(value) for value in kept] + [whole(swapped(sent, "core"))],
+        [shape_of(hidden, width)] * 3,
+        5,
     )
 
     returned_pieces = []
@@ -422,7 +461,8 @@
             whole(mixed),
         ],
         [shape_of(local, width)],
-        flops=4 * slots * local * width,
+        3,
+        after=[grad_gate],
     )
     return (layer_out[None], grad_gate, grad_up, grad_down)
 

time: 216 us -> 252 us (1.17)
  blocking collectives: 30.9 us -> 52 us
  waiting for transfers between devices: 83.6 us -> 104 us
  starting transfers between devices: 36.7 us -> 31.1 us
  local copies, waits for them, and re-layouts: 7.61 us -> 3.2 us
  Pallas kernels: 55.5 us -> 59.8 us
    all_to_all x1 -> x2, blocking collectives: 30.9 us -> 52 us  [exchanged(): lax.all_to_all(shaped, ('ctx', 'group'), split_axis=0, concat_axis=0, til...]
    ppermute x12 -> x8, waiting for transfers between devices: 54.8 us -> 70.7 us  [swapped(): lax.ppermute(value, axis, [(n, n ^ 1) for n in range(lax.axis_size(axis))])]
    all_to_all x5 -> x4, waiting for transfers between devices: 11.7 us -> 19.7 us  [exchanged(): lax.all_to_all(shaped, ('ctx', 'group'), split_axis=0, concat_axis=0, til...]
    all_to_all x5 -> x4, starting transfers between devices: 26.2 us -> 21.5 us  [exchanged(): lax.all_to_all(shaped, ('ctx', 'group'), split_axis=0, concat_axis=0, til...]
    unnamed x36 -> x14, local copies, waits for them, and re-layouts: 7.61 us -> 3.2 us
    pallas_call x11 -> x12, Pallas kernels: 55.5 us -> 59.8 us  [call(): pl.pallas_call(kernel, out_shape=tuple(outs), in_specs=[ANY] * n_in, out_...]
    ppermute x2, waiting for transfers between devices: 17.1 us -> 13.5 us  [turned(): lax.ppermute(value, 'ctx', [(n, (n + step) % size) for n in range(size)])]
    ppermute x12 -> x8, starting transfers between devices: 8.42 us -> 7.46 us  [swapped(): lax.ppermute(value, axis, [(n, n ^ 1) for n in range(lax.axis_size(axis))])]
  transfers between devices with their start and end apart: 19 -> 14, of which waited for: 10 -> 9; matrix products, arithmetic and copies ran while one was open for 0% -> 0% of each run, Pallas kernels for 21% -> 14%
where the time goes in v5:
time: 252 us; the launch traced here: 251 us
  waiting for transfers between devices  104 us (41%)
  Pallas kernels  59.8 us (24%)
  blocking collectives  52 us (21%)
  starting transfers between devices  31.1 us (12%)
  local copies, waits for them, and re-layouts  3.2 us (1%)
    ppermute x8, waiting for transfers between devices, swapped(): lax.ppermute(value, axis, [(n, n ^ 1) for n in range(lax.axis_size(axis))])  70.7 us
    pallas_call x12, Pallas kernels, call(): pl.pallas_call(kernel, out_shape=tuple(outs), in_specs=[ANY] * n_in, out_...  59.8 us
    all_to_all x2, blocking collectives, exchanged(): lax.all_to_all(shaped, ('ctx', 'group'), split_axis=0, concat_axis=0, til...  52 us
    all_to_all x4, starting transfers between devices, exchanged(): lax.all_to_all(shaped, ('ctx', 'group'), split_axis=0, concat_axis=0, til...  21.5 us
    all_to_all x4, waiting for transfers between devices, exchanged(): lax.all_to_all(shaped, ('ctx', 'group'), split_axis=0, concat_axis=0, til...  19.7 us
    ppermute x2, waiting for transfers between devices, turned(): lax.ppermute(value, 'ctx', [(n, (n + step) % size) for n in range(size)])  13.5 us
    ppermute x8, starting transfers between devices, swapped(): lax.ppermute(value, axis, [(n, n ^ 1) for n in range(lax.axis_size(axis))])  7.46 us
  transfers between devices with their start and end apart: 14, of which 9 were waited for; matrix products, arithmetic and copies ran while one was open for 0% of the time, Pallas kernels for 14%

profile of v5, /device:TPU:0, one launch (start us, length us, event | category | flops | bytes accessed | tf_op | source)
XLA Modules:
  0.0 250.9 jit_solution(2289888062074425755)
XLA Ops:
  3.2 7.3 %all-to-all-start = ((bf16[8,16,2048]{2,1,0:T(8,128)(2,1)}), bf16[8,16,2048]{2,1,0:T(8,128)(2,1)S(1)}, u32[]{:S(2)}, u32[]{:S(2)}) async-start(bf16[8,16,2048]{2,1,0:T(8,128)(2,1)} %get-tuple-element.27), calls=%async_computation | async-start | bytes 1048576 | tf_op jit(solution)/shard_map/all_to_all | solution.py:302
  12.6 3.6 %pack.1 = bf16[768,2048]{1,0:T(8,128)(2,1)} custom-call(bf16[256,2048]{1,0:T(8,128)(2,1)} %refs_2_.5, bf16[256,2048]{1,0:T(8,128)(2,1)} %refs_4_.4, bf16[256,2048]{1,0:T(8,128)(2,1)} %refs_4_.5), custom_call_target="tpu_custom_call" | custom-call | flops 3449999872 | tf_op jit(solution)/shard_map/pack/pallas_call | solution.py:70
  16.3 8.6 %collective-permute-done.refs_2_ = bf16[128,1024]{1,0:T(8,128)(2,1)} collective-permute-done((bf16[128,1024]{1,0:T(8,128)(2,1)S(1)}, bf16[128,1024]{1,0:T(8,128)(2,1)}, u32[]{:S(2)}, u32[]{:S(2)}) %collective-permute-start) | collective-permute-done | bytes 262176 | tf_op jit(solution)/shard_map/ppermute | solution.py:307
  25.0 4.9 %collective-permute-done.1.refs_4_ = bf16[128,1024]{1,0:T(8,128)(2,1)} collective-permute-done((bf16[128,1024]{1,0:T(8,128)(2,1)}, bf16[128,1024]{1,0:T(8,128)(2,1)}, u32[]{:S(2)}, u32[]{:S(2)}) %collective-permute-start.1) | collective-permute-done | bytes 262176 | tf_op jit(solution)/shard_map/ppermute | solution.py:307
  29.8 4.8 %attend.1 = (f32[128,2048]{1,0:T(8,128)}, bf16[128,2048]{1,0:T(8,128)(2,1)}) custom-call(bf16[128,1024]{1,0:T(8,128)(2,1)} %bitcast.15, bf16[128,1024]{1,0:T(8,128)(2,1)} %bitcast.16, bf16[128,1024]{1,0:T(8,128)(2,1)} %collective-permute-done.refs_2_, bf16[128,1024]{1,0:T(8,128)(2,1)} %bitcast.19, bf16[128,1024]{1,0:T(8,128)(2,1)} %collective-permute-done.1.refs_4_, ...), custom_call_target="tpu_custom_call" | custom-call | flops 69000003584 | tf_op jit(solution)/shard_map/attend/pallas_call | solution.py:70
  35.5 2.8 %place.1 = (bf16[8,32,2048]{2,1,0:T(8,128)(2,1)}, bf16[8,16,2048]{2,1,0:T(8,128)(2,1)}) custom-call(s32[128,2]{1,0:T(8,128)} %get-tuple-element.25.refs_0_, bf16[128,2048]{1,0:T(8,128)(2,1)} %get-tuple-element.26.refs_1_, bf16[8,16,2048]{2,1,0:T(8,128)(2,1)} %copy-done, bf16[768,2048]{1,0:T(8,128)(2,1)} %collective-permute-done.2.refs_3_.refs_5_), custom_call_target="tpu_custom_call" | custom-call | flops 3449999872 | tf_op jit(solution)/shard_map/place/pallas_call | solution.py:70
  38.3 31.1 %all_to_all.30.refs_0_.refs_3_.refs_10_ = bf16[8,32,2048]{2,1,0:T(8,128)(2,1)} all-to-all(bf16[8,32,2048]{2,1,0:T(8,128)(2,1)} %get-tuple-element.28), channel_id=1, replica_groups=mesh['ctx'=2,'group'=4,'side'=2,'core'=2] {'ctx','group'}, dimensions={0} | all-to-all | bytes 2097152 | tf_op jit(solution)/shard_map/all_to_all | solution.py:302
  69.5 4.1 %all-to-all-start.3 = ((bf16[8,16,2048]{2,1,0:T(8,128)(2,1)}), bf16[8,16,2048]{2,1,0:T(8,128)(2,1)}, u32[]{:S(2)}, u32[]{:S(2)}) async-start(bf16[8,16,2048]{2,1,0:T(8,128)(2,1)} %get-tuple-element.31), calls=%async_computation.3 | async-start | bytes 1048576 | tf_op jit(solution)/shard_map/all_to_all | solution.py:302
  75.7 12.8 %collective-permute-done.7.refs_5_.refs_2_ = bf16[8,16,2048]{2,1,0:T(8,128)(2,1)S(1)} collective-permute-done((bf16[8,16,2048]{2,1,0:T(8,128)(2,1)S(1)}, bf16[8,16,2048]{2,1,0:T(8,128)(2,1)S(1)}, u32[]{:S(2)}, u32[]{:S(2)}) %collective-permute-start.7) | collective-permute-done | bytes 524320 | tf_op jit(solution)/shard_map/ppermute | solution.py:298
  89.3 2.8 %late_slots.1 = bf16[8,32,2048]{2,1,0:T(8,128)(2,1)} custom-call(s32[128,2]{1,0:T(8,128)} %get-tuple-element.25.refs_0_, f32[2,128]{1,0:T(2,128)} %bitcast.22, bf16[128,2048]{1,0:T(8,128)(2,1)} %bitcast.14, bf16[8,32,2048]{2,1,0:T(8,128)(2,1)} %all_to_all.30.refs_0_.refs_3_.refs_10_, bf16[8,16,2048]{2,1,0:T(8,128)(2,1)} %all-to-all-done.3.refs_0_.refs_4_.refs_12_, ...), custom_call_target="tpu_custom_call" | custom-call | flops 3449999872 | tf_op jit(solution)/shard_map/late_slots/pallas_call | solution.py:70
  92.2 5.8 %all-to-all-start.4 = ((bf16[8,32,2048]{2,1,0:T(8,128)(2,1)}), bf16[8,32,2048]{2,1,0:T(8,128)(2,1)}, u32[]{:S(2)}, u32[]{:S(2)}) async-start(bf16[8,32,2048]{2,1,0:T(8,128)(2,1)} %late_slots.1), calls=%async_computation.4 | async-start | bytes 2097152 | tf_op jit(solution)/shard_map/all_to_all | solution.py:302
  99.5 11.6 %collective-permute-done.3.refs_1_.refs_11_ = bf16[8,32,2048]{2,1,0:T(8,128)(2,1)} collective-permute-done((bf16[8,32,2048]{2,1,0:T(8,128)(2,1)}, bf16[8,32,2048]{2,1,0:T(8,128)(2,1)}, u32[]{:S(2)}, u32[]{:S(2)}) %collective-permute-start.3) | collective-permute-done | bytes 1048608 | tf_op jit(solution)/shard_map/ppermute | solution.py:298
  111.1 7.7 %forward.2 = (bf16[256,2048]{1,0:T(8,128)(2,1)}, bf16[256,2048]{1,0:T(8,128)(2,1)}, f32[512,512]{1,0:T(8,128)}, f32[512,512]{1,0:T(8,128)}) custom-call(bf16[8,32,2048]{2,1,0:T(8,128)(2,1)} %all_to_all.30.refs_0_.refs_3_.refs_10_, bf16[8,32,2048]{2,1,0:T(8,128)(2,1)} %collective-permute-done.3.refs_1_.refs_11_, bf16[256,2048]{1,0:T(8,128)(2,1)} %refs_2_.5, ...), custom_call_target="tpu_custom_call" | custom-call | flops 8049999872 | tf_op jit(solution)/shard_map/forward/pallas_call | solution.py:70
  123.1 6.3 %forward.3 = (bf16[128,2048]{1,0:T(8,128)(2,1)}, bf16[128,2048]{1,0:T(8,128)(2,1)}, f32[512,256]{1,0:T(8,128)}, f32[512,256]{1,0:T(8,128)}) custom-call(bf16[8,16,2048]{2,1,0:T(8,128)(2,1)} %all-to-all-done.3.refs_0_.refs_4_.refs_12_, bf16[8,16,2048]{2,1,0:T(8,128)(2,1)} %copy-done.3, bf16[256,2048]{1,0:T(8,128)(2,1)} %refs_2_.5, ...), custom_call_target="tpu_custom_call" | custom-call | flops 8049999872 | tf_op jit(solution)/shard_map/forward/pallas_call | solution.py:70
  129.4 15.9 %collective-permute-done.4.refs_1_ = bf16[256,2048]{1,0:T(8,128)(2,1)} collective-permute-done((bf16[256,2048]{1,0:T(8,128)(2,1)}, bf16[256,2048]{1,0:T(8,128)(2,1)}, u32[]{:S(2)}, u32[]{:S(2)}) %collective-permute-start.4) | collective-permute-done | bytes 1048608 | tf_op jit(solution)/shard_map/ppermute | solution.py:298
  145.3 2.7 %add.2.refs_14_ = bf16[8,32,2048]{2,1,0:T(8,128)(2,1)} custom-call(bf16[256,2048]{1,0:T(8,128)(2,1)} %get-tuple-element.29.refs_0_.refs_6_, bf16[256,2048]{1,0:T(8,128)(2,1)} %collective-permute-done.4.refs_1_), custom_call_target="tpu_custom_call" | custom-call | flops 2300000000 | tf_op jit(solution)/shard_map/add/pallas_call | solution.py:70
  148.0 16.3 %collective-permute-done.8.refs_3_ = bf16[8,32,2048]{2,1,0:T(8,128)(2,1)} collective-permute-done((bf16[8,32,2048]{2,1,0:T(8,128)(2,1)}, bf16[8,32,2048]{2,1,0:T(8,128)(2,1)}, u32[]{:S(2)}, u32[]{:S(2)}) %collective-permute-start.8) | collective-permute-done | bytes 1048608 | tf_op jit(solution)/shard_map/ppermute | solution.py:298
  164.3 15.2 %backward.1 = (f32[256,2048]{1,0:T(8,128)}, f32[256,2048]{1,0:T(8,128)}, f32[256,2048]{1,0:T(8,128)}, bf16[768,2048]{1,0:T(8,128)(2,1)}) custom-call(bf16[8,16,2048]{2,1,0:T(8,128)(2,1)} %copy-done, bf16[8,32,2048]{2,1,0:T(8,128)(2,1)} %all-to-all-done.4.refs_1_, bf16[8,16,2048]{2,1,0:T(8,128)(2,1)} %copy-done.2, ...), custom_call_target="tpu_custom_call" | custom-call | flops 46000001024 | tf_op jit(solution)/shard_map/backward/pallas_call | solution.py:70
  181.2 12.8 %collective-permute-done.6.refs_1_ = bf16[128,2048]{1,0:T(8,128)(2,1)S(1)} collective-permute-done((bf16[128,2048]{1,0:T(8,128)(2,1)S(1)}, bf16[128,2048]{1,0:T(8,128)(2,1)S(1)}, u32[]{:S(2)}, u32[]{:S(2)}) %collective-permute-start.6) | collective-permute-done | bytes 524320 | tf_op jit(solution)/shard_map/ppermute | solution.py:298
  196.9 20.9 %all_to_all.31.refs_3_ = bf16[8,16,2048]{2,1,0:T(8,128)(2,1)} all-to-all(bf16[8,16,2048]{2,1,0:T(8,128)(2,1)} %add.3), channel_id=1, replica_groups=mesh['ctx'=2,'group'=4,'side'=2,'core'=2] {'ctx','group'}, dimensions={0} | all-to-all | bytes 1048576 | tf_op jit(solution)/shard_map/all_to_all | solution.py:302
  217.7 4.2 %all-to-all-start.2 = ((bf16[8,32,2048]{2,1,0:T(8,128)(2,1)}), bf16[8,32,2048]{2,1,0:T(8,128)(2,1)}, u32[]{:S(2)}, u32[]{:S(2)}) async-start(bf16[8,32,2048]{2,1,0:T(8,128)(2,1)} %add.2.refs_14_), calls=%async_computation.2 | async-start | bytes 2097152 | tf_op jit(solution)/shard_map/all_to_all | solution.py:302
  222.0 5.8 %finish.1 = (bf16[256,2048]{1,0:T(8,128)(2,1)}, bf16[256,2048]{1,0:T(8,128)(2,1)}, bf16[256,2048]{1,0:T(8,128)(2,1)}) custom-call(f32[256,2048]{1,0:T(8,128)} %get-tuple-element.38.refs_2_.refs_0_, f32[256,2048]{1,0:T(8,128)} %get-tuple-element.40.refs_1_, f32[256,2048]{1,0:T(8,128)} %get-tuple-element.41.refs_2_, ...), custom_call_target="tpu_custom_call" | custom-call | flops 5750000128 | tf_op jit(solution)/shard_map/finish/pallas_call | solution.py:70
  227.8 19.7 %all-to-all-done.2.refs_2_ = bf16[8,32,2048]{2,1,0:T(8,128)(2,1)} async-done(((bf16[8,32,2048]{2,1,0:T(8,128)(2,1)}), bf16[8,32,2048]{2,1,0:T(8,128)(2,1)}, u32[]{:S(2)}, u32[]{:S(2)}) %all-to-all-start.2) | async-done | bytes 1048608 | tf_op jit(solution)/shard_map/all_to_all | solution.py:302
  247.5 3.3 %combine.1 = bf16[128,2048]{1,0:T(8,128)(2,1)} custom-call(s32[128,2]{1,0:T(8,128)} %get-tuple-element.25.refs_0_, f32[2,128]{1,0:T(2,128)} %bitcast.23, bf16[8,32,2048]{2,1,0:T(8,128)(2,1)} %all-to-all-done.2.refs_2_, bf16[8,16,2048]{2,1,0:T(8,128)(2,1)} %all_to_all.31.refs_3_, f32[128,2048]{1,0:T(8,128)} %get-tuple-element.39.refs_4_, ...), custom_call_target="tpu_custom_call" | custom-call | flops 3449999872 | tf_op jit(solution)/shard_map/combine/pallas_call | solution.py:70
  (32 shorter events, 18.7 us)
Async XLA Ops:
  0.6 9.9 %copy-start.6 = (bf16[1,128,1024]{2,1,0:T(8,128)(2,1)S(1)}, bf16[1,128,1024]{2,1,0:T(8,128)(2,1)}, u32[]{:S(2)}) copy-start(bf16[1,128,1024]{2,1,0:T(8,128)(2,1)} %param.15) | copy-start | bytes 786436
  3.2 31.4 %all-to-all-start = ((bf16[8,16,2048]{2,1,0:T(8,128)(2,1)}), bf16[8,16,2048]{2,1,0:T(8,128)(2,1)S(1)}, u32[]{:S(2)}, u32[]{:S(2)}) async-start(bf16[8,16,2048]{2,1,0:T(8,128)(2,1)} %get-tuple-element.27), calls=%async_computation | async-start | bytes 1048576 | tf_op jit(solution)/shard_map/all_to_all | solution.py:302
  10.5 14.5 %collective-permute-start = (bf16[128,1024]{1,0:T(8,128)(2,1)S(1)}, bf16[128,1024]{1,0:T(8,128)(2,1)}, u32[]{:S(2)}, u32[]{:S(2)}) collective-permute-start(bf16[128,1024]{1,0:T(8,128)(2,1)S(1)} %bitcast.17), channel_id=1, source_target_pairs={{0,16},{16,0},{1,17},{17,1},{2,18},{18,2},{3,19},{19,3},{4,20},{20... | collective-permute-start | bytes 786440 | tf_op jit(solution)/shard_map/ppermute | solution.py:307
  12.5 17.3 %collective-permute-start.1 = (bf16[128,1024]{1,0:T(8,128)(2,1)}, bf16[128,1024]{1,0:T(8,128)(2,1)}, u32[]{:S(2)}, u32[]{:S(2)}) collective-permute-start(bf16[128,1024]{1,0:T(8,128)(2,1)} %bitcast.18), channel_id=1, source_target_pairs={{0,16},{16,0},{1,17},{17,1},{2,18},{18,2},{3,19},{19,3},{4,20},{20... | collective-permute-start | bytes 786440 | tf_op jit(solution)/shard_map/ppermute | solution.py:307
  16.2 18.4 %collective-permute-start.2 = (bf16[768,2048]{1,0:T(8,128)(2,1)}, bf16[768,2048]{1,0:T(8,128)(2,1)}, u32[]{:S(2)}, u32[]{:S(2)}) collective-permute-start(bf16[768,2048]{1,0:T(8,128)(2,1)} %pack.1), channel_id=1, source_target_pairs={{0,1},{1,0},{2,3},{3,2},{4,5},{5,4},{6,7},{7,6},{8,9},{9,8},{10,11... | collective-permute-start | bytes 9437192 | tf_op jit(solution)/shard_map/ppermute | solution.py:298
  34.7 0.8 copy-start
  38.3 35.3 %copy-start.1 = (bf16[8,16,2048]{2,1,0:T(8,128)(2,1)S(1)}, bf16[8,16,2048]{2,1,0:T(8,128)(2,1)}, u32[]{:S(2)}) copy-start(bf16[8,16,2048]{2,1,0:T(8,128)(2,1)} %copy-done) | copy-start | bytes 1572868
  69.5 19.1 %all-to-all-start.3 = ((bf16[8,16,2048]{2,1,0:T(8,128)(2,1)}), bf16[8,16,2048]{2,1,0:T(8,128)(2,1)}, u32[]{:S(2)}, u32[]{:S(2)}) async-start(bf16[8,16,2048]{2,1,0:T(8,128)(2,1)} %get-tuple-element.31), calls=%async_computation.3 | async-start | bytes 1048576 | tf_op jit(solution)/shard_map/all_to_all | solution.py:302
  73.6 14.9 %collective-permute-start.7 = (bf16[8,16,2048]{2,1,0:T(8,128)(2,1)S(1)}, bf16[8,16,2048]{2,1,0:T(8,128)(2,1)S(1)}, u32[]{:S(2)}, u32[]{:S(2)}) collective-permute-start(bf16[8,16,2048]{2,1,0:T(8,128)(2,1)S(1)} %copy-done.1), channel_id=1, source_target_pairs={{0,2},{2,0},{1,3},{3,1},{4,6},{6,4},{5,7},{7,5},{8,10},{10,8},{9,1... | collective-permute-start | bytes 1572872 | tf_op jit(solution)/shard_map/ppermute | solution.py:298
  75.2 35.9 %collective-permute-start.3 = (bf16[8,32,2048]{2,1,0:T(8,128)(2,1)}, bf16[8,32,2048]{2,1,0:T(8,128)(2,1)}, u32[]{:S(2)}, u32[]{:S(2)}) collective-permute-start(bf16[8,32,2048]{2,1,0:T(8,128)(2,1)} %all_to_all.30.refs_0_.refs_3_.refs_10_), channel_id=1, source_target_pairs={{0,2},{2,0},{1,3},{3,1},{4,6},{6,4},{5,7},{7,5},{8,10},{10,8},{9,1... | collective-permute-start | bytes 3145736 | tf_op jit(solution)/shard_map/ppermute | solution.py:298
  88.5 0.8 copy-start.2
  92.2 28.2 %all-to-all-start.4 = ((bf16[8,32,2048]{2,1,0:T(8,128)(2,1)}), bf16[8,32,2048]{2,1,0:T(8,128)(2,1)}, u32[]{:S(2)}, u32[]{:S(2)}) async-start(bf16[8,32,2048]{2,1,0:T(8,128)(2,1)} %late_slots.1), calls=%async_computation.4 | async-start | bytes 2097152 | tf_op jit(solution)/shard_map/all_to_all | solution.py:302
  98.0 24.2 %collective-permute-start.5 = (bf16[8,16,2048]{2,1,0:T(8,128)(2,1)}, bf16[8,16,2048]{2,1,0:T(8,128)(2,1)S(1)}, u32[]{:S(2)}, u32[]{:S(2)}) collective-permute-start(bf16[8,16,2048]{2,1,0:T(8,128)(2,1)} %all-to-all-done.3.refs_0_.refs_4_.refs_12_), channel_id=1, source_target_pairs={{0,2},{2,0},{1,3},{3,1},{4,6},{6,4},{5,7},{7,5},{8,10},{10,8},{9,1... | collective-permute-start | bytes 1572872 | tf_op jit(solution)/shard_map/ppermute | solution.py:298
  118.8 26.5 %collective-permute-start.4 = (bf16[256,2048]{1,0:T(8,128)(2,1)}, bf16[256,2048]{1,0:T(8,128)(2,1)}, u32[]{:S(2)}, u32[]{:S(2)}) collective-permute-start(bf16[256,2048]{1,0:T(8,128)(2,1)} %get-tuple-element.30), channel_id=1, source_target_pairs={{0,2},{2,0},{1,3},{3,1},{4,6},{6,4},{5,7},{7,5},{8,10},{10,8},{9,1... | collective-permute-start | bytes 3145736 | tf_op jit(solution)/shard_map/ppermute | solution.py:298
  120.4 43.9 %collective-permute-start.8 = (bf16[8,32,2048]{2,1,0:T(8,128)(2,1)}, bf16[8,32,2048]{2,1,0:T(8,128)(2,1)}, u32[]{:S(2)}, u32[]{:S(2)}) collective-permute-start(bf16[8,32,2048]{2,1,0:T(8,128)(2,1)} %all-to-all-done.4.refs_1_), channel_id=1, source_target_pairs={{0,2},{2,0},{1,3},{3,1},{4,6},{6,4},{5,7},{7,5},{8,10},{10,8},{9,1... | collective-permute-start | bytes 3145736 | tf_op jit(solution)/shard_map/ppermute | solution.py:298
  122.2 0.8 copy-start.3
  164.3 15.3 %copy-start.4 = (bf16[128,2048]{1,0:T(8,128)(2,1)S(1)}, bf16[128,2048]{1,0:T(8,128)(2,1)}, u32[]{:S(2)}) copy-start(bf16[128,2048]{1,0:T(8,128)(2,1)} %get-tuple-element.33) | copy-start | bytes 1572868
  179.5 42.4 %collective-permute-start.9 = (bf16[768,2048]{1,0:T(8,128)(2,1)}, bf16[768,2048]{1,0:T(8,128)(2,1)}, u32[]{:S(2)}, u32[]{:S(2)}) collective-permute-start(bf16[768,2048]{1,0:T(8,128)(2,1)} %get-tuple-element.42), channel_id=1, source_target_pairs={{0,1},{1,0},{2,3},{3,2},{4,5},{5,4},{6,7},{7,6},{8,9},{9,8},{10,11... | collective-permute-start | bytes 9437192 | tf_op jit(solution)/shard_map/ppermute | solution.py:298
  179.6 14.3 %collective-permute-start.6 = (bf16[128,2048]{1,0:T(8,128)(2,1)S(1)}, bf16[128,2048]{1,0:T(8,128)(2,1)S(1)}, u32[]{:S(2)}, u32[]{:S(2)}) collective-permute-start(bf16[128,2048]{1,0:T(8,128)(2,1)S(1)} %copy-done.4), channel_id=1, source_target_pairs={{0,2},{2,0},{1,3},{3,1},{4,6},{6,4},{5,7},{7,5},{8,10},{10,8},{9,1... | collective-permute-start | bytes 1572872 | tf_op jit(solution)/shard_map/ppermute | solution.py:298
  194.0 0.8 copy-start.5
  217.7 29.8 %all-to-all-start.2 = ((bf16[8,32,2048]{2,1,0:T(8,128)(2,1)}), bf16[8,32,2048]{2,1,0:T(8,128)(2,1)}, u32[]{:S(2)}, u32[]{:S(2)}) async-start(bf16[8,32,2048]{2,1,0:T(8,128)(2,1)} %add.2.refs_14_), calls=%async_computation.2 | async-start | bytes 2097152 | tf_op jit(solution)/shard_map/all_to_all | solution.py:302

commit v6 on v5

--- a/solution.py
+++ b/solution.py
@@ -319,7 +319,7 @@
         "slots",
         [whole(ids_rows), whole(gate_rows), whole(out_grad[0])],
         [shape_of(local, 2, dtype=jnp.int32)] + chunk_shapes(cot_cuts[:1]),
-        3,
+        0.35,
     )
     cots = [exchanged(first_cots)]
     cots_across = [swapped(cots[0], "side")]
@@ -329,7 +329,7 @@
         "pack",
         [whole(w_gate), whole(w_up), whole(w_down)],
         [shape_of(3 * hidden, width)],
-        3,
+        0,
     )
     other_weights = swapped(packed, "core")
 
@@ -346,14 +346,14 @@
             whole(mod_shift),
         ],
         [shape_of(local, width, dtype=jnp.float32), shape_of(local, width)],
-        60,
+        0.93,
     )
     placed = call(
         functools.partial(place_body, capacity, [first for first, _ in row_cuts]),
         "place",
         [whole(pos), whole(normed)],
         chunk_shapes(row_cuts),
-        3,
+        0.2,
         after=cots + [other_weights],
     )
     rows = [exchanged(value) for value in placed]
@@ -365,8 +365,8 @@
             "late_slots",
             [whole(pos), whole(gate_rows), whole(out_grad[0])],
             [shape_of(blocks, count, width)],
-            3,
-            after=rows + cots_across[:1],
+            0.35,
+            after=rows,
         )
         cots.append(exchanged(late_cots))
         cots_across.append(swapped(cots[-1], "side"))
@@ -386,7 +386,7 @@
             [([(own, None, 0), (across, None, 1)], (2,) + own.shape)]
             + pairs,
             [shape_of(half, width)] * 2 + [pre] * 2,
-            7,
+            24e-6 * half * hidden * width / 1150,
             after=after,
         )
         after = [keep]
@@ -394,18 +394,17 @@
         up_pres.append(up_pre)
         partials.append((keep, swapped(send, "side"), count))
 
-    def summed(keep, other, count, after):
+    def summed(keep, other, count):
         (sums,) = call(
             add_body,
             "add",
             [whole(keep), whole(other)],
             [shape_of(blocks, count, width)],
-            2,
-            after=after,
+            0,
         )
         return sums
 
-    totals = [summed(*partial, []) for partial in partials[:-1]]
+    returned = [exchanged(summed(*partial)) for partial in partials]
 
     total_rows = 2 * slots
     row_pieces, cot_pieces, pre_pieces, line = [], [], [[], []], 0
@@ -435,17 +434,14 @@
             (row_pieces, (total_rows, width)),
         ],
         [shape_of(hidden, width, dtype=jnp.float32)] * 3 + [shape_of(3 * hidden, width)],
-        40,
-        after=totals,
-    )
-    totals.append(summed(*partials[-1], kept[:1] if totals else []))
-    returned = [exchanged(total) for total in totals]
+        16e-6 * total_rows * hidden * width / 1150,
+    )
     grad_gate, grad_up, grad_down = call(
         finish_body,
         "finish",
         [whole(value) for value in kept] + [whole(swapped(sent, "core"))],
         [shape_of(hidden, width)] * 3,
-        5,
+        0,
     )
 
     returned_pieces = []
@@ -461,8 +457,7 @@
             whole(mixed),
         ],
         [shape_of(local, width)],
-        3,
-        after=[grad_gate],
+        0.35,
     )
     return (layer_out[None], grad_gate, grad_up, grad_down)
 

time: 252 us -> 259 us (1.028)
  blocking collectives: 52 us -> 81.1 us
  waiting for transfers between devices: 104 us -> 88.1 us
  starting transfers between devices: 31.1 us -> 25.7 us
    all_to_all x2 -> x3, blocking collectives: 52 us -> 81.1 us  [exchanged(): lax.all_to_all(shaped, ('ctx', 'group'), split_axis=0, concat_axis=0, til...]
    ppermute x8, waiting for transfers between devices: 70.7 us -> 47.7 us  [swapped(): lax.ppermute(value, axis, [(n, n ^ 1) for n in range(lax.axis_size(axis))])]
    all_to_all x4 -> x3, starting transfers between devices: 21.5 us -> 14.8 us  [exchanged(): lax.all_to_all(shaped, ('ctx', 'group'), split_axis=0, concat_axis=0, til...]
    all_to_all x4 -> x3, waiting for transfers between devices: 19.7 us -> 23.4 us  [exchanged(): lax.all_to_all(shaped, ('ctx', 'group'), split_axis=0, concat_axis=0, til...]
    ppermute x2, waiting for transfers between devices: 13.5 us -> 17.1 us  [turned(): lax.ppermute(value, 'ctx', [(n, (n + step) % size) for n in range(size)])]
  transfers between devices with their start and end apart: 14 -> 13, of which waited for: 9 -> 6; matrix products, arithmetic and copies ran while one was open for 0% -> 0% of each run, Pallas kernels for 14% -> 17%
where the time goes in v6:
time: 259 us
  waiting for transfers between devices  88.1 us (34%)
  blocking collectives  81.1 us (31%)
  Pallas kernels  59.8 us (23%)
  starting transfers between devices  25.7 us (10%)
  local copies, waits for them, and re-layouts  3 us (1%)
    all_to_all x3, blocking collectives, exchanged(): lax.all_to_all(shaped, ('ctx', 'group'), split_axis=0, concat_axis=0, til...  81.1 us
    pallas_call x12, Pallas kernels, call(): pl.pallas_call(kernel, out_shape=tuple(outs), in_specs=[ANY] * n_in, out_...  59.8 us
    ppermute x8, waiting for transfers between devices, swapped(): lax.ppermute(value, axis, [(n, n ^ 1) for n in range(lax.axis_size(axis))])  47.7 us
    all_to_all x3, waiting for transfers between devices, exchanged(): lax.all_to_all(shaped, ('ctx', 'group'), split_axis=0, concat_axis=0, til...  23.4 us
    ppermute x2, waiting for transfers between devices, turned(): lax.ppermute(value, 'ctx', [(n, (n + step) % size) for n in range(size)])  17.1 us
    all_to_all x3, starting transfers between devices, exchanged(): lax.all_to_all(shaped, ('ctx', 'group'), split_axis=0, concat_axis=0, til...  14.8 us
    ppermute x8, starting transfers between devices, swapped(): lax.ppermute(value, axis, [(n, n ^ 1) for n in range(lax.axis_size(axis))])  8.77 us
  transfers between devices with their start and end apart: 13, of which 6 were waited for; matrix products, arithmetic and copies ran while one was open for 0% of the time, Pallas kernels for 17%

profile of v6, /device:TPU:0, one launch (start us, length us, event | category | flops | bytes accessed | tf_op | source)
XLA Modules:
  0.0 258.7 jit_solution(5252266893096299674)
XLA Ops:
  0.6 3.6 %pack.1 = bf16[768,2048]{1,0:T(8,128)(2,1)} custom-call(bf16[256,2048]{1,0:T(8,128)(2,1)} %refs_2_.5, bf16[256,2048]{1,0:T(8,128)(2,1)} %refs_4_.4, bf16[256,2048]{1,0:T(8,128)(2,1)} %refs_4_.5), custom_call_target="tpu_custom_call" | custom-call | tf_op jit(solution)/shard_map/pack/pallas_call | solution.py:70
  4.8 2.5 slots.1
  7.3 6.9 %all-to-all-start = ((bf16[8,16,2048]{2,1,0:T(8,128)(2,1)}), bf16[8,16,2048]{2,1,0:T(8,128)(2,1)S(1)}, u32[]{:S(2)}, u32[]{:S(2)}) async-start(bf16[8,16,2048]{2,1,0:T(8,128)(2,1)} %get-tuple-element.27), calls=%async_computation | async-start | bytes 1048576 | tf_op jit(solution)/shard_map/all_to_all | solution.py:302
  16.3 10.4 %collective-permute-done.refs_2_ = bf16[128,1024]{1,0:T(8,128)(2,1)S(1)} collective-permute-done((bf16[128,1024]{1,0:T(8,128)(2,1)S(1)}, bf16[128,1024]{1,0:T(8,128)(2,1)S(1)}, u32[]{:S(2)}, u32[]{:S(2)}) %collective-permute-start) | collective-permute-done | bytes 262176 | tf_op jit(solution)/shard_map/ppermute | solution.py:307
  27.4 6.7 %collective-permute-done.1.refs_4_ = bf16[128,1024]{1,0:T(8,128)(2,1)S(1)} collective-permute-done((bf16[128,1024]{1,0:T(8,128)(2,1)}, bf16[128,1024]{1,0:T(8,128)(2,1)S(1)}, u32[]{:S(2)}, u32[]{:S(2)}) %collective-permute-start.1) | collective-permute-done | bytes 262176 | tf_op jit(solution)/shard_map/ppermute | solution.py:307
  34.8 4.8 %attend.1 = (f32[128,2048]{1,0:T(8,128)}, bf16[128,2048]{1,0:T(8,128)(2,1)}) custom-call(bf16[128,1024]{1,0:T(8,128)(2,1)} %bitcast.16, bf16[128,1024]{1,0:T(8,128)(2,1)} %bitcast.17, bf16[128,1024]{1,0:T(8,128)(2,1)} %copy-done.5, bf16[128,1024]{1,0:T(8,128)(2,1)} %bitcast.20, bf16[128,1024]{1,0:T(8,128)(2,1)} %copy-done.6, bf16[128,2048]{1,0:T(8,128)(2,1)} %bitcast.12, ...), custom_call_target="tpu_custom_call" | custom-call | flops 1069500032 | tf_op jit(solution)/shard_map/attend/pallas_call | solution.py:70
  40.4 2.9 %place.1 = (bf16[8,32,2048]{2,1,0:T(8,128)(2,1)}, bf16[8,16,2048]{2,1,0:T(8,128)(2,1)}) custom-call(s32[128,2]{1,0:T(8,128)} %get-tuple-element.25.refs_0_, bf16[128,2048]{1,0:T(8,128)(2,1)} %get-tuple-element.26.refs_1_, bf16[8,16,2048]{2,1,0:T(8,128)(2,1)} %copy-done.2, bf16[768,2048]{1,0:T(8,128)(2,1)} %collective-permute-done.2.refs_3_.refs_5_), custom_call_target="tpu_custom_call" | custom-call | flops 230000000 | tf_op jit(solution)/shard_map/place/pallas_call | solution.py:70
  43.2 20.2 %all_to_all.30.refs_0_.refs_4_.refs_12_ = bf16[8,16,2048]{2,1,0:T(8,128)(2,1)} all-to-all(bf16[8,16,2048]{2,1,0:T(8,128)(2,1)} %get-tuple-element.31), channel_id=1, replica_groups=mesh['ctx'=2,'group'=4,'side'=2,'core'=2] {'ctx','group'}, dimensions={0} | all-to-all | bytes 1048576 | tf_op jit(solution)/shard_map/all_to_all | solution.py:302
  63.5 29.9 %all_to_all.31.refs_0_.refs_3_.refs_10_ = bf16[8,32,2048]{2,1,0:T(8,128)(2,1)} all-to-all(bf16[8,32,2048]{2,1,0:T(8,128)(2,1)} %get-tuple-element.28), channel_id=1, replica_groups=mesh['ctx'=2,'group'=4,'side'=2,'core'=2] {'ctx','group'}, dimensions={0} | all-to-all | bytes 2097152 | tf_op jit(solution)/shard_map/all_to_all | solution.py:302
  93.4 2.9 %late_slots.1 = bf16[8,32,2048]{2,1,0:T(8,128)(2,1)} custom-call(s32[128,2]{1,0:T(8,128)} %get-tuple-element.25.refs_0_, f32[2,128]{1,0:T(2,128)} %bitcast.22, bf16[128,2048]{1,0:T(8,128)(2,1)} %bitcast.14, bf16[8,32,2048]{2,1,0:T(8,128)(2,1)} %all_to_all.31.refs_0_.refs_3_.refs_10_, bf16[8,16,2048]{2,1,0:T(8,128)(2,1)} %all_to_all.30.refs_0_.refs_4_.refs_12_), custom_call_target="tpu_custom_call" | custom-call | flops 402500000 | tf_op jit(solution)/shard_map/late_slots/pallas_call | solution.py:70
  96.3 4.4 %all-to-all-start.5 = ((bf16[8,32,2048]{2,1,0:T(8,128)(2,1)}), bf16[8,32,2048]{2,1,0:T(8,128)(2,1)}, u32[]{:S(2)}, u32[]{:S(2)}) async-start(bf16[8,32,2048]{2,1,0:T(8,128)(2,1)} %late_slots.1), calls=%async_computation.5 | async-start | bytes 2097152 | tf_op jit(solution)/shard_map/all_to_all | solution.py:302
  102.3 23.4 %all-to-all-done.5.refs_1_ = bf16[8,32,2048]{2,1,0:T(8,128)(2,1)} async-done(((bf16[8,32,2048]{2,1,0:T(8,128)(2,1)}), bf16[8,32,2048]{2,1,0:T(8,128)(2,1)}, u32[]{:S(2)}, u32[]{:S(2)}) %all-to-all-start.5) | async-done | bytes 1048608 | tf_op jit(solution)/shard_map/all_to_all | solution.py:302
  129.2 7.7 %forward.2 = (bf16[256,2048]{1,0:T(8,128)(2,1)}, bf16[256,2048]{1,0:T(8,128)(2,1)}, f32[512,512]{1,0:T(8,128)}, f32[512,512]{1,0:T(8,128)}) custom-call(bf16[8,32,2048]{2,1,0:T(8,128)(2,1)} %all_to_all.31.refs_0_.refs_3_.refs_10_, bf16[8,32,2048]{2,1,0:T(8,128)(2,1)} %collective-permute-done.3.refs_1_.refs_11_, bf16[256,2048]{1,0:T(8,128)(2,1)} %refs_2_.5, ...), custom_call_target="tpu_custom_call" | custom-call | flops 3221225472 | tf_op jit(solution)/shard_map/forward/pallas_call | solution.py:70
  136.9 26.4 %collective-permute-done.5.refs_1_.refs_13_ = bf16[8,16,2048]{2,1,0:T(8,128)(2,1)} collective-permute-done((bf16[8,16,2048]{2,1,0:T(8,128)(2,1)S(1)}, bf16[8,16,2048]{2,1,0:T(8,128)(2,1)}, u32[]{:S(2)}, u32[]{:S(2)}) %collective-permute-start.5) | collective-permute-done | bytes 524320 | tf_op jit(solution)/shard_map/ppermute | solution.py:298
  163.3 6.3 %forward.3 = (bf16[128,2048]{1,0:T(8,128)(2,1)}, bf16[128,2048]{1,0:T(8,128)(2,1)}, f32[512,256]{1,0:T(8,128)}, f32[512,256]{1,0:T(8,128)}) custom-call(bf16[8,16,2048]{2,1,0:T(8,128)(2,1)} %all_to_all.30.refs_0_.refs_4_.refs_12_, bf16[8,16,2048]{2,1,0:T(8,128)(2,1)} %collective-permute-done.5.refs_1_.refs_13_, bf16[256,2048]{1,0:T(8,128)(2,1)} %refs_2_.5, ...), custom_call_target="tpu_custom_call" | custom-call | flops 1610612736 | tf_op jit(solution)/shard_map/forward/pallas_call | solution.py:70
  171.2 3.3 %collective-permute-done.7.refs_2_ = bf16[8,16,2048]{2,1,0:T(8,128)(2,1)} collective-permute-done((bf16[8,16,2048]{2,1,0:T(8,128)(2,1)}, bf16[8,16,2048]{2,1,0:T(8,128)(2,1)}, u32[]{:S(2)}, u32[]{:S(2)}) %collective-permute-start.7) | collective-permute-done | bytes 524320 | tf_op jit(solution)/shard_map/ppermute | solution.py:298
  174.6 15.2 %backward.1 = (f32[256,2048]{1,0:T(8,128)}, f32[256,2048]{1,0:T(8,128)}, f32[256,2048]{1,0:T(8,128)}, bf16[768,2048]{1,0:T(8,128)(2,1)}) custom-call(bf16[8,16,2048]{2,1,0:T(8,128)(2,1)} %copy-done.2, bf16[8,32,2048]{2,1,0:T(8,128)(2,1)} %all-to-all-done.5.refs_1_, bf16[8,16,2048]{2,1,0:T(8,128)(2,1)} %collective-permute-done.7.refs_2_, ...), custom_call_target="tpu_custom_call" | custom-call | flops 6442450944 | tf_op jit(solution)/shard_map/backward/pallas_call | solution.py:70
  192.2 2.1 add.3
  194.3 3.5 %all-to-all-start.4 = ((bf16[8,16,2048]{2,1,0:T(8,128)(2,1)}), bf16[8,16,2048]{2,1,0:T(8,128)(2,1)S(1)}, u32[]{:S(2)}, u32[]{:S(2)}) async-start(bf16[8,16,2048]{2,1,0:T(8,128)(2,1)} %add.3), calls=%async_computation.4 | async-start | bytes 1048576 | tf_op jit(solution)/shard_map/all_to_all | solution.py:302
  197.8 17.9 %collective-permute-done.4.refs_1_ = bf16[256,2048]{1,0:T(8,128)(2,1)} collective-permute-done((bf16[256,2048]{1,0:T(8,128)(2,1)}, bf16[256,2048]{1,0:T(8,128)(2,1)}, u32[]{:S(2)}, u32[]{:S(2)}) %collective-permute-start.4) | collective-permute-done | bytes 1048608 | tf_op jit(solution)/shard_map/ppermute | solution.py:298
  215.7 2.7 %add.2 = bf16[8,32,2048]{2,1,0:T(8,128)(2,1)} custom-call(bf16[256,2048]{1,0:T(8,128)(2,1)} %get-tuple-element.29.refs_0_.refs_6_, bf16[256,2048]{1,0:T(8,128)(2,1)} %collective-permute-done.4.refs_1_), custom_call_target="tpu_custom_call" | custom-call | tf_op jit(solution)/shard_map/add/pallas_call | solution.py:70
  218.5 31.0 %all_to_all.32.refs_2_ = bf16[8,32,2048]{2,1,0:T(8,128)(2,1)} all-to-all(bf16[8,32,2048]{2,1,0:T(8,128)(2,1)} %add.2), channel_id=1, replica_groups=mesh['ctx'=2,'group'=4,'side'=2,'core'=2] {'ctx','group'}, dimensions={0} | all-to-all | bytes 2097152 | tf_op jit(solution)/shard_map/all_to_all | solution.py:302
  249.4 3.3 %combine.1 = bf16[128,2048]{1,0:T(8,128)(2,1)} custom-call(s32[128,2]{1,0:T(8,128)} %get-tuple-element.25.refs_0_, f32[2,128]{1,0:T(2,128)} %bitcast.23, bf16[8,32,2048]{2,1,0:T(8,128)(2,1)} %all_to_all.32.refs_2_, bf16[8,16,2048]{2,1,0:T(8,128)(2,1)} %copy-done.1, f32[128,2048]{1,0:T(8,128)} %get-tuple-element.34.refs_4_), custom_call_target="tpu_custom_call" | custom-call | flops 402500000 | tf_op jit(solution)/shard_map/combine/pallas_call | solution.py:70
  252.7 5.8 %finish.1 = (bf16[256,2048]{1,0:T(8,128)(2,1)}, bf16[256,2048]{1,0:T(8,128)(2,1)}, bf16[256,2048]{1,0:T(8,128)(2,1)}) custom-call(f32[256,2048]{1,0:T(8,128)} %get-tuple-element.39.refs_0_, f32[256,2048]{1,0:T(8,128)} %get-tuple-element.40.refs_1_, f32[256,2048]{1,0:T(8,128)} %get-tuple-element.41.refs_2_, bf16[768,2048]{1,0:T(8,128)(2,1)} %collective-permute-done.9.refs_3_), custom_call_target="tpu_custom_call" | custom-call | tf_op jit(solution)/shard_map/finish/pallas_call | solution.py:70
  (31 shorter events, 13.9 us)
Async XLA Ops:
  0.6 13.5 %copy-start.4 = (bf16[1,128,1024]{2,1,0:T(8,128)(2,1)S(1)}, bf16[1,128,1024]{2,1,0:T(8,128)(2,1)}, u32[]{:S(2)}) copy-start(bf16[1,128,1024]{2,1,0:T(8,128)(2,1)} %param.15) | copy-start | bytes 786436
  4.3 35.3 %collective-permute-start.2 = (bf16[768,2048]{1,0:T(8,128)(2,1)}, bf16[768,2048]{1,0:T(8,128)(2,1)}, u32[]{:S(2)}, u32[]{:S(2)}) collective-permute-start(bf16[768,2048]{1,0:T(8,128)(2,1)} %pack.1), channel_id=1, source_target_pairs={{0,1},{1,0},{2,3},{3,2},{4,5},{5,4},{6,7},{7,6},{8,9},{9,8},{10,11... | collective-permute-start | bytes 9437192 | tf_op jit(solution)/shard_map/ppermute | solution.py:298
  7.3 32.3 %all-to-all-start = ((bf16[8,16,2048]{2,1,0:T(8,128)(2,1)}), bf16[8,16,2048]{2,1,0:T(8,128)(2,1)S(1)}, u32[]{:S(2)}, u32[]{:S(2)}) async-start(bf16[8,16,2048]{2,1,0:T(8,128)(2,1)} %get-tuple-element.27), calls=%async_computation | async-start | bytes 1048576 | tf_op jit(solution)/shard_map/all_to_all | solution.py:302
  14.2 12.5 %collective-permute-start = (bf16[128,1024]{1,0:T(8,128)(2,1)S(1)}, bf16[128,1024]{1,0:T(8,128)(2,1)S(1)}, u32[]{:S(2)}, u32[]{:S(2)}) collective-permute-start(bf16[128,1024]{1,0:T(8,128)(2,1)S(1)} %bitcast.18), channel_id=1, source_target_pairs={{0,16},{16,0},{1,17},{17,1},{2,18},{18,2},{3,19},{19,3},{4,20},{20... | collective-permute-start | bytes 786440 | tf_op jit(solution)/shard_map/ppermute | solution.py:307
  16.2 17.8 %collective-permute-start.1 = (bf16[128,1024]{1,0:T(8,128)(2,1)}, bf16[128,1024]{1,0:T(8,128)(2,1)S(1)}, u32[]{:S(2)}, u32[]{:S(2)}) collective-permute-start(bf16[128,1024]{1,0:T(8,128)(2,1)} %bitcast.19), channel_id=1, source_target_pairs={{0,16},{16,0},{1,17},{17,1},{2,18},{18,2},{3,19},{19,3},{4,20},{20... | collective-permute-start | bytes 786440 | tf_op jit(solution)/shard_map/ppermute | solution.py:307
  26.7 0.7 copy-start.5
  34.0 0.7 copy-start.6
  39.6 0.8 copy-start.2
  93.4 33.8 %copy-start = (bf16[8,16,2048]{2,1,0:T(8,128)(2,1)S(1)}, bf16[8,16,2048]{2,1,0:T(8,128)(2,1)}, u32[]{:S(2)}) copy-start(bf16[8,16,2048]{2,1,0:T(8,128)(2,1)} %all_to_all.30.refs_0_.refs_4_.refs_12_) | copy-start | bytes 1572868
  96.3 29.4 %all-to-all-start.5 = ((bf16[8,32,2048]{2,1,0:T(8,128)(2,1)}), bf16[8,32,2048]{2,1,0:T(8,128)(2,1)}, u32[]{:S(2)}, u32[]{:S(2)}) async-start(bf16[8,32,2048]{2,1,0:T(8,128)(2,1)} %late_slots.1), calls=%async_computation.5 | async-start | bytes 2097152 | tf_op jit(solution)/shard_map/all_to_all | solution.py:302
  100.7 28.5 %collective-permute-start.3 = (bf16[8,32,2048]{2,1,0:T(8,128)(2,1)}, bf16[8,32,2048]{2,1,0:T(8,128)(2,1)}, u32[]{:S(2)}, u32[]{:S(2)}) collective-permute-start(bf16[8,32,2048]{2,1,0:T(8,128)(2,1)} %all_to_all.31.refs_0_.refs_3_.refs_10_), channel_id=1, source_target_pairs={{0,2},{2,0},{1,3},{3,1},{4,6},{6,4},{5,7},{7,5},{8,10},{10,8},{9,1... | collective-permute-start | bytes 3145736 | tf_op jit(solution)/shard_map/ppermute | solution.py:298
  125.7 48.9 %collective-permute-start.8 = (bf16[8,32,2048]{2,1,0:T(8,128)(2,1)}, bf16[8,32,2048]{2,1,0:T(8,128)(2,1)}, u32[]{:S(2)}, u32[]{:S(2)}) collective-permute-start(bf16[8,32,2048]{2,1,0:T(8,128)(2,1)} %all-to-all-done.5.refs_1_), channel_id=1, source_target_pairs={{0,2},{2,0},{1,3},{3,1},{4,6},{6,4},{5,7},{7,5},{8,10},{10,8},{9,1... | collective-permute-start | bytes 3145736 | tf_op jit(solution)/shard_map/ppermute | solution.py:298
  127.2 36.2 %collective-permute-start.5 = (bf16[8,16,2048]{2,1,0:T(8,128)(2,1)S(1)}, bf16[8,16,2048]{2,1,0:T(8,128)(2,1)}, u32[]{:S(2)}, u32[]{:S(2)}) collective-permute-start(bf16[8,16,2048]{2,1,0:T(8,128)(2,1)S(1)} %copy-done), channel_id=1, source_target_pairs={{0,2},{2,0},{1,3},{3,1},{4,6},{6,4},{5,7},{7,5},{8,10},{10,8},{9,1... | collective-permute-start | bytes 1572872 | tf_op jit(solution)/shard_map/ppermute | solution.py:298
  127.7 46.9 %collective-permute-start.7 = (bf16[8,16,2048]{2,1,0:T(8,128)(2,1)}, bf16[8,16,2048]{2,1,0:T(8,128)(2,1)}, u32[]{:S(2)}, u32[]{:S(2)}) collective-permute-start(bf16[8,16,2048]{2,1,0:T(8,128)(2,1)} %copy-done.2), channel_id=1, source_target_pairs={{0,2},{2,0},{1,3},{3,1},{4,6},{6,4},{5,7},{7,5},{8,10},{10,8},{9,1... | collective-permute-start | bytes 1572872 | tf_op jit(solution)/shard_map/ppermute | solution.py:298
  169.7 21.8 %collective-permute-start.6 = (bf16[128,2048]{1,0:T(8,128)(2,1)}, bf16[128,2048]{1,0:T(8,128)(2,1)S(1)}, u32[]{:S(2)}, u32[]{:S(2)}) collective-permute-start(bf16[128,2048]{1,0:T(8,128)(2,1)} %get-tuple-element.33), channel_id=1, source_target_pairs={{0,2},{2,0},{1,3},{3,1},{4,6},{6,4},{5,7},{7,5},{8,10},{10,8},{9,1... | collective-permute-start | bytes 1572872 | tf_op jit(solution)/shard_map/ppermute | solution.py:298
  189.8 62.9 %collective-permute-start.9 = (bf16[768,2048]{1,0:T(8,128)(2,1)}, bf16[768,2048]{1,0:T(8,128)(2,1)}, u32[]{:S(2)}, u32[]{:S(2)}) collective-permute-start(bf16[768,2048]{1,0:T(8,128)(2,1)} %get-tuple-element.42), channel_id=1, source_target_pairs={{0,1},{1,0},{2,3},{3,2},{4,5},{5,4},{6,7},{7,6},{8,9},{9,8},{10,11... | collective-permute-start | bytes 9437192 | tf_op jit(solution)/shard_map/ppermute | solution.py:298
  189.9 25.9 %collective-permute-start.4 = (bf16[256,2048]{1,0:T(8,128)(2,1)}, bf16[256,2048]{1,0:T(8,128)(2,1)}, u32[]{:S(2)}, u32[]{:S(2)}) collective-permute-start(bf16[256,2048]{1,0:T(8,128)(2,1)} %get-tuple-element.30), channel_id=1, source_target_pairs={{0,2},{2,0},{1,3},{3,1},{4,6},{6,4},{5,7},{7,5},{8,10},{10,8},{9,1... | collective-permute-start | bytes 3145736 | tf_op jit(solution)/shard_map/ppermute | solution.py:298
  191.4 0.8 copy-start.3
  194.3 24.1 %all-to-all-start.4 = ((bf16[8,16,2048]{2,1,0:T(8,128)(2,1)}), bf16[8,16,2048]{2,1,0:T(8,128)(2,1)S(1)}, u32[]{:S(2)}, u32[]{:S(2)}) async-start(bf16[8,16,2048]{2,1,0:T(8,128)(2,1)} %add.3), calls=%async_computation.4 | async-start | bytes 1048576 | tf_op jit(solution)/shard_map/all_to_all | solution.py:302
  218.5 31.0 %copy-start.1 = (bf16[8,16,2048]{2,1,0:T(8,128)(2,1)}, bf16[8,16,2048]{2,1,0:T(8,128)(2,1)S(1)}, u32[]{:S(2)}) copy-start(bf16[8,16,2048]{2,1,0:T(8,128)(2,1)S(1)} %all-to-all-done.4.refs_3_) | copy-start | bytes 1572868

commit v7 on v4

--- a/solution.py
+++ b/solution.py
@@ -228,10 +228,10 @@
     both = jnp.concatenate([gate_cot.astype(jnp.bfloat16), up_cot.astype(jnp.bfloat16)], axis=0)
     grads = dot(both, ready(4)[...])
     for n in range(2):
-        kept[n][...] = grads[2 * n * half : (2 * n + 1) * half]
+        kept[n][...] = grads[2 * n * half : (2 * n + 1) * half].astype(jnp.bfloat16)
         sent[n][...] = grads[(2 * n + 1) * half : (2 * n + 2) * half].astype(jnp.bfloat16)
     grads = dot((active * up_pre).astype(jnp.bfloat16), cots)
-    kept[2][...] = grads[:half]
+    kept[2][...] = grads[:half].astype(jnp.bfloat16)
     sent[2][...] = grads[half:].astype(jnp.bfloat16)
 
 
@@ -348,7 +348,7 @@
 
     pairs = [[weight, swapped(weight, "core")] for weight in (w_gate, w_up, w_down)]
     gate_pres, up_pres, returned = [], [], []
-    after = cots_across[:1]
+    after = []
     for (_, count), own, across in zip(row_cuts, rows, rows_across):
         half = blocks * count
         pre = shape_of(2 * hidden, 2 * half, dtype=jnp.float32)
@@ -361,7 +361,7 @@
             flops=24 * half * hidden * width,
             after=after,
         )
-        after = [keep]
+        after = [keep] + cots_across[:1]
         gate_pres.append(gate_pre)
         up_pres.append(up_pre)
         (sums,) = call(
@@ -399,7 +399,7 @@
             (pre_pieces[1], (2 * hidden, total_rows)),
             (row_pieces, (total_rows, width)),
         ],
-        [shape_of(hidden, width, dtype=jnp.float32)] * 3 + [shape_of(hidden, width)] * 3,
+        [shape_of(hidden, width)] * 6,
         flops=16 * total_rows * hidden * width,
     )
     operands = []

time: 216 us -> 214 us (level)
    unnamed x36 -> x32, local copies, waits for them, and re-layouts: 7.61 us -> 6.81 us
  transfers between devices with their start and end apart: 19 -> 19, of which waited for: 10 -> 11; matrix products, arithmetic and copies ran while one was open for 0% -> 0% of each run, Pallas kernels for 21% -> 20%
where the time goes in v7:
time: 214 us
  waiting for transfers between devices  83.9 us (39%)
  Pallas kernels  53.6 us (25%)
  starting transfers between devices  37.3 us (17%)
  blocking collectives  31 us (14%)
  local copies, waits for them, and re-layouts  6.81 us (3%)
    ppermute x12, waiting for transfers between devices, swapped(): lax.ppermute(value, axis, [(n, n ^ 1) for n in range(lax.axis_size(axis))])  55.1 us
    pallas_call x11, Pallas kernels, call(): pl.pallas_call(kernel, out_shape=tuple(outs), in_specs=[ANY] * n_in, out_...  53.6 us
    all_to_all x1, blocking collectives, exchanged(): lax.all_to_all(shaped, ('ctx', 'group'), split_axis=0, concat_axis=0, til...  31 us
    all_to_all x5, starting transfers between devices, exchanged(): lax.all_to_all(shaped, ('ctx', 'group'), split_axis=0, concat_axis=0, til...  26.8 us
    ppermute x2, waiting for transfers between devices, turned(): lax.ppermute(value, 'ctx', [(n, (n + step) % size) for n in range(size)])  17.1 us
    all_to_all x5, waiting for transfers between devices, exchanged(): lax.all_to_all(shaped, ('ctx', 'group'), split_axis=0, concat_axis=0, til...  11.6 us
    ppermute x12, starting transfers between devices, swapped(): lax.ppermute(value, axis, [(n, n ^ 1) for n in range(lax.axis_size(axis))])  8.51 us
    unnamed x32, local copies, waits for them, and re-layouts  6.81 us
  transfers between devices with their start and end apart: 19, of which 11 were waited for; matrix products, arithmetic and copies ran while one was open for 0% of the time, Pallas kernels for 20%

profile of v7, /device:TPU:0, one launch (start us, length us, event | category | flops | bytes accessed | tf_op | source)
XLA Modules:
  0.0 213.7 jit_solution(13941168357389067305)
XLA Ops:
  3.2 7.3 %all-to-all-start = ((bf16[8,16,2048]{2,1,0:T(8,128)(2,1)}), bf16[8,16,2048]{2,1,0:T(8,128)(2,1)S(1)}, u32[]{:S(2)}, u32[]{:S(2)}) async-start(bf16[8,16,2048]{2,1,0:T(8,128)(2,1)} %get-tuple-element.29), calls=%async_computation | async-start | bytes 1048576 | tf_op jit(solution)/shard_map/all_to_all | solution.py:286
  12.5 12.3 %collective-permute-done.refs_2_ = bf16[128,1024]{1,0:T(8,128)(2,1)S(1)} collective-permute-done((bf16[128,1024]{1,0:T(8,128)(2,1)}, bf16[128,1024]{1,0:T(8,128)(2,1)S(1)}, u32[]{:S(2)}, u32[]{:S(2)}) %collective-permute-start) | collective-permute-done | bytes 262176 | tf_op jit(solution)/shard_map/ppermute | solution.py:291
  24.8 4.8 %collective-permute-done.1.refs_4_ = bf16[128,1024]{1,0:T(8,128)(2,1)S(1)} collective-permute-done((bf16[128,1024]{1,0:T(8,128)(2,1)}, bf16[128,1024]{1,0:T(8,128)(2,1)S(1)}, u32[]{:S(2)}, u32[]{:S(2)}) %collective-permute-start.1) | collective-permute-done | bytes 262176 | tf_op jit(solution)/shard_map/ppermute | solution.py:291
  30.4 4.9 %attend.1 = (f32[128,2048]{1,0:T(8,128)}, bf16[128,2048]{1,0:T(8,128)(2,1)}) custom-call(bf16[128,1024]{1,0:T(8,128)(2,1)} %bitcast.16, bf16[128,1024]{1,0:T(8,128)(2,1)} %bitcast.18, bf16[128,1024]{1,0:T(8,128)(2,1)} %copy-done.13, bf16[128,1024]{1,0:T(8,128)(2,1)} %bitcast.20, bf16[128,1024]{1,0:T(8,128)(2,1)} %copy-done.14, bf16[128,2048]{1,0:T(8,128)(2,1)} %bitcast.12, ...), custom_call_target="tpu_custom_call" | custom-call | flops 1073741824 | bytes 6045696 | tf_op jit(solution)/shard_map/attend/pallas_call | solution.py:71
  36.1 2.8 %place.1 = (bf16[8,32,2048]{2,1,0:T(8,128)(2,1)}, bf16[8,16,2048]{2,1,0:T(8,128)(2,1)}) custom-call(s32[128,2]{1,0:T(8,128)} %get-tuple-element.27.refs_0_, bf16[128,2048]{1,0:T(8,128)(2,1)} %get-tuple-element.28.refs_1_, bf16[8,16,2048]{2,1,0:T(8,128)(2,1)} %copy-done.3), custom_call_target="tpu_custom_call" | custom-call | flops 201326592 | bytes 525312 | tf_op jit(solution)/shard_map/place/pallas_call | solution.py:71
  38.9 31.0 %all_to_all.30.refs_0_.refs_3_.refs_10_ = bf16[8,32,2048]{2,1,0:T(8,128)(2,1)S(1)} all-to-all(bf16[8,32,2048]{2,1,0:T(8,128)(2,1)} %get-tuple-element.30), channel_id=1, replica_groups=mesh['ctx'=2,'group'=4,'side'=2,'core'=2] {'ctx','group'}, dimensions={0} | all-to-all | bytes 2097152 | tf_op jit(solution)/shard_map/all_to_all | solution.py:286
  70.0 3.5 %all-to-all-start.3 = ((bf16[8,16,2048]{2,1,0:T(8,128)(2,1)}), bf16[8,16,2048]{2,1,0:T(8,128)(2,1)S(1)}, u32[]{:S(2)}, u32[]{:S(2)}) async-start(bf16[8,16,2048]{2,1,0:T(8,128)(2,1)} %get-tuple-element.33), calls=%async_computation.3 | async-start | bytes 1048576 | tf_op jit(solution)/shard_map/all_to_all | solution.py:286
  75.6 11.6 %all-to-all-done.3.refs_0_.refs_4_.refs_12_ = bf16[8,16,2048]{2,1,0:T(8,128)(2,1)S(1)} async-done(((bf16[8,16,2048]{2,1,0:T(8,128)(2,1)}), bf16[8,16,2048]{2,1,0:T(8,128)(2,1)S(1)}, u32[]{:S(2)}, u32[]{:S(2)}) %all-to-all-start.3) | async-done | bytes 524320 | tf_op jit(solution)/shard_map/all_to_all | solution.py:286
  88.1 2.8 %late_slots.1 = bf16[8,32,2048]{2,1,0:T(8,128)(2,1)} custom-call(s32[128,2]{1,0:T(8,128)} %get-tuple-element.27.refs_0_, f32[2,128]{1,0:T(2,128)} %bitcast.22, bf16[128,2048]{1,0:T(8,128)(2,1)} %bitcast.14, bf16[8,32,2048]{2,1,0:T(8,128)(2,1)} %copy-done.1, bf16[8,16,2048]{2,1,0:T(8,128)(2,1)} %copy-done), custom_call_target="tpu_custom_call" | custom-call | flops 402653184 | bytes 526336 | tf_op jit(solution)/shard_map/late_slots/pallas_call | solution.py:71
  90.9 4.3 %all-to-all-start.5 = ((bf16[8,32,2048]{2,1,0:T(8,128)(2,1)}), bf16[8,32,2048]{2,1,0:T(8,128)(2,1)}, u32[]{:S(2)}, u32[]{:S(2)}) async-start(bf16[8,32,2048]{2,1,0:T(8,128)(2,1)} %late_slots.1), calls=%async_computation.5 | async-start | bytes 2097152 | tf_op jit(solution)/shard_map/all_to_all | solution.py:286
  97.3 2.9 %collective-permute-done.2.refs_1_.refs_11_ = bf16[8,32,2048]{2,1,0:T(8,128)(2,1)} collective-permute-done((bf16[8,32,2048]{2,1,0:T(8,128)(2,1)S(1)}, bf16[8,32,2048]{2,1,0:T(8,128)(2,1)}, u32[]{:S(2)}, u32[]{:S(2)}) %collective-permute-start.2) | collective-permute-done | bytes 1048608 | tf_op jit(solution)/shard_map/ppermute | solution.py:282
  100.2 7.7 %forward.2 = (bf16[256,2048]{1,0:T(8,128)(2,1)}, bf16[256,2048]{1,0:T(8,128)(2,1)}, f32[512,512]{1,0:T(8,128)}, f32[512,512]{1,0:T(8,128)}) custom-call(bf16[8,32,2048]{2,1,0:T(8,128)(2,1)} %copy-done.1, bf16[8,32,2048]{2,1,0:T(8,128)(2,1)} %collective-permute-done.2.refs_1_.refs_11_, bf16[256,2048]{1,0:T(8,128)(2,1)} %refs_2_.3, ...), custom_call_target="tpu_custom_call" | custom-call | flops 3221225472 | bytes 8388608 | tf_op jit(solution)/shard_map/forward/pallas_call | solution.py:71
  107.9 3.4 %collective-permute-done.8.refs_9_.refs_2_ = bf16[8,16,2048]{2,1,0:T(8,128)(2,1)S(1)} collective-permute-done((bf16[8,16,2048]{2,1,0:T(8,128)(2,1)S(1)}, bf16[8,16,2048]{2,1,0:T(8,128)(2,1)S(1)}, u32[]{:S(2)}, u32[]{:S(2)}) %collective-permute-start.8) | collective-permute-done | bytes 524320 | tf_op jit(solution)/shard_map/ppermute | solution.py:282
  111.3 10.8 %collective-permute-done.7.refs_1_.refs_13_ = bf16[8,16,2048]{2,1,0:T(8,128)(2,1)S(1)} collective-permute-done((bf16[8,16,2048]{2,1,0:T(8,128)(2,1)}, bf16[8,16,2048]{2,1,0:T(8,128)(2,1)S(1)}, u32[]{:S(2)}, u32[]{:S(2)}) %collective-permute-start.7) | collective-permute-done | bytes 524320 | tf_op jit(solution)/shard_map/ppermute | solution.py:282
  122.9 6.4 %forward.3 = (bf16[128,2048]{1,0:T(8,128)(2,1)}, bf16[128,2048]{1,0:T(8,128)(2,1)}, f32[512,256]{1,0:T(8,128)}, f32[512,256]{1,0:T(8,128)}) custom-call(bf16[8,16,2048]{2,1,0:T(8,128)(2,1)} %copy-done, bf16[8,16,2048]{2,1,0:T(8,128)(2,1)} %copy-done.11, bf16[256,2048]{1,0:T(8,128)(2,1)} %refs_2_.3, bf16[256,2048]{1,0:T(8,128)(2,1)} %collective-permute-done.3.refs_3_, ...), custom_call_target="tpu_custom_call" | custom-call | flops 1610612736 | bytes 7340032 | tf_op jit(solution)/shard_map/forward/pallas_call | solution.py:71
  131.4 13.0 %collective-permute-done.9.refs_1_ = bf16[128,2048]{1,0:T(8,128)(2,1)S(1)} collective-permute-done((bf16[128,2048]{1,0:T(8,128)(2,1)}, bf16[128,2048]{1,0:T(8,128)(2,1)S(1)}, u32[]{:S(2)}, u32[]{:S(2)}) %collective-permute-start.9) | collective-permute-done | bytes 524320 | tf_op jit(solution)/shard_map/ppermute | solution.py:282
  147.3 5.9 %all-to-all-start.4 = ((bf16[8,16,2048]{2,1,0:T(8,128)(2,1)}), bf16[8,16,2048]{2,1,0:T(8,128)(2,1)S(1)}, u32[]{:S(2)}, u32[]{:S(2)}) async-start(bf16[8,16,2048]{2,1,0:T(8,128)(2,1)} %add.3), calls=%async_computation.4 | async-start | bytes 1048576 | tf_op jit(solution)/shard_map/all_to_all | solution.py:286
  154.7 12.2 %collective-permute-done.6.refs_1_ = bf16[256,2048]{1,0:T(8,128)(2,1)S(1)} collective-permute-done((bf16[256,2048]{1,0:T(8,128)(2,1)S(1)}, bf16[256,2048]{1,0:T(8,128)(2,1)S(1)}, u32[]{:S(2)}, u32[]{:S(2)}) %collective-permute-start.6) | collective-permute-done | bytes 1048608 | tf_op jit(solution)/shard_map/ppermute | solution.py:282
  167.9 2.7 %add.2 = bf16[8,32,2048]{2,1,0:T(8,128)(2,1)} custom-call(bf16[256,2048]{1,0:T(8,128)(2,1)} %get-tuple-element.31.refs_0_.refs_8_, bf16[256,2048]{1,0:T(8,128)(2,1)} %copy-done.7), custom_call_target="tpu_custom_call" | custom-call | bytes 2097152 | tf_op jit(solution)/shard_map/add/pallas_call | solution.py:71
  170.6 5.9 %all-to-all-start.2 = ((bf16[8,32,2048]{2,1,0:T(8,128)(2,1)}), bf16[8,32,2048]{2,1,0:T(8,128)(2,1)S(1)}, u32[]{:S(2)}, u32[]{:S(2)}) async-start(bf16[8,32,2048]{2,1,0:T(8,128)(2,1)} %add.2), calls=%async_computation.2 | async-start | bytes 2097152 | tf_op jit(solution)/shard_map/all_to_all | solution.py:286
  176.4 11.7 %collective-permute-done.10.refs_3_ = bf16[8,32,2048]{2,1,0:T(8,128)(2,1)} collective-permute-done((bf16[8,32,2048]{2,1,0:T(8,128)(2,1)}, bf16[8,32,2048]{2,1,0:T(8,128)(2,1)}, u32[]{:S(2)}, u32[]{:S(2)}) %collective-permute-start.10) | collective-permute-done | bytes 1048608 | tf_op jit(solution)/shard_map/ppermute | solution.py:282
  188.1 13.9 %backward.1 = (bf16[256,2048]{1,0:T(8,128)(2,1)}, bf16[256,2048]{1,0:T(8,128)(2,1)}, bf16[256,2048]{1,0:T(8,128)(2,1)}, bf16[256,2048]{1,0:T(8,128)(2,1)}, bf16[...) custom-call(bf16[8,16,2048]{2,1,0:T(8,128)(2,1)} %copy-done.3, bf16[8,32,2048]{2,1,0:T(8,128)(2,1)} %all-to-all-done.5.refs_1_, ...), custom_call_target="tpu_custom_call" | custom-call | flops 6442450944 | bytes 11534336 | tf_op jit(solution)/shard_map/backward/pallas_call | solution.py:71
  203.7 3.3 %combine.1 = bf16[128,2048]{1,0:T(8,128)(2,1)} custom-call(s32[128,2]{1,0:T(8,128)} %get-tuple-element.27.refs_0_, f32[2,128]{1,0:T(2,128)} %bitcast.23, bf16[8,32,2048]{2,1,0:T(8,128)(2,1)} %copy-done.2, bf16[8,16,2048]{2,1,0:T(8,128)(2,1)} %copy-done.5, f32[128,2048]{1,0:T(8,128)} %get-tuple-element.36.refs_4_), custom_call_target="tpu_custom_call" | custom-call | flops 402653184 | bytes 2623488 | tf_op jit(solution)/shard_map/combine/pallas_call | solution.py:71
  209.0 4.5 %finish.1 = (bf16[256,2048]{1,0:T(8,128)(2,1)}, bf16[256,2048]{1,0:T(8,128)(2,1)}, bf16[256,2048]{1,0:T(8,128)(2,1)}) custom-call(bf16[256,2048]{1,0:T(8,128)(2,1)} %get-tuple-element.41.refs_0_, bf16[256,2048]{1,0:T(8,128)(2,1)} %copy-done.8, bf16[256,2048]{1,0:T(8,128)(2,1)} %get-tuple-element.43.refs_2_, bf16[256,2048]{1,0:T(8,128)(2,1)} %copy-done.9, ...), custom_call_target="tpu_custom_call" | custom-call | bytes 6291456 | tf_op jit(solution)/shard_map/finish/pallas_call | solution.py:71
  (58 shorter events, 23.2 us)
Async XLA Ops:
  3.2 32.1 %all-to-all-start = ((bf16[8,16,2048]{2,1,0:T(8,128)(2,1)}), bf16[8,16,2048]{2,1,0:T(8,128)(2,1)S(1)}, u32[]{:S(2)}, u32[]{:S(2)}) async-start(bf16[8,16,2048]{2,1,0:T(8,128)(2,1)} %get-tuple-element.29), calls=%async_computation | async-start | bytes 1048576 | tf_op jit(solution)/shard_map/all_to_all | solution.py:286
  10.5 14.4 %collective-permute-start = (bf16[128,1024]{1,0:T(8,128)(2,1)}, bf16[128,1024]{1,0:T(8,128)(2,1)S(1)}, u32[]{:S(2)}, u32[]{:S(2)}) collective-permute-start(bf16[128,1024]{1,0:T(8,128)(2,1)} %bitcast.17), channel_id=1, source_target_pairs={{0,16},{16,0},{1,17},{17,1},{2,18},{18,2},{3,19},{19,3},{4,20},{20... | collective-permute-start | bytes 786440 | tf_op jit(solution)/shard_map/ppermute | solution.py:291
  12.5 17.2 %collective-permute-start.1 = (bf16[128,1024]{1,0:T(8,128)(2,1)}, bf16[128,1024]{1,0:T(8,128)(2,1)S(1)}, u32[]{:S(2)}, u32[]{:S(2)}) collective-permute-start(bf16[128,1024]{1,0:T(8,128)(2,1)} %bitcast.19), channel_id=1, source_target_pairs={{0,16},{16,0},{1,17},{17,1},{2,18},{18,2},{3,19},{19,3},{4,20},{20... | collective-permute-start | bytes 786440 | tf_op jit(solution)/shard_map/ppermute | solution.py:291
  30.4 43.1 %copy-start.6 = (bf16[256,2048]{1,0:T(8,128)(2,1)S(1)}, bf16[256,2048]{1,0:T(8,128)(2,1)}, u32[]{:S(2)}) copy-start(bf16[256,2048]{1,0:T(8,128)(2,1)} %refs_2_.3) | copy-start | bytes 3145732
  38.9 56.3 %copy-start.4 = (bf16[8,16,2048]{2,1,0:T(8,128)(2,1)S(1)}, bf16[8,16,2048]{2,1,0:T(8,128)(2,1)}, u32[]{:S(2)}) copy-start(bf16[8,16,2048]{2,1,0:T(8,128)(2,1)} %copy-done.3) | copy-start | bytes 1572868
  70.0 17.3 %copy-start.1 = (bf16[8,32,2048]{2,1,0:T(8,128)(2,1)}, bf16[8,32,2048]{2,1,0:T(8,128)(2,1)S(1)}, u32[]{:S(2)}) copy-start(bf16[8,32,2048]{2,1,0:T(8,128)(2,1)S(1)} %all_to_all.30.refs_0_.refs_3_.refs_10_) | copy-start | bytes 3145732
  70.0 17.3 %all-to-all-start.3 = ((bf16[8,16,2048]{2,1,0:T(8,128)(2,1)}), bf16[8,16,2048]{2,1,0:T(8,128)(2,1)S(1)}, u32[]{:S(2)}, u32[]{:S(2)}) async-start(bf16[8,16,2048]{2,1,0:T(8,128)(2,1)} %get-tuple-element.33), calls=%async_computation.3 | async-start | bytes 1048576 | tf_op jit(solution)/shard_map/all_to_all | solution.py:286
  73.5 23.3 %collective-permute-start.3 = (bf16[256,2048]{1,0:T(8,128)(2,1)S(1)}, bf16[256,2048]{1,0:T(8,128)(2,1)}, u32[]{:S(2)}, u32[]{:S(2)}) collective-permute-start(bf16[256,2048]{1,0:T(8,128)(2,1)S(1)} %copy-done.6), channel_id=1, source_target_pairs={{0,1},{1,0},{2,3},{3,2},{4,5},{5,4},{6,7},{7,6},{8,9},{9,8},{10,11... | collective-permute-start | bytes 3145736 | tf_op jit(solution)/shard_map/ppermute | solution.py:282
  73.6 23.7 %collective-permute-start.4 = (bf16[256,2048]{1,0:T(8,128)(2,1)}, bf16[256,2048]{1,0:T(8,128)(2,1)}, u32[]{:S(2)}, u32[]{:S(2)}) collective-permute-start(bf16[256,2048]{1,0:T(8,128)(2,1)} %refs_4_.4), channel_id=1, source_target_pairs={{0,1},{1,0},{2,3},{3,2},{4,5},{5,4},{6,7},{7,6},{8,9},{9,8},{10,11... | collective-permute-start | bytes 3145736 | tf_op jit(solution)/shard_map/ppermute | solution.py:282
  74.0 23.2 %collective-permute-start.5 = (bf16[256,2048]{1,0:T(8,128)(2,1)}, bf16[256,2048]{1,0:T(8,128)(2,1)}, u32[]{:S(2)}, u32[]{:S(2)}) collective-permute-start(bf16[256,2048]{1,0:T(8,128)(2,1)} %refs_4_.5), channel_id=1, source_target_pairs={{0,1},{1,0},{2,3},{3,2},{4,5},{5,4},{6,7},{7,6},{8,9},{9,8},{10,11... | collective-permute-start | bytes 3145736 | tf_op jit(solution)/shard_map/ppermute | solution.py:282
  74.1 26.1 %collective-permute-start.2 = (bf16[8,32,2048]{2,1,0:T(8,128)(2,1)S(1)}, bf16[8,32,2048]{2,1,0:T(8,128)(2,1)}, u32[]{:S(2)}, u32[]{:S(2)}) collective-permute-start(bf16[8,32,2048]{2,1,0:T(8,128)(2,1)S(1)} %all_to_all.30.refs_0_.refs_3_.refs_10_), channel_id=1, source_target_pairs={{0,2},{2,0},{1,3},{3,1},{4,6},{6,4},{5,7},{7,5},{8,10},{10,8},{9,1... | collective-permute-start | bytes 3145736 | tf_op jit(solution)/shard_map/ppermute | solution.py:282
  90.9 56.4 %all-to-all-start.5 = ((bf16[8,32,2048]{2,1,0:T(8,128)(2,1)}), bf16[8,32,2048]{2,1,0:T(8,128)(2,1)}, u32[]{:S(2)}, u32[]{:S(2)}) async-start(bf16[8,32,2048]{2,1,0:T(8,128)(2,1)} %late_slots.1), calls=%async_computation.5 | async-start | bytes 2097152 | tf_op jit(solution)/shard_map/all_to_all | solution.py:286
  95.2 16.1 %collective-permute-start.8 = (bf16[8,16,2048]{2,1,0:T(8,128)(2,1)S(1)}, bf16[8,16,2048]{2,1,0:T(8,128)(2,1)S(1)}, u32[]{:S(2)}, u32[]{:S(2)}) collective-permute-start(bf16[8,16,2048]{2,1,0:T(8,128)(2,1)S(1)} %copy-done.4), channel_id=1, source_target_pairs={{0,2},{2,0},{1,3},{3,1},{4,6},{6,4},{5,7},{7,5},{8,10},{10,8},{9,1... | collective-permute-start | bytes 1572872 | tf_op jit(solution)/shard_map/ppermute | solution.py:282
  96.8 25.3 %collective-permute-start.7 = (bf16[8,16,2048]{2,1,0:T(8,128)(2,1)}, bf16[8,16,2048]{2,1,0:T(8,128)(2,1)S(1)}, u32[]{:S(2)}, u32[]{:S(2)}) collective-permute-start(bf16[8,16,2048]{2,1,0:T(8,128)(2,1)} %copy-done), channel_id=1, source_target_pairs={{0,2},{2,0},{1,3},{3,1},{4,6},{6,4},{5,7},{7,5},{8,10},{10,8},{9,1... | collective-permute-start | bytes 1572872 | tf_op jit(solution)/shard_map/ppermute | solution.py:282
  111.3 10.8 %copy-start.10 = (bf16[8,16,2048]{2,1,0:T(8,128)(2,1)}, bf16[8,16,2048]{2,1,0:T(8,128)(2,1)S(1)}, u32[]{:S(2)}) copy-start(bf16[8,16,2048]{2,1,0:T(8,128)(2,1)S(1)} %collective-permute-done.8.refs_9_.refs_2_) | copy-start | bytes 1572868
  129.3 15.1 %collective-permute-start.9 = (bf16[128,2048]{1,0:T(8,128)(2,1)}, bf16[128,2048]{1,0:T(8,128)(2,1)S(1)}, u32[]{:S(2)}, u32[]{:S(2)}) collective-permute-start(bf16[128,2048]{1,0:T(8,128)(2,1)} %get-tuple-element.35), channel_id=1, source_target_pairs={{0,2},{2,0},{1,3},{3,1},{4,6},{6,4},{5,7},{7,5},{8,10},{10,8},{9,1... | collective-permute-start | bytes 1572872 | tf_op jit(solution)/shard_map/ppermute | solution.py:282
  130.9 36.0 %collective-permute-start.6 = (bf16[256,2048]{1,0:T(8,128)(2,1)S(1)}, bf16[256,2048]{1,0:T(8,128)(2,1)S(1)}, u32[]{:S(2)}, u32[]{:S(2)}) collective-permute-start(bf16[256,2048]{1,0:T(8,128)(2,1)S(1)} %copy-done.15), channel_id=1, source_target_pairs={{0,2},{2,0},{1,3},{3,1},{4,6},{6,4},{5,7},{7,5},{8,10},{10,8},{9,1... | collective-permute-start | bytes 3145736 | tf_op jit(solution)/shard_map/ppermute | solution.py:282
  147.3 23.2 %all-to-all-start.4 = ((bf16[8,16,2048]{2,1,0:T(8,128)(2,1)}), bf16[8,16,2048]{2,1,0:T(8,128)(2,1)S(1)}, u32[]{:S(2)}, u32[]{:S(2)}) async-start(bf16[8,16,2048]{2,1,0:T(8,128)(2,1)} %add.3), calls=%async_computation.4 | async-start | bytes 1048576 | tf_op jit(solution)/shard_map/all_to_all | solution.py:286
  153.2 34.9 %collective-permute-start.10 = (bf16[8,32,2048]{2,1,0:T(8,128)(2,1)}, bf16[8,32,2048]{2,1,0:T(8,128)(2,1)}, u32[]{:S(2)}, u32[]{:S(2)}) collective-permute-start(bf16[8,32,2048]{2,1,0:T(8,128)(2,1)} %all-to-all-done.5.refs_1_), channel_id=1, source_target_pairs={{0,2},{2,0},{1,3},{3,1},{4,6},{6,4},{5,7},{7,5},{8,10},{10,8},{9,1... | collective-permute-start | bytes 3145736 | tf_op jit(solution)/shard_map/ppermute | solution.py:282
  170.6 31.5 %copy-start.5 = (bf16[8,16,2048]{2,1,0:T(8,128)(2,1)}, bf16[8,16,2048]{2,1,0:T(8,128)(2,1)S(1)}, u32[]{:S(2)}) copy-start(bf16[8,16,2048]{2,1,0:T(8,128)(2,1)S(1)} %all-to-all-done.4.refs_3_) | copy-start | bytes 1572868
  170.6 32.1 %all-to-all-start.2 = ((bf16[8,32,2048]{2,1,0:T(8,128)(2,1)}), bf16[8,32,2048]{2,1,0:T(8,128)(2,1)S(1)}, u32[]{:S(2)}, u32[]{:S(2)}) async-start(bf16[8,32,2048]{2,1,0:T(8,128)(2,1)} %add.2), calls=%async_computation.2 | async-start | bytes 2097152 | tf_op jit(solution)/shard_map/all_to_all | solution.py:286
  202.1 4.9 %collective-permute-start.11 = (bf16[256,2048]{1,0:T(8,128)(2,1)}, bf16[256,2048]{1,0:T(8,128)(2,1)S(1)}, u32[]{:S(2)}, u32[]{:S(2)}) collective-permute-start(bf16[256,2048]{1,0:T(8,128)(2,1)} %get-tuple-element.42), channel_id=1, source_target_pairs={{0,1},{1,0},{2,3},{3,2},{4,5},{5,4},{6,7},{7,6},{8,9},{9,8},{10,11... | collective-permute-start | bytes 3145736 | tf_op jit(solution)/shard_map/ppermute | solution.py:282
  202.1 5.9 %collective-permute-start.12 = (bf16[256,2048]{1,0:T(8,128)(2,1)}, bf16[256,2048]{1,0:T(8,128)(2,1)S(1)}, u32[]{:S(2)}, u32[]{:S(2)}) collective-permute-start(bf16[256,2048]{1,0:T(8,128)(2,1)} %get-tuple-element.44), channel_id=1, source_target_pairs={{0,1},{1,0},{2,3},{3,2},{4,5},{5,4},{6,7},{7,6},{8,9},{9,8},{10,11... | collective-permute-start | bytes 3145736 | tf_op jit(solution)/shard_map/ppermute | solution.py:282
  202.6 5.5 %collective-permute-start.13 = (bf16[256,2048]{1,0:T(8,128)(2,1)}, bf16[256,2048]{1,0:T(8,128)(2,1)}, u32[]{:S(2)}, u32[]{:S(2)}) collective-permute-start(bf16[256,2048]{1,0:T(8,128)(2,1)} %get-tuple-element.46), channel_id=1, source_target_pairs={{0,1},{1,0},{2,3},{3,2},{4,5},{5,4},{6,7},{7,6},{8,9},{9,8},{10,11... | collective-permute-start | bytes 3145736 | tf_op jit(solution)/shard_map/ppermute | solution.py:282
  (11 other events, 20.9 us)

commit v8 on v7

--- a/solution.py
+++ b/solution.py
@@ -361,7 +361,6 @@
             flops=24 * half * hidden * width,
             after=after,
         )
-        after = [keep] + cots_across[:1]
         gate_pres.append(gate_pre)
         up_pres.append(up_pre)
         (sums,) = call(
@@ -370,6 +369,7 @@
             [whole(keep), whole(swapped(send, "side"))],
             [shape_of(blocks, count, width)],
         )
+        after = [sums] + cots_across[:1]
         returned.append(exchanged(sums))
 
     total_rows = 2 * slots

time: 214 us -> 221 us (1.033)
  waiting for transfers between devices: 83.9 us -> 107 us
  blocking collectives: 31 us -> 17.7 us
  starting transfers between devices: 37.3 us -> 33.6 us
    all_to_all x5, waiting for transfers between devices: 11.6 us -> 36.4 us  [exchanged(): lax.all_to_all(shaped, ('ctx', 'group'), split_axis=0, concat_axis=0, til...]
    all_to_all x1, blocking collectives: 31 us -> 17.7 us  [exchanged(): lax.all_to_all(shaped, ('ctx', 'group'), split_axis=0, concat_axis=0, til...]
where the time goes in v8:
time: 221 us; the launch traced here: 220 us
  waiting for transfers between devices  107 us (48%)
  Pallas kernels  53.7 us (24%)
  starting transfers between devices  33.6 us (15%)
  blocking collectives  17.7 us (8%)
  local copies, waits for them, and re-layouts  6.89 us (3%)
    ppermute x12, waiting for transfers between devices, swapped(): lax.ppermute(value, axis, [(n, n ^ 1) for n in range(lax.axis_size(axis))])  53.7 us
    pallas_call x11, Pallas kernels, call(): pl.pallas_call(kernel, out_shape=tuple(outs), in_specs=[ANY] * n_in, out_...  53.7 us
    all_to_all x5, waiting for transfers between devices, exchanged(): lax.all_to_all(shaped, ('ctx', 'group'), split_axis=0, concat_axis=0, til...  36.4 us
    all_to_all x5, starting transfers between devices, exchanged(): lax.all_to_all(shaped, ('ctx', 'group'), split_axis=0, concat_axis=0, til...  25.2 us
    all_to_all x1, blocking collectives, exchanged(): lax.all_to_all(shaped, ('ctx', 'group'), split_axis=0, concat_axis=0, til...  17.7 us
    ppermute x2, waiting for transfers between devices, turned(): lax.ppermute(value, 'ctx', [(n, (n + step) % size) for n in range(size)])  17.1 us
    unnamed x32, local copies, waits for them, and re-layouts  6.89 us
    ppermute x12, starting transfers between devices, swapped(): lax.ppermute(value, axis, [(n, n ^ 1) for n in range(lax.axis_size(axis))])  6.41 us
  transfers between devices with their start and end apart: 19, of which 11 were waited for; matrix products, arithmetic and copies ran while one was open for 0% of the time, Pallas kernels for 20%

profile of v8, /device:TPU:0, one launch (start us, length us, event | category | flops | bytes accessed | tf_op | source)
XLA Modules:
  0.0 220.3 jit_solution(16845327611660914036)
XLA Ops:
  3.2 7.3 %all-to-all-start = ((bf16[8,16,2048]{2,1,0:T(8,128)(2,1)}), bf16[8,16,2048]{2,1,0:T(8,128)(2,1)S(1)}, u32[]{:S(2)}, u32[]{:S(2)}) async-start(bf16[8,16,2048]{2,1,0:T(8,128)(2,1)} %get-tuple-element.29), calls=%async_computation | async-start | bytes 1048576 | tf_op jit(solution)/shard_map/all_to_all | solution.py:286
  12.5 12.3 %collective-permute-done.refs_2_ = bf16[128,1024]{1,0:T(8,128)(2,1)S(1)} collective-permute-done((bf16[128,1024]{1,0:T(8,128)(2,1)}, bf16[128,1024]{1,0:T(8,128)(2,1)S(1)}, u32[]{:S(2)}, u32[]{:S(2)}) %collective-permute-start) | collective-permute-done | bytes 262176 | tf_op jit(solution)/shard_map/ppermute | solution.py:291
  24.8 4.8 %collective-permute-done.1.refs_4_ = bf16[128,1024]{1,0:T(8,128)(2,1)S(1)} collective-permute-done((bf16[128,1024]{1,0:T(8,128)(2,1)}, bf16[128,1024]{1,0:T(8,128)(2,1)S(1)}, u32[]{:S(2)}, u32[]{:S(2)}) %collective-permute-start.1) | collective-permute-done | bytes 262176 | tf_op jit(solution)/shard_map/ppermute | solution.py:291
  30.4 4.9 %attend.1 = (f32[128,2048]{1,0:T(8,128)}, bf16[128,2048]{1,0:T(8,128)(2,1)}) custom-call(bf16[128,1024]{1,0:T(8,128)(2,1)} %bitcast.16, bf16[128,1024]{1,0:T(8,128)(2,1)} %bitcast.18, bf16[128,1024]{1,0:T(8,128)(2,1)} %copy-done.13, bf16[128,1024]{1,0:T(8,128)(2,1)} %bitcast.20, bf16[128,1024]{1,0:T(8,128)(2,1)} %copy-done.14, bf16[128,2048]{1,0:T(8,128)(2,1)} %bitcast.12, ...), custom_call_target="tpu_custom_call" | custom-call | flops 1073741824 | bytes 6045696 | tf_op jit(solution)/shard_map/attend/pallas_call | solution.py:71
  36.1 2.8 %place.1 = (bf16[8,32,2048]{2,1,0:T(8,128)(2,1)}, bf16[8,16,2048]{2,1,0:T(8,128)(2,1)}) custom-call(s32[128,2]{1,0:T(8,128)} %get-tuple-element.27.refs_0_, bf16[128,2048]{1,0:T(8,128)(2,1)} %get-tuple-element.28.refs_1_, bf16[8,16,2048]{2,1,0:T(8,128)(2,1)} %copy-done.3), custom_call_target="tpu_custom_call" | custom-call | flops 201326592 | bytes 525312 | tf_op jit(solution)/shard_map/place/pallas_call | solution.py:71
  38.9 4.6 %all-to-all-start.1 = ((bf16[8,32,2048]{2,1,0:T(8,128)(2,1)}), bf16[8,32,2048]{2,1,0:T(8,128)(2,1)S(1)}, u32[]{:S(2)}, u32[]{:S(2)}) async-start(bf16[8,32,2048]{2,1,0:T(8,128)(2,1)} %get-tuple-element.30), calls=%async_computation.1 | async-start | bytes 2097152 | tf_op jit(solution)/shard_map/all_to_all | solution.py:286
  44.1 25.6 %all-to-all-done.1.refs_0_.refs_3_.refs_10_ = bf16[8,32,2048]{2,1,0:T(8,128)(2,1)S(1)} async-done(((bf16[8,32,2048]{2,1,0:T(8,128)(2,1)}), bf16[8,32,2048]{2,1,0:T(8,128)(2,1)S(1)}, u32[]{:S(2)}, u32[]{:S(2)}) %all-to-all-start.1) | async-done | bytes 1048608 | tf_op jit(solution)/shard_map/all_to_all | solution.py:286
  71.3 17.7 %all_to_all.30.refs_0_.refs_4_.refs_12_ = bf16[8,16,2048]{2,1,0:T(8,128)(2,1)} all-to-all(bf16[8,16,2048]{2,1,0:T(8,128)(2,1)} %get-tuple-element.33), channel_id=1, replica_groups=mesh['ctx'=2,'group'=4,'side'=2,'core'=2] {'ctx','group'}, dimensions={0} | all-to-all | bytes 1048576 | tf_op jit(solution)/shard_map/all_to_all | solution.py:286
  89.0 2.8 %late_slots.1 = bf16[8,32,2048]{2,1,0:T(8,128)(2,1)} custom-call(s32[128,2]{1,0:T(8,128)} %get-tuple-element.27.refs_0_, f32[2,128]{1,0:T(2,128)} %bitcast.22, bf16[128,2048]{1,0:T(8,128)(2,1)} %bitcast.14, bf16[8,32,2048]{2,1,0:T(8,128)(2,1)} %copy-done.1, bf16[8,16,2048]{2,1,0:T(8,128)(2,1)} %all_to_all.30.refs_0_.refs_4_.refs_12_), custom_call_target="tpu_custom_call" | custom-call | flops 402653184 | bytes 526336 | tf_op jit(solution)/shard_map/late_slots/pallas_call | solution.py:71
  91.9 4.2 %all-to-all-start.5 = ((bf16[8,32,2048]{2,1,0:T(8,128)(2,1)}), bf16[8,32,2048]{2,1,0:T(8,128)(2,1)}, u32[]{:S(2)}, u32[]{:S(2)}) async-start(bf16[8,32,2048]{2,1,0:T(8,128)(2,1)} %late_slots.1), calls=%async_computation.5 | async-start | bytes 2097152 | tf_op jit(solution)/shard_map/all_to_all | solution.py:286
  96.2 7.8 %forward.2 = (bf16[256,2048]{1,0:T(8,128)(2,1)}, bf16[256,2048]{1,0:T(8,128)(2,1)}, f32[512,512]{1,0:T(8,128)}, f32[512,512]{1,0:T(8,128)}) custom-call(bf16[8,32,2048]{2,1,0:T(8,128)(2,1)} %copy-done.1, bf16[8,32,2048]{2,1,0:T(8,128)(2,1)} %collective-permute-done.2.refs_1_.refs_11_, bf16[256,2048]{1,0:T(8,128)(2,1)} %refs_2_.3, ...), custom_call_target="tpu_custom_call" | custom-call | flops 3221225472 | bytes 8388608 | tf_op jit(solution)/shard_map/forward/pallas_call | solution.py:71
  106.6 23.8 %collective-permute-done.6.refs_1_ = bf16[256,2048]{1,0:T(8,128)(2,1)S(1)} collective-permute-done((bf16[256,2048]{1,0:T(8,128)(2,1)}, bf16[256,2048]{1,0:T(8,128)(2,1)S(1)}, u32[]{:S(2)}, u32[]{:S(2)}) %collective-permute-start.6) | collective-permute-done | bytes 1048608 | tf_op jit(solution)/shard_map/ppermute | solution.py:282
  131.3 2.7 %add.2.refs_8_ = bf16[8,32,2048]{2,1,0:T(8,128)(2,1)} custom-call(bf16[256,2048]{1,0:T(8,128)(2,1)} %get-tuple-element.31.refs_0_, bf16[256,2048]{1,0:T(8,128)(2,1)} %copy-done.7), custom_call_target="tpu_custom_call" | custom-call | bytes 2097152 | tf_op jit(solution)/shard_map/add/pallas_call | solution.py:71
  134.1 7.6 %collective-permute-done.8.refs_9_.refs_2_ = bf16[8,16,2048]{2,1,0:T(8,128)(2,1)S(1)} collective-permute-done((bf16[8,16,2048]{2,1,0:T(8,128)(2,1)S(1)}, bf16[8,16,2048]{2,1,0:T(8,128)(2,1)S(1)}, u32[]{:S(2)}, u32[]{:S(2)}) %collective-permute-start.8) | collective-permute-done | bytes 524320 | tf_op jit(solution)/shard_map/ppermute | solution.py:282
  141.6 7.0 %collective-permute-done.7.refs_1_.refs_13_ = bf16[8,16,2048]{2,1,0:T(8,128)(2,1)S(1)} collective-permute-done((bf16[8,16,2048]{2,1,0:T(8,128)(2,1)S(1)}, bf16[8,16,2048]{2,1,0:T(8,128)(2,1)S(1)}, u32[]{:S(2)}, u32[]{:S(2)}) %collective-permute-start.7) | collective-permute-done | bytes 524320 | tf_op jit(solution)/shard_map/ppermute | solution.py:282
  149.5 6.3 %forward.3 = (bf16[128,2048]{1,0:T(8,128)(2,1)}, bf16[128,2048]{1,0:T(8,128)(2,1)}, f32[512,256]{1,0:T(8,128)}, f32[512,256]{1,0:T(8,128)}) custom-call(bf16[8,16,2048]{2,1,0:T(8,128)(2,1)} %all_to_all.30.refs_0_.refs_4_.refs_12_, bf16[8,16,2048]{2,1,0:T(8,128)(2,1)} %copy-done.11, bf16[256,2048]{1,0:T(8,128)(2,1)} %refs_2_.3, ...), custom_call_target="tpu_custom_call" | custom-call | flops 1610612736 | bytes 7340032 | tf_op jit(solution)/shard_map/forward/pallas_call | solution.py:71
  156.3 9.5 %collective-permute-done.9.refs_1_ = bf16[128,2048]{1,0:T(8,128)(2,1)S(1)} collective-permute-done((bf16[128,2048]{1,0:T(8,128)(2,1)}, bf16[128,2048]{1,0:T(8,128)(2,1)S(1)}, u32[]{:S(2)}, u32[]{:S(2)}) %collective-permute-start.9) | collective-permute-done | bytes 524320 | tf_op jit(solution)/shard_map/ppermute | solution.py:282
  168.7 5.3 %all-to-all-start.4 = ((bf16[8,16,2048]{2,1,0:T(8,128)(2,1)}), bf16[8,16,2048]{2,1,0:T(8,128)(2,1)S(1)}, u32[]{:S(2)}, u32[]{:S(2)}) async-start(bf16[8,16,2048]{2,1,0:T(8,128)(2,1)} %add.3), calls=%async_computation.4 | async-start | bytes 1048576 | tf_op jit(solution)/shard_map/all_to_all | solution.py:286
  174.5 10.8 %all-to-all-done.4.refs_3_ = bf16[8,16,2048]{2,1,0:T(8,128)(2,1)S(1)} async-done(((bf16[8,16,2048]{2,1,0:T(8,128)(2,1)}), bf16[8,16,2048]{2,1,0:T(8,128)(2,1)S(1)}, u32[]{:S(2)}, u32[]{:S(2)}) %all-to-all-start.4) | async-done | bytes 524320 | tf_op jit(solution)/shard_map/all_to_all | solution.py:286
  185.3 3.7 %all-to-all-start.2 = ((bf16[8,32,2048]{2,1,0:T(8,128)(2,1)}), bf16[8,32,2048]{2,1,0:T(8,128)(2,1)S(1)}, u32[]{:S(2)}, u32[]{:S(2)}) async-start(bf16[8,32,2048]{2,1,0:T(8,128)(2,1)} %add.2.refs_8_), calls=%async_computation.2 | async-start | bytes 2097152 | tf_op jit(solution)/shard_map/all_to_all | solution.py:286
  189.0 4.7 %collective-permute-done.10.refs_3_ = bf16[8,32,2048]{2,1,0:T(8,128)(2,1)S(1)} collective-permute-done((bf16[8,32,2048]{2,1,0:T(8,128)(2,1)}, bf16[8,32,2048]{2,1,0:T(8,128)(2,1)S(1)}, u32[]{:S(2)}, u32[]{:S(2)}) %collective-permute-start.10) | collective-permute-done | bytes 1048608 | tf_op jit(solution)/shard_map/ppermute | solution.py:282
  194.7 14.0 %backward.1 = (bf16[256,2048]{1,0:T(8,128)(2,1)}, bf16[256,2048]{1,0:T(8,128)(2,1)}, bf16[256,2048]{1,0:T(8,128)(2,1)}, bf16[256,2048]{1,0:T(8,128)(2,1)}, bf16[...) custom-call(bf16[8,16,2048]{2,1,0:T(8,128)(2,1)} %copy-done.3, bf16[8,32,2048]{2,1,0:T(8,128)(2,1)} %all-to-all-done.5.refs_1_, ...), custom_call_target="tpu_custom_call" | custom-call | flops 6442450944 | bytes 11534336 | tf_op jit(solution)/shard_map/backward/pallas_call | solution.py:71
  210.3 3.3 %combine.1 = bf16[128,2048]{1,0:T(8,128)(2,1)} custom-call(s32[128,2]{1,0:T(8,128)} %get-tuple-element.27.refs_0_, f32[2,128]{1,0:T(2,128)} %bitcast.23, bf16[8,32,2048]{2,1,0:T(8,128)(2,1)} %copy-done.2, bf16[8,16,2048]{2,1,0:T(8,128)(2,1)} %copy-done.5, f32[128,2048]{1,0:T(8,128)} %get-tuple-element.36.refs_4_), custom_call_target="tpu_custom_call" | custom-call | flops 402653184 | bytes 2623488 | tf_op jit(solution)/shard_map/combine/pallas_call | solution.py:71
  215.6 4.5 %finish.1 = (bf16[256,2048]{1,0:T(8,128)(2,1)}, bf16[256,2048]{1,0:T(8,128)(2,1)}, bf16[256,2048]{1,0:T(8,128)(2,1)}) custom-call(bf16[256,2048]{1,0:T(8,128)(2,1)} %get-tuple-element.41.refs_0_, bf16[256,2048]{1,0:T(8,128)(2,1)} %copy-done.8, bf16[256,2048]{1,0:T(8,128)(2,1)} %get-tuple-element.43.refs_2_, bf16[256,2048]{1,0:T(8,128)(2,1)} %copy-done.9, ...), custom_call_target="tpu_custom_call" | custom-call | bytes 6291456 | tf_op jit(solution)/shard_map/finish/pallas_call | solution.py:71
  (58 shorter events, 21.1 us)
Async XLA Ops:
  3.2 32.1 %all-to-all-start = ((bf16[8,16,2048]{2,1,0:T(8,128)(2,1)}), bf16[8,16,2048]{2,1,0:T(8,128)(2,1)S(1)}, u32[]{:S(2)}, u32[]{:S(2)}) async-start(bf16[8,16,2048]{2,1,0:T(8,128)(2,1)} %get-tuple-element.29), calls=%async_computation | async-start | bytes 1048576 | tf_op jit(solution)/shard_map/all_to_all | solution.py:286
  10.5 14.4 %collective-permute-start = (bf16[128,1024]{1,0:T(8,128)(2,1)}, bf16[128,1024]{1,0:T(8,128)(2,1)S(1)}, u32[]{:S(2)}, u32[]{:S(2)}) collective-permute-start(bf16[128,1024]{1,0:T(8,128)(2,1)} %bitcast.17), channel_id=1, source_target_pairs={{0,16},{16,0},{1,17},{17,1},{2,18},{18,2},{3,19},{19,3},{4,20},{20... | collective-permute-start | bytes 786440 | tf_op jit(solution)/shard_map/ppermute | solution.py:291
  12.5 17.2 %collective-permute-start.1 = (bf16[128,1024]{1,0:T(8,128)(2,1)}, bf16[128,1024]{1,0:T(8,128)(2,1)S(1)}, u32[]{:S(2)}, u32[]{:S(2)}) collective-permute-start(bf16[128,1024]{1,0:T(8,128)(2,1)} %bitcast.19), channel_id=1, source_target_pairs={{0,16},{16,0},{1,17},{17,1},{2,18},{18,2},{3,19},{19,3},{4,20},{20... | collective-permute-start | bytes 786440 | tf_op jit(solution)/shard_map/ppermute | solution.py:291
  30.4 13.1 %copy-start.6 = (bf16[256,2048]{1,0:T(8,128)(2,1)S(1)}, bf16[256,2048]{1,0:T(8,128)(2,1)}, u32[]{:S(2)}) copy-start(bf16[256,2048]{1,0:T(8,128)(2,1)} %refs_2_.3) | copy-start | bytes 3145732
  38.9 30.9 %all-to-all-start.1 = ((bf16[8,32,2048]{2,1,0:T(8,128)(2,1)}), bf16[8,32,2048]{2,1,0:T(8,128)(2,1)S(1)}, u32[]{:S(2)}, u32[]{:S(2)}) async-start(bf16[8,32,2048]{2,1,0:T(8,128)(2,1)} %get-tuple-element.30), calls=%async_computation.1 | async-start | bytes 2097152 | tf_op jit(solution)/shard_map/all_to_all | solution.py:286
  43.5 52.7 %collective-permute-start.3 = (bf16[256,2048]{1,0:T(8,128)(2,1)S(1)}, bf16[256,2048]{1,0:T(8,128)(2,1)}, u32[]{:S(2)}, u32[]{:S(2)}) collective-permute-start(bf16[256,2048]{1,0:T(8,128)(2,1)S(1)} %copy-done.6), channel_id=1, source_target_pairs={{0,1},{1,0},{2,3},{3,2},{4,5},{5,4},{6,7},{7,6},{8,9},{9,8},{10,11... | collective-permute-start | bytes 3145736 | tf_op jit(solution)/shard_map/ppermute | solution.py:282
  43.6 52.6 %collective-permute-start.4 = (bf16[256,2048]{1,0:T(8,128)(2,1)}, bf16[256,2048]{1,0:T(8,128)(2,1)}, u32[]{:S(2)}, u32[]{:S(2)}) collective-permute-start(bf16[256,2048]{1,0:T(8,128)(2,1)} %refs_4_.4), channel_id=1, source_target_pairs={{0,1},{1,0},{2,3},{3,2},{4,5},{5,4},{6,7},{7,6},{8,9},{9,8},{10,11... | collective-permute-start | bytes 3145736 | tf_op jit(solution)/shard_map/ppermute | solution.py:282
  44.1 52.1 %collective-permute-start.5 = (bf16[256,2048]{1,0:T(8,128)(2,1)}, bf16[256,2048]{1,0:T(8,128)(2,1)}, u32[]{:S(2)}, u32[]{:S(2)}) collective-permute-start(bf16[256,2048]{1,0:T(8,128)(2,1)} %refs_4_.5), channel_id=1, source_target_pairs={{0,1},{1,0},{2,3},{3,2},{4,5},{5,4},{6,7},{7,6},{8,9},{9,8},{10,11... | collective-permute-start | bytes 3145736 | tf_op jit(solution)/shard_map/ppermute | solution.py:282
  69.8 19.2 %copy-start.1 = (bf16[8,32,2048]{2,1,0:T(8,128)(2,1)}, bf16[8,32,2048]{2,1,0:T(8,128)(2,1)S(1)}, u32[]{:S(2)}) copy-start(bf16[8,32,2048]{2,1,0:T(8,128)(2,1)S(1)} %all-to-all-done.1.refs_0_.refs_3_.refs_10_) | copy-start | bytes 3145732
  69.8 26.4 %collective-permute-start.2 = (bf16[8,32,2048]{2,1,0:T(8,128)(2,1)S(1)}, bf16[8,32,2048]{2,1,0:T(8,128)(2,1)}, u32[]{:S(2)}, u32[]{:S(2)}) collective-permute-start(bf16[8,32,2048]{2,1,0:T(8,128)(2,1)S(1)} %all-to-all-done.1.refs_0_.refs_3_.refs_10_), channel_id=1, source_target_pairs={{0,2},{2,0},{1,3},{3,1},{4,6},{6,4},{5,7},{7,5},{8,10},{10,8},{9,1... | collective-permute-start | bytes 3145736 | tf_op jit(solution)/shard_map/ppermute | solution.py:282
  91.9 76.8 %all-to-all-start.5 = ((bf16[8,32,2048]{2,1,0:T(8,128)(2,1)}), bf16[8,32,2048]{2,1,0:T(8,128)(2,1)}, u32[]{:S(2)}, u32[]{:S(2)}) async-start(bf16[8,32,2048]{2,1,0:T(8,128)(2,1)} %late_slots.1), calls=%async_computation.5 | async-start | bytes 2097152 | tf_op jit(solution)/shard_map/all_to_all | solution.py:286
  96.1 8.5 %copy-start.4 = (bf16[8,16,2048]{2,1,0:T(8,128)(2,1)S(1)}, bf16[8,16,2048]{2,1,0:T(8,128)(2,1)}, u32[]{:S(2)}) copy-start(bf16[8,16,2048]{2,1,0:T(8,128)(2,1)} %copy-done.3) | copy-start | bytes 1572868
  96.1 10.0 %copy-start = (bf16[8,16,2048]{2,1,0:T(8,128)(2,1)S(1)}, bf16[8,16,2048]{2,1,0:T(8,128)(2,1)}, u32[]{:S(2)}) copy-start(bf16[8,16,2048]{2,1,0:T(8,128)(2,1)} %all_to_all.30.refs_0_.refs_4_.refs_12_) | copy-start | bytes 1572868
  104.0 26.4 %collective-permute-start.6 = (bf16[256,2048]{1,0:T(8,128)(2,1)}, bf16[256,2048]{1,0:T(8,128)(2,1)S(1)}, u32[]{:S(2)}, u32[]{:S(2)}) collective-permute-start(bf16[256,2048]{1,0:T(8,128)(2,1)} %get-tuple-element.32), channel_id=1, source_target_pairs={{0,2},{2,0},{1,3},{3,1},{4,6},{6,4},{5,7},{7,5},{8,10},{10,8},{9,1... | collective-permute-start | bytes 3145736 | tf_op jit(solution)/shard_map/ppermute | solution.py:282
  104.6 37.0 %collective-permute-start.8 = (bf16[8,16,2048]{2,1,0:T(8,128)(2,1)S(1)}, bf16[8,16,2048]{2,1,0:T(8,128)(2,1)S(1)}, u32[]{:S(2)}, u32[]{:S(2)}) collective-permute-start(bf16[8,16,2048]{2,1,0:T(8,128)(2,1)S(1)} %copy-done.4), channel_id=1, source_target_pairs={{0,2},{2,0},{1,3},{3,1},{4,6},{6,4},{5,7},{7,5},{8,10},{10,8},{9,1... | collective-permute-start | bytes 1572872 | tf_op jit(solution)/shard_map/ppermute | solution.py:282
  106.1 42.6 %collective-permute-start.7 = (bf16[8,16,2048]{2,1,0:T(8,128)(2,1)S(1)}, bf16[8,16,2048]{2,1,0:T(8,128)(2,1)S(1)}, u32[]{:S(2)}, u32[]{:S(2)}) collective-permute-start(bf16[8,16,2048]{2,1,0:T(8,128)(2,1)S(1)} %copy-done), channel_id=1, source_target_pairs={{0,2},{2,0},{1,3},{3,1},{4,6},{6,4},{5,7},{7,5},{8,10},{10,8},{9,1... | collective-permute-start | bytes 1572872 | tf_op jit(solution)/shard_map/ppermute | solution.py:282
  155.8 10.0 %collective-permute-start.9 = (bf16[128,2048]{1,0:T(8,128)(2,1)}, bf16[128,2048]{1,0:T(8,128)(2,1)S(1)}, u32[]{:S(2)}, u32[]{:S(2)}) collective-permute-start(bf16[128,2048]{1,0:T(8,128)(2,1)} %get-tuple-element.35), channel_id=1, source_target_pairs={{0,2},{2,0},{1,3},{3,1},{4,6},{6,4},{5,7},{7,5},{8,10},{10,8},{9,1... | collective-permute-start | bytes 1572872 | tf_op jit(solution)/shard_map/ppermute | solution.py:282
  168.7 16.6 %all-to-all-start.4 = ((bf16[8,16,2048]{2,1,0:T(8,128)(2,1)}), bf16[8,16,2048]{2,1,0:T(8,128)(2,1)S(1)}, u32[]{:S(2)}, u32[]{:S(2)}) async-start(bf16[8,16,2048]{2,1,0:T(8,128)(2,1)} %add.3), calls=%async_computation.4 | async-start | bytes 1048576 | tf_op jit(solution)/shard_map/all_to_all | solution.py:286
  174.1 19.7 %collective-permute-start.10 = (bf16[8,32,2048]{2,1,0:T(8,128)(2,1)}, bf16[8,32,2048]{2,1,0:T(8,128)(2,1)S(1)}, u32[]{:S(2)}, u32[]{:S(2)}) collective-permute-start(bf16[8,32,2048]{2,1,0:T(8,128)(2,1)} %all-to-all-done.5.refs_1_), channel_id=1, source_target_pairs={{0,2},{2,0},{1,3},{3,1},{4,6},{6,4},{5,7},{7,5},{8,10},{10,8},{9,1... | collective-permute-start | bytes 3145736 | tf_op jit(solution)/shard_map/ppermute | solution.py:282
  185.3 23.4 %copy-start.5 = (bf16[8,16,2048]{2,1,0:T(8,128)(2,1)}, bf16[8,16,2048]{2,1,0:T(8,128)(2,1)S(1)}, u32[]{:S(2)}) copy-start(bf16[8,16,2048]{2,1,0:T(8,128)(2,1)S(1)} %all-to-all-done.4.refs_3_) | copy-start | bytes 1572868
  185.3 24.1 %all-to-all-start.2 = ((bf16[8,32,2048]{2,1,0:T(8,128)(2,1)}), bf16[8,32,2048]{2,1,0:T(8,128)(2,1)S(1)}, u32[]{:S(2)}, u32[]{:S(2)}) async-start(bf16[8,32,2048]{2,1,0:T(8,128)(2,1)} %add.2.refs_8_), calls=%async_computation.2 | async-start | bytes 2097152 | tf_op jit(solution)/shard_map/all_to_all | solution.py:286
  208.7 4.9 %collective-permute-start.11 = (bf16[256,2048]{1,0:T(8,128)(2,1)}, bf16[256,2048]{1,0:T(8,128)(2,1)S(1)}, u32[]{:S(2)}, u32[]{:S(2)}) collective-permute-start(bf16[256,2048]{1,0:T(8,128)(2,1)} %get-tuple-element.42), channel_id=1, source_target_pairs={{0,1},{1,0},{2,3},{3,2},{4,5},{5,4},{6,7},{7,6},{8,9},{9,8},{10,11... | collective-permute-start | bytes 3145736 | tf_op jit(solution)/shard_map/ppermute | solution.py:282
  208.8 5.9 %collective-permute-start.12 = (bf16[256,2048]{1,0:T(8,128)(2,1)}, bf16[256,2048]{1,0:T(8,128)(2,1)S(1)}, u32[]{:S(2)}, u32[]{:S(2)}) collective-permute-start(bf16[256,2048]{1,0:T(8,128)(2,1)} %get-tuple-element.44), channel_id=1, source_target_pairs={{0,1},{1,0},{2,3},{3,2},{4,5},{5,4},{6,7},{7,6},{8,9},{9,8},{10,11... | collective-permute-start | bytes 3145736 | tf_op jit(solution)/shard_map/ppermute | solution.py:282
  209.3 5.5 %collective-permute-start.13 = (bf16[256,2048]{1,0:T(8,128)(2,1)}, bf16[256,2048]{1,0:T(8,128)(2,1)}, u32[]{:S(2)}, u32[]{:S(2)}) collective-permute-start(bf16[256,2048]{1,0:T(8,128)(2,1)} %get-tuple-element.46), channel_id=1, source_target_pairs={{0,1},{1,0},{2,3},{3,2},{4,5},{5,4},{6,7},{7,6},{8,9},{9,8},{10,11... | collective-permute-start | bytes 3145736 | tf_op jit(solution)/shard_map/ppermute | solution.py:282
  (11 other events, 20.0 us)
